TPU v7x, 32 devices: a whole 2x2x4 slice. The times are simulated.
32 devices in a mesh: fsdp: 4 (over y, x), ed: 8 (over z, core).
Axes of the slice: x: 2, y: 2, z: 4, core: 2. Of those that a mesh axis runs over, the one named last changes fastest.
Arguments:
- tokens: bfloat16 [2304, 6144], P('ed', 'fsdp'), may hold values from -6 to 6
- expert_ids: int32 [2304, 2], P('ed'), may hold values from 0 to 7, all different within a row; in each aligned block of 288 rows (0 to 287, 288 to 575, ...) at most 81 rows name the same one
- route_weights: float32 [2304, 2], P('ed'), may hold values from 0.1 to 1
- w_gate: bfloat16 [1, 6144, 8192], P(None, 'fsdp', 'ed'), may hold values from -0.078125 to 0.078125
- w_up: bfloat16 [1, 6144, 8192], P(None, 'fsdp', 'ed'), may hold values from -0.078125 to 0.078125
- w_down: bfloat16 [1, 8192, 6144], P(None, 'ed', 'fsdp'), may hold values from -0.0625 to 0.0625
Outputs:
- mixed: bfloat16 [2304, 6144], P('ed', 'fsdp')
Inputs may be any that keep to these rules, and one draw needn't show every extreme that they name: `expert_ids`: each row names two different experts. In each block of 288 rows that one index of ed holds, no expert is named by more than 81 rows, a bound that some block reaches.
All inputs are finite; a program needn't handle non-finite values.
Results may differ from a plain program's by a relative error of at most 0.025.
Values may be sent and summed in bfloat16 or wider, within the bound.
No kernel may reach another device: no remote copies, remote signals or barrier semaphores. Data moves between devices by JAX's collectives and lax.ppermute only.
A program may use at most 128 MiB of HBM per device.

v0:
```python
import jax
import jax.numpy as jnp
from jax import lax
from jax.sharding import PartitionSpec as P

CAP = 81


def slot_match(routes, window, capacity):
    window_ids = jnp.arange(window, dtype=jnp.int32)
    routed = jnp.any(routes[:, :, None, :] == window_ids[None, None, :, None], axis=3)
    position = jnp.cumsum(routed.astype(jnp.int32), axis=1) - 1
    slot_ids = jnp.arange(capacity, dtype=jnp.int32)
    hits = routed[:, :, :, None] & (position[:, :, :, None] == slot_ids[None, None, None, :])
    return hits.astype(jnp.int32)


def take_block(block_rows, row_list):
    return jnp.take(block_rows, row_list, axis=0)


def pick_rows(blocks, routes, window, capacity):
    match = slot_match(routes, window, capacity)
    row_numbers = jnp.arange(blocks.shape[1], dtype=jnp.int32)
    source_row = jnp.sum(match * row_numbers[None, :, None, None], axis=1).reshape(
        blocks.shape[0], window * capacity
    )
    filled = jnp.sum(match, axis=1).reshape(blocks.shape[0], window * capacity)
    picked = jax.vmap(take_block)(blocks, source_row)
    picked = jnp.where(filled[:, :, None] > 0, picked, jnp.zeros_like(picked))
    return picked.reshape(blocks.shape[0], window, capacity, blocks.shape[2])


def combine_matrix(routes, weights, window, capacity):
    match = slot_match(routes[None], window, capacity)[0]
    window_ids = jnp.arange(window, dtype=jnp.int32)
    per_expert = jnp.sum(
        jnp.where(
            routes[:, None, :] == window_ids[None, :, None],
            weights[:, None, :],
            jnp.zeros_like(weights[:, None, :]),
        ),
        axis=2,
    )
    return (per_expert[:, :, None] * match.astype(weights.dtype)).reshape(
        routes.shape[0], window * capacity
    )


def local(tokens, expert_ids, route_weights, w_gate, w_up, w_down):
    window = w_gate.shape[0]
    features_dev = tokens.shape[1]
    own_slots = pick_rows(tokens[None], expert_ids[None], window, CAP)[0]
    selected = lax.all_gather(own_slots, "ed", axis=1, tiled=True)
    rows_full = lax.all_to_all(selected, "fsdp", split_axis=1, concat_axis=2, tiled=True)
    gate_part = jnp.einsum(
        "hnm,hmq->hnq",
        rows_full,
        lax.all_gather(w_gate, "fsdp", axis=1, tiled=True),
        preferred_element_type=jnp.float32,
    )
    up_part = jnp.einsum(
        "hnm,hmq->hnq",
        rows_full,
        lax.all_gather(w_up, "fsdp", axis=1, tiled=True),
        preferred_element_type=jnp.float32,
    )
    activation = (jax.nn.silu(gate_part) * up_part).astype(jnp.bfloat16)
    act_one = activation[0]

    def columns_out(shard_piece, first_col, act_one=act_one):
        return jnp.dot(act_one, shard_piece, preferred_element_type=jnp.float32)

    whole_rows = columns_out(lax.all_gather(w_down[0], "fsdp", axis=1, tiled=True), jnp.int32(0))
    outputs_list = [whole_rows.astype(jnp.bfloat16)]
    stacked = jnp.stack(outputs_list)
    exchanged = lax.all_to_all(stacked, "fsdp", split_axis=2, concat_axis=1, tiled=True)
    partial_out = exchanged.astype(jnp.float32)
    slot_out = lax.psum_scatter(
        partial_out.astype(jnp.bfloat16), "ed", scatter_dimension=1, tiled=True
    ).astype(jnp.float32)
    weights_matrix = combine_matrix(expert_ids, route_weights, window, CAP)
    mixed = jnp.dot(
        weights_matrix,
        slot_out.reshape(window * CAP, features_dev),
        precision=lax.Precision.HIGHEST,
        preferred_element_type=jnp.float32,
    )
    return mixed.astype(jnp.bfloat16)


def solution(mesh):
    return jax.shard_map(
        local,
        mesh=mesh,
        in_specs=(
            P("ed", "fsdp"),
            P("ed", None),
            P("ed", None),
            P(None, "fsdp", "ed"),
            P(None, "fsdp", "ed"),
            P(None, "ed", "fsdp"),
        ),
        out_specs=P("ed", "fsdp"),
        check_vma=False,
    )
```

profile of v0, /device:TPU:0, one launch (start us, length us, event | category | flops | bytes accessed | tf_op | source)
XLA Modules:
  0.0 628.3 jit_solution(4195720996211715929)
XLA Ops:
  6.5 0.8 fusion.28
  8.2 3.0 convert_reduce_fusion
  11.2 1.9 gather_fusion
  13.2 1.2 copy.18
  16.4 46.0 %all-gather.6.cloned.1.call-done = bf16[1,648,1536]{2,0,1:T(2,128)(2,1)} async-done(((bf16[1,81,1536]{2,0,1:T(2,128)(2,1)}), bf16[1,648,1536]{2,0,1:T(2,128)(2,1)}) %all-gather.6.cloned.1.call-update) | async-done | bytes 1990672 | tf_op jit(solution)/shard_map/all_gather | solution.py:54
  62.9 12.6 %reduce.14 = bf16[648,1536]{1,0:T(8,128)(2,1)S(1)} reduce(bf16[648,1,1536]{2,1,0:T(2,128)(2,1)} %bitcast.74, bf16[]{:T(256)} %broadcast.283), dimensions={1}, to_apply=%bitcast.58.reduce_sub_computation | reduce | bytes 3981314
  75.5 2.0 reshape.463
  77.6 50.5 %all_to_all.33 = bf16[4,2,124416]{2,1,0:T(2,128)(2,1)S(1)} all-to-all(bf16[4,2,124416]{2,1,0:T(2,128)(2,1)} %reshape.463), channel_id=1, replica_groups=mesh['fsdp'=4,'ed'=8] {'fsdp'}, dimensions={0} | all-to-all | bytes 3981312 | tf_op jit(solution)/shard_map/all_to_all | solution.py:55
  128.0 3.0 reshape.464
  131.0 13.7 %bitcast_reduce_fusion = bf16[648,1536]{1,0:T(8,128)(2,1)} fusion(bf16[648,1,1536]{2,1,0:T(2,128)(2,1)} %reshape.464), kind=kLoop, calls=%fused_computation.41 | loop fusion | bytes 3981312 | tf_op jit(solution)/shard_map/all_to_all | solution.py:55
  144.7 2.1 all_to_all.25
  146.8 1.0 copy.28
  147.8 0.8 pad.7
  149.1 57.9 %all-gather.8.cloned.1.call-done = bf16[1,6144,1024]{2,1,0:T(8,128)(2,1)} async-done(((bf16[1,1536,1024]{2,1,0:T(8,128)(2,1)}), bf16[1,6144,1024]{2,1,0:T(8,128)(2,1)}) %all-gather.8.cloned.1.call-update) | async-done | bytes 12582928 | tf_op jit(solution)/shard_map/all_gather | solution.py:59
  207.0 6.9 %fusion.5 = f32[162,1024]{1,0:T(8,128)S(1)} fusion(bf16[162,6144]{1,0:T(8,128)(2,1)S(1)} %bitcast.75, bf16[1,6144,1024]{2,1,0:T(8,128)(2,1)} %all-gather.8.cloned.1.call-done), kind=kOutput, calls=%fused_computation.5 | convolution fusion | flops 2038431744 | bytes 15237120 | tf_op jit(solution)/shard_map/hnm,hmq->hnq/dot_general | solution.py:56
  213.8 117.5 %all-gather.10.cloned.1.call-done = bf16[1,6144,1024]{2,1,0:T(8,128)(2,1)} async-done(((bf16[1,1536,1024]{2,1,0:T(8,128)(2,1)}), bf16[1,6144,1024]{2,1,0:T(8,128)(2,1)}) %all-gather.10.cloned.1.call-update) | async-done | bytes 12582928 | tf_op jit(solution)/shard_map/all_gather | solution.py:65
  331.3 124.2 %all-gather.12.cloned.1.call-done = bf16[1,1024,6144]{2,1,0:T(8,128)(2,1)} async-done(((bf16[1,1024,1536]{2,1,0:T(8,128)(2,1)}), bf16[1,1024,6144]{2,1,0:T(8,128)(2,1)}) %all-gather.12.cloned.1.call-update) | async-done | bytes 12582928 | tf_op jit(solution)/shard_map/all_gather | solution.py:74
  455.6 14.0 %fusion.10 = bf16[1,162,6144]{2,1,0:T(8,128)(2,1)} fusion(bf16[1,1024,6144]{2,1,0:T(8,128)(2,1)} %all-gather.12.cloned.1.call-done, bf16[162,6144]{1,0:T(8,128)(2,1)S(1)} %bitcast.76, bf16[1,6144,1024]{2,1,0:T(8,128)(2,1)} %all-gather.10.cloned.1.call-done, f32[162,1024]{1,0:T(8,128)S(1)} %fusion.5), kind=kOutput, calls=%fused_computation.8 | convolution fusion | flops 4078854144 | bytes 29810688 | tf_op jit(solution)/shard_map/dot_general | solution.py:72
  469.6 13.7 %copy.20 = bf16[1,162,6144]{1,0,2:T(2,128)(2,1)} copy(bf16[1,162,6144]{2,1,0:T(8,128)(2,1)} %fusion.10) | data formatting | bytes 3981312 | tf_op jit(solution)/shard_map/stack | solution.py:76
  483.3 36.3 %reduce.15 = bf16[6144,162]{1,0:T(8,128)(2,1)} reduce(bf16[6144,1,162]{2,1,0:T(2,128)(2,1)} %bitcast.68, bf16[]{:T(256)} %broadcast.283), dimensions={1}, to_apply=%bitcast.60.reduce_sub_computation | reduce | bytes 3981314
  519.6 7.9 %reshape.465 = bf16[4,2,124416]{2,1,0:T(2,128)(2,1)} reshape(bf16[6144,162]{1,0:T(8,128)(2,1)} %reduce.15) | data formatting | bytes 3981312
  527.5 3.7 all-to-all-start.1
  532.6 22.7 %all-to-all-done.1 = bf16[4,2,124416]{2,1,0:T(2,128)(2,1)S(1)} async-done(((bf16[4,2,124416]{2,1,0:T(2,128)(2,1)}), bf16[4,2,124416]{2,1,0:T(2,128)(2,1)S(1)}, u32[]{:S(2)}, u32[]{:S(2)}) %all-to-all-start.1) | async-done | bytes 1990688 | tf_op jit(solution)/shard_map/all_to_all | solution.py:77
  555.3 11.0 %reshape.466 = bf16[6144,1,162]{2,1,0:T(2,128)(2,1)} reshape(bf16[4,2,124416]{2,1,0:T(2,128)(2,1)S(1)} %all-to-all-done.1) | data formatting | bytes 3981312
  566.3 13.8 %copy.21 = bf16[1,162,6144]{2,1,0:T(8,128)(2,1)S(1)} copy(bf16[1,162,6144]{1,0,2:T(2,128)(2,1)} %bitcast.69) | data formatting | bytes 3981312 | tf_op jit(solution)/shard_map/all_to_all | solution.py:77
  580.0 2.4 all_to_all.28
  582.5 1.9 copy.22
  584.4 1.8 all_to_all.30
  586.2 30.3 %fusion = bf16[88,1536]{1,0:T(8,128)(2,1)S(1)} fusion(bf16[1,648,1536]{2,1,0:T(8,128)(2,1)} %all_to_all.30), kind=kCustom, calls=%all-reduce-scatter | all-reduce-scatter fusion | flops 1081345 | bytes 2261504
  616.5 1.3 collective-permute-start
  617.8 1.7 convert_multiply_fusion
  620.0 1.8 convolution_convert_fusion
  (40 shorter events, 5.1 us)
Async XLA Ops:
  6.5 4.6 copy-start
  6.5 55.9 %all-gather.6.cloned.1.call-start = ((), (), s32[]{:S(2)}) async-start(), calls=%async_computation.2 | async-start | bytes 4478976 | tf_op jit(solution)/shard_map/all_gather | solution.py:54
  14.4 192.6 %all-gather.8.cloned.1.call-start = ((), (), s32[]{:S(2)}) async-start(), calls=%async_computation.3 | async-start | bytes 15728640 | tf_op jit(solution)/shard_map/all_gather | solution.py:59
  15.1 316.2 %all-gather.10.cloned.1.call-start = ((), (), s32[]{:S(2)}) async-start(), calls=%async_computation.4 | async-start | bytes 15728640 | tf_op jit(solution)/shard_map/all_gather | solution.py:65
  15.9 439.7 %all-gather.12.cloned.1.call-start = ((), (), s32[]{:S(2)}) async-start(), calls=%async_computation.5 | async-start | bytes 15728640 | tf_op jit(solution)/shard_map/all_gather | solution.py:74
  527.5 3.8 copy-start.4
  527.5 5.0 copy-start.2
  527.5 5.0 copy-start.3
  527.5 27.7 %all-to-all-start.1 = ((bf16[4,2,124416]{2,1,0:T(2,128)(2,1)}), bf16[4,2,124416]{2,1,0:T(2,128)(2,1)S(1)}, u32[]{:S(2)}, u32[]{:S(2)}) async-start(bf16[4,2,124416]{2,1,0:T(2,128)(2,1)} %reshape.465), calls=%async_computation.1 | async-start | bytes 3981312 | tf_op jit(solution)/shard_map/all_to_all | solution.py:77
  584.4 37.4 %copy-start.1 = (bf16[288,1536]{1,0:T(8,128)(2,1)S(1)}, bf16[288,1536]{1,0:T(8,128)(2,1)}, u32[]{:S(2)}) copy-start(bf16[288,1536]{1,0:T(8,128)(2,1)} %param.6) | copy-start | bytes 2654212
  616.5 3.0 collective-permute-start
Sparse Core Ops, SparseCore 0:
  14.5 47.8 all-gather.5
  64.2 142.6 all-gather.7
  208.8 122.5 all-gather.9
  333.0 122.5 all-gather.11
where the time goes:
time: 630 us; the launch traced here: 628 us
  waiting for transfers between devices  370 us (59%)
  blocking collectives  80.7 us (13%)
  local copies, waits for them, and re-layouts  80.5 us (13%)
  other arithmetic  55 us (9%)
  matrix products  22.7 us (4%)
  between operations  14 us (2%)
    all_gather x1, waiting for transfers between devices, local(): lax.all_gather(w_down[0], 'fsdp', axis=1, tiled=True)  124 us
    all_gather x1, waiting for transfers between devices, local(): lax.all_gather(w_up, 'fsdp', axis=1, tiled=True)  118 us
    all_gather x1, waiting for transfers between devices, local(): lax.all_gather(w_gate, 'fsdp', axis=1, tiled=True)  57.9 us
    all_to_all x1, blocking collectives, local(): lax.all_to_all(selected, 'fsdp', split_axis=1, concat_axis=2, tiled=True)  50.5 us
    unnamed x2, other arithmetic  48.9 us
    all_gather x1, waiting for transfers between devices, local(): selected = lax.all_gather(own_slots, 'ed', axis=1, tiled=True)  46 us
    unnamed x1, blocking collectives  30.3 us
    unnamed x20, local copies, waits for them, and re-layouts  26.8 us
  transfers between devices with their start and end apart: 6, of which 5 were waited for; matrix products, arithmetic and copies ran while one was open for 7% of the time, Pallas kernels for 0%

commit v1 on v0

v1 whole, which is shorter than its diff:
```python
import functools
import jax
import jax.numpy as jnp
from jax import lax
from jax.experimental import pallas as pl
from jax.experimental.pallas import tpu as pltpu
from jax.sharding import PartitionSpec as P

CAP = 81
LIMIT = 40 * 1024 * 1024


def params():
    return pltpu.CompilerParams(vmem_limit_bytes=LIMIT)


def vmem():
    return pl.BlockSpec(memory_space=pltpu.VMEM)


def one_hot_slots(ids_ref, slots, kind):
    ids = ids_ref[...]
    tokens = ids.shape[1]
    routed = jnp.max(jnp.where(ids == 0, 1.0, 0.0), axis=0, keepdims=True)
    below = lax.broadcasted_iota(jnp.int32, (tokens, tokens), 0) <= lax.broadcasted_iota(
        jnp.int32, (tokens, tokens), 1
    )
    place = jnp.dot(
        jnp.broadcast_to(routed, (8, tokens)).astype(jnp.bfloat16),
        jnp.where(below, 1.0, 0.0).astype(jnp.bfloat16),
        preferred_element_type=jnp.float32,
    )[0:1]
    place = jnp.where(routed > 0, place, 0.0)
    numbers = lax.broadcasted_iota(jnp.int32, (slots, tokens), 0).astype(jnp.float32) + 1.0
    return jnp.where(numbers == place, 1.0, 0.0).astype(kind)


def pick_kernel(ids_ref, tokens_ref, out_ref):
    hits = one_hot_slots(ids_ref, out_ref.shape[0], jnp.bfloat16)
    out_ref[...] = jnp.dot(hits, tokens_ref[...], preferred_element_type=jnp.float32).astype(
        out_ref.dtype
    )


def pick(ids, tokens, slots):
    return pl.pallas_call(
        pick_kernel,
        out_shape=jax.ShapeDtypeStruct((slots, tokens.shape[1]), tokens.dtype),
        in_specs=[vmem(), vmem()],
        out_specs=vmem(),
        compiler_params=params(),
        name="pick",
    )(ids, tokens)


def project_kernel(col, x_ref, *refs):
    weights, outs = refs[:4], refs[4:]
    step = pl.program_id(0)
    x = x_ref[...]
    quarter = weights[0].shape[1]
    for n, out in enumerate(outs):

        @pl.when(step == n)
        def _(out=out):
            for j, w in enumerate(weights):
                out[:, j * quarter : (j + 1) * quarter] = jnp.dot(
                    x, w[...], preferred_element_type=jnp.float32
                ).astype(out.dtype)


def project(columns, x, weights, order):
    rows, depth = x.shape
    parts = len(order)
    quarter = weights[0].shape[1] // parts
    kinds = [jnp.float32 if k == 0 else jnp.bfloat16 for k in order]
    if quarter % 128:
        outs = []
        for n, kind in enumerate(kinds):
            cut = [
                lax.dynamic_slice_in_dim(w, columns[n] * quarter, quarter, axis=1) for w in weights
            ]
            out = jnp.dot(x, jnp.concatenate(cut, axis=1), preferred_element_type=jnp.float32)
            outs.append(out.astype(kind))
        return outs
    whole = lambda n, col: (0, 0)
    grid_spec = pltpu.PrefetchScalarGridSpec(
        num_scalar_prefetch=1,
        grid=(parts,),
        in_specs=[pl.BlockSpec((rows, depth), whole)]
        + [pl.BlockSpec((depth, quarter), lambda n, col: (0, col[n]))] * 4,
        out_specs=[pl.BlockSpec((rows, 4 * quarter), whole)] * parts,
    )
    return pl.pallas_call(
        project_kernel,
        out_shape=[jax.ShapeDtypeStruct((rows, 4 * quarter), k) for k in kinds],
        grid_spec=grid_spec,
        compiler_params=params(),
        name="project",
    )(columns, x, *weights)


def down_kernel(col, *refs):
    parts = len(refs) - 4
    acts, (own, par, out_ref, total) = refs[:parts], refs[parts:]
    step = pl.program_id(0)
    quarter = own.shape[0]
    for n, act in enumerate(acts):

        @pl.when(step == n)
        def _(n=n, act=act):
            term = jnp.dot(act[:, :quarter], own[...], preferred_element_type=jnp.float32)
            term += jnp.dot(act[:, quarter:], par[...], preferred_element_type=jnp.float32)
            if n == 0:
                total[...] = term
            elif n < parts - 1:
                total[...] += term
            else:
                out_ref[...] = (total[...] + term).astype(out_ref.dtype)


def down(columns, acts, weights):
    parts = len(acts)
    rows = acts[0].shape[0]
    quarter, width = weights[0].shape[0] // parts, weights[0].shape[1]
    whole = lambda n, col: (0, 0)
    grid_spec = pltpu.PrefetchScalarGridSpec(
        num_scalar_prefetch=1,
        grid=(parts,),
        in_specs=[pl.BlockSpec((rows, 2 * quarter), whole)] * parts
        + [pl.BlockSpec((quarter, width), lambda n, col: (col[n], 0))] * 2,
        out_specs=pl.BlockSpec((rows, width), whole),
        scratch_shapes=[pltpu.VMEM((rows, width), jnp.float32)],
    )
    return pl.pallas_call(
        down_kernel,
        out_shape=jax.ShapeDtypeStruct((rows, width), jnp.bfloat16),
        grid_spec=grid_spec,
        compiler_params=params(),
        name="down",
    )(columns, *acts, *weights)


def combine_kernel(ids_ref, weights_ref, *refs):
    terms, out_ref = refs[:-1], refs[-1]
    slots = terms[0].shape[0]
    hits = one_hot_slots(ids_ref, slots, jnp.float32)
    scale = jnp.sum(jnp.where(ids_ref[...] == 0, weights_ref[...], 0.0), axis=0, keepdims=True)
    slot_out = terms[0][...].astype(jnp.float32)
    for term in terms[1:]:
        slot_out += term[...].astype(jnp.float32)
    out_ref[...] = lax.dot_general(
        hits * scale,
        slot_out,
        (((0,), (0,)), ((), ())),
        precision=lax.Precision.HIGHEST,
        preferred_element_type=jnp.float32,
    ).astype(out_ref.dtype)


def combine(ids, weights, terms):
    return pl.pallas_call(
        combine_kernel,
        out_shape=jax.ShapeDtypeStruct((ids.shape[1], terms[0].shape[1]), jnp.bfloat16),
        in_specs=[vmem()] * (2 + len(terms)),
        out_specs=vmem(),
        compiler_params=params(),
        name="combine",
    )(ids, weights, *terms)


def local(n_fsdp, n_ed, groups, tokens, expert_ids, route_weights, w_gate, w_up, w_down):
    slots = -(-CAP // 8) * 8
    swap = lambda v, axis, size, k: lax.ppermute(v, axis, [(i, i ^ k) for i in range(size)])
    partner = lambda v: swap(v, "ed", n_ed, 1)
    me = lax.axis_index("fsdp").astype(jnp.int32)
    order = list(range(n_fsdp))
    columns = me ^ jnp.array(order, jnp.int32)

    own = [w_gate[0], w_up[0], w_down[0]]
    other = [partner(w) for w in own]
    ids, scales = expert_ids.T, route_weights.T
    mine = pick(ids, tokens, slots)
    blocks = {0: mine}
    for s in range(1, n_ed // 2):
        blocks[s] = swap(mine, "ed", n_ed, 2 * s)

    sums = {}
    for group in groups:
        x = jnp.concatenate([blocks[s] for s in group], axis=0)
        parts = project(columns, x, [own[0], other[0], own[1], other[1]], order)
        total = parts[0]
        for k in range(1, n_fsdp):
            total = total + swap(parts[k], "fsdp", n_fsdp, k).astype(jnp.float32)
        half = total.shape[1] // 2
        act = (jax.nn.silu(total[:, :half]) * total[:, half:]).astype(jnp.bfloat16)
        acts = [act] + [swap(act, "fsdp", n_fsdp, k) for k in range(1, n_fsdp)]
        out = down(columns, acts, [own[2], other[2]])
        for i, s in enumerate(group):
            sums[s] = out[i * slots : (i + 1) * slots]
    terms = [sums[0]] + [swap(sums[s], "ed", n_ed, 2 * s) for s in range(1, n_ed // 2)]
    return combine(ids, scales, terms)


def solution(mesh):
    n_fsdp, n_ed = mesh.shape["fsdp"], mesh.shape["ed"]
    half = n_ed // 4
    groups = [list(range(half)), list(range(half, n_ed // 2))]
    return jax.shard_map(
        functools.partial(local, n_fsdp, n_ed, groups),
        mesh=mesh,
        in_specs=(
            P("ed", "fsdp"),
            P("ed", None),
            P("ed", None),
            P(None, "fsdp", "ed"),
            P(None, "fsdp", "ed"),
            P(None, "ed", "fsdp"),
        ),
        out_specs=P("ed", "fsdp"),
        check_vma=False,
    )
```

time: 630 us -> 112 us (0.18)
  waiting for transfers between devices: 370 us -> 53.1 us
  blocking collectives: 80.7 us -> 0 us
  local copies, waits for them, and re-layouts: 80.5 us -> 5.72 us
  other arithmetic: 55 us -> 2.63 us
  starting transfers between devices: 5.16 us -> 28.3 us
  matrix products: 22.7 us -> 0 us
  Pallas kernels: 0 us -> 21.4 us
  between operations: 14 us -> 0.18 us
    all_gather x4 -> x0, waiting for transfers between devices: 346 us -> none  [the longest x1 124 us: local(): lax.all_gather(w_down[0], 'fsdp', axis=1, tiled=True)]
    ppermute x0 -> x21, waiting for transfers between devices: none -> 53.1 us  [local(): lax.ppermute(v, axis, [(i, i ^ k) for i in range(size)])]
    all_to_all x1 -> x0, blocking collectives: 50.5 us -> none  [local(): lax.all_to_all(selected, 'fsdp', split_axis=1, concat_axis=2, tiled=True)]
    unnamed x2 -> x0, other arithmetic: 48.9 us -> none
    all_to_all x7 -> x0, local copies, waits for them, and re-layouts: 36.7 us -> none  [the longest x4 19.9 us: local(): lax.all_to_all(stacked, 'fsdp', split_axis=2, concat_axis=1, tiled=True)]
    unnamed x1 -> x0, blocking collectives: 30.3 us -> none
    ppermute x0 -> x21, starting transfers between devices: none -> 28.3 us  [local(): lax.ppermute(v, axis, [(i, i ^ k) for i in range(size)])]
    dot_general x3 -> x0, matrix products: 22.7 us -> none  [the longest x1 14 us: columns_out(): return jnp.dot(act_one, shard_piece, preferred_element_type=jnp.float32)]
  transfers between devices with their start and end apart: 6 -> 21, of which waited for: 5 -> 11; matrix products, arithmetic and copies ran while one was open for 7% -> 2% of each run, Pallas kernels for 0% -> 15%
where the time goes in v1:
time: 112 us; the launch traced here: 111 us
  waiting for transfers between devices  53.1 us (47%)
  starting transfers between devices  28.3 us (25%)
  Pallas kernels  21.4 us (19%)
  local copies, waits for them, and re-layouts  5.72 us (5%)
  other arithmetic  2.63 us (2%)
    ppermute x21, waiting for transfers between devices, local(): lax.ppermute(v, axis, [(i, i ^ k) for i in range(size)])  53.1 us
    ppermute x21, starting transfers between devices, local(): lax.ppermute(v, axis, [(i, i ^ k) for i in range(size)])  28.3 us
    pallas_call x2, Pallas kernels, project(): pl.pallas_call(project_kernel, out_shape=[jax.ShapeDtypeStruct((rows, 4 *...  13.4 us
    unnamed x18, local copies, waits for them, and re-layouts  5.65 us
    pallas_call x2, Pallas kernels, down(): pl.pallas_call(down_kernel, out_shape=jax.ShapeDtypeStruct((rows, width),...  4.93 us
    pallas_call x1, Pallas kernels, combine(): pl.pallas_call(combine_kernel, out_shape=jax.ShapeDtypeStruct((ids.shape[...  2.66 us
  transfers between devices with their start and end apart: 21, of which 11 were waited for; matrix products, arithmetic and copies ran while one was open for 2% of the time, Pallas kernels for 15%

profile of v1, /device:TPU:0, one launch (start us, length us, event | category | flops | bytes accessed | tf_op | source)
XLA Modules:
  0.0 111.3 jit_solution(785255005887682102)
XLA Ops:
  1.0 1.2 %copy-done.5 = bf16[288,1536]{1,0:T(8,128)(2,1)S(1)} copy-done((bf16[288,1536]{1,0:T(8,128)(2,1)S(1)}, bf16[288,1536]{1,0:T(8,128)(2,1)}, u32[]{:S(2)}) %copy-start.5) | copy-done | bytes 884760
  3.3 2.6 %collective-permute-start = (bf16[88,1536]{1,0:T(8,128)(2,1)S(1)}, bf16[88,1536]{1,0:T(8,128)(2,1)}, u32[]{:S(2)}, u32[]{:S(2)}) collective-permute-start(bf16[88,1536]{1,0:T(8,128)(2,1)S(1)} %pick.1), channel_id=1, source_target_pairs={{0,2},{1,3},{2,0},{3,1},{4,6},{5,7},{6,4},{7,5},{8,10},{9,11},{10,... | collective-permute-start | bytes 811016 | tf_op jit(solution)/shard_map/ppermute | solution.py:173
  5.9 2.5 %collective-permute-start.12 = (bf16[88,1536]{1,0:T(8,128)(2,1)S(1)}, bf16[88,1536]{1,0:T(8,128)(2,1)}, u32[]{:S(2)}, u32[]{:S(2)}) collective-permute-start(bf16[88,1536]{1,0:T(8,128)(2,1)S(1)} %pick.1), channel_id=1, source_target_pairs={{0,6},{1,7},{2,4},{3,5},{4,2},{5,3},{6,0},{7,1},{8,14},{9,15},{10,... | collective-permute-start | bytes 811016 | tf_op jit(solution)/shard_map/ppermute | solution.py:173
  8.4 4.8 %collective-permute-done = bf16[88,1536]{1,0:T(8,128)(2,1)} collective-permute-done((bf16[88,1536]{1,0:T(8,128)(2,1)S(1)}, bf16[88,1536]{1,0:T(8,128)(2,1)}, u32[]{:S(2)}, u32[]{:S(2)}) %collective-permute-start) | collective-permute-done | bytes 270368 | tf_op jit(solution)/shard_map/ppermute | solution.py:173
  13.2 3.1 %collective-permute-start.11 = (bf16[88,1536]{1,0:T(8,128)(2,1)S(1)}, bf16[88,1536]{1,0:T(8,128)(2,1)S(1)}, u32[]{:S(2)}, u32[]{:S(2)}) collective-permute-start(bf16[88,1536]{1,0:T(8,128)(2,1)S(1)} %pick.1), channel_id=1, source_target_pairs={{0,4},{1,5},{2,6},{3,7},{4,0},{5,1},{6,2},{7,3},{8,12},{9,13},{10,... | collective-permute-start | bytes 811016 | tf_op jit(solution)/shard_map/ppermute | solution.py:173
  16.3 1.0 pad_maximum_fusion.x_ref
  17.3 1.9 %copy-done = bf16[1,1536,1024]{2,1,0:T(8,128)(2,1)S(1)} copy-done((bf16[1,1536,1024]{2,1,0:T(8,128)(2,1)S(1)}, bf16[1,1536,1024]{2,1,0:T(8,128)(2,1)}, u32[]{:S(2)}) %copy-start) | copy-done | bytes 3145752
  19.2 1.9 %copy-done.2 = bf16[1,1536,1024]{2,1,0:T(8,128)(2,1)S(1)} copy-done((bf16[1,1536,1024]{2,1,0:T(8,128)(2,1)S(1)}, bf16[1,1536,1024]{2,1,0:T(8,128)(2,1)}, u32[]{:S(2)}) %copy-start.2) | copy-done | bytes 3145752
  21.1 7.1 %project.2 = (f32[176,1024]{1,0:T(8,128)S(1)}, bf16[176,1024]{1,0:T(8,128)(2,1)S(1)}, bf16[176,1024]{1,0:T(8,128)(2,1)S(1)}, bf16[176,1024]{1,0:T(8,128)(2,1)S(1)}) custom-call(s32[4]{0:T(128)S(1)} %iota_xor_fusion.col, bf16[176,1536]{1,0:T(8,128)(2,1)S(1)} %pad_maximum_fusion.x_ref, bf16[1536,1024]{1,0:T(8,128)(2,1)S(1)} %bitcast.6, ...), custom_call_target="tpu_custom_call" | custom-call | tf_op jit(solution)/shard_map/project/pallas_call | solution.py:93
  28.2 1.6 %collective-permute-start.3 = (bf16[176,1024]{1,0:T(8,128)(2,1)S(1)}, bf16[176,1024]{1,0:T(8,128)(2,1)S(1)}, u32[]{:S(2)}, u32[]{:S(2)}) collective-permute-start(bf16[176,1024]{1,0:T(8,128)(2,1)S(1)} %get-tuple-element.14), channel_id=1, source_target_pairs={{0,8},{8,0},{16,24},{24,16},{1,9},{9,1},{17,25},{25,17},{2,10},{10... | collective-permute-start | bytes 1081352 | tf_op jit(solution)/shard_map/ppermute | solution.py:173
  29.8 1.5 %collective-permute-start.4 = (bf16[176,1024]{1,0:T(8,128)(2,1)S(1)}, bf16[176,1024]{1,0:T(8,128)(2,1)S(1)}, u32[]{:S(2)}, u32[]{:S(2)}) collective-permute-start(bf16[176,1024]{1,0:T(8,128)(2,1)S(1)} %get-tuple-element.15), channel_id=1, source_target_pairs={{0,16},{8,24},{16,0},{24,8},{1,17},{9,25},{17,1},{25,9},{2,18},{10... | collective-permute-start | bytes 1081352 | tf_op jit(solution)/shard_map/ppermute | solution.py:173
  32.7 1.0 pad_maximum_fusion.1.x_ref
  33.7 6.3 %project.3 = (f32[176,1024]{1,0:T(8,128)S(1)}, bf16[176,1024]{1,0:T(8,128)(2,1)S(1)}, bf16[176,1024]{1,0:T(8,128)(2,1)S(1)}, bf16[176,1024]{1,0:T(8,128)(2,1)S(1)}) custom-call(s32[4]{0:T(128)S(1)} %iota_xor_fusion.col, bf16[176,1536]{1,0:T(8,128)(2,1)S(1)} %pad_maximum_fusion.1.x_ref, bf16[1536,1024]{1,0:T(8,128)(2,1)S(1)} %bitcast.7, ...), custom_call_target="tpu_custom_call" | custom-call | tf_op jit(solution)/shard_map/project/pallas_call | solution.py:93
  40.0 1.5 %collective-permute-start.13 = (bf16[176,1024]{1,0:T(8,128)(2,1)S(1)}, bf16[176,1024]{1,0:T(8,128)(2,1)S(1)}, u32[]{:S(2)}, u32[]{:S(2)}) collective-permute-start(bf16[176,1024]{1,0:T(8,128)(2,1)S(1)} %get-tuple-element.18), channel_id=1, source_target_pairs={{0,8},{8,0},{16,24},{24,16},{1,9},{9,1},{17,25},{25,17},{2,10},{10... | collective-permute-start | bytes 1081352 | tf_op jit(solution)/shard_map/ppermute | solution.py:173
  41.6 1.5 %collective-permute-start.14 = (bf16[176,1024]{1,0:T(8,128)(2,1)S(1)}, bf16[176,1024]{1,0:T(8,128)(2,1)S(1)}, u32[]{:S(2)}, u32[]{:S(2)}) collective-permute-start(bf16[176,1024]{1,0:T(8,128)(2,1)S(1)} %get-tuple-element.19), channel_id=1, source_target_pairs={{0,16},{8,24},{16,0},{24,8},{1,17},{9,25},{17,1},{25,9},{2,18},{10... | collective-permute-start | bytes 1081352 | tf_op jit(solution)/shard_map/ppermute | solution.py:173
  43.1 3.6 %collective-permute-done.4 = bf16[176,1024]{1,0:T(8,128)(2,1)S(1)} collective-permute-done((bf16[176,1024]{1,0:T(8,128)(2,1)S(1)}, bf16[176,1024]{1,0:T(8,128)(2,1)S(1)}, u32[]{:S(2)}, u32[]{:S(2)}) %collective-permute-start.4) | collective-permute-done | bytes 360480 | tf_op jit(solution)/shard_map/ppermute | solution.py:173
  47.0 1.3 %collective-permute-done.5 = bf16[176,1024]{1,0:T(8,128)(2,1)S(1)} collective-permute-done((bf16[176,1024]{1,0:T(8,128)(2,1)S(1)}, bf16[176,1024]{1,0:T(8,128)(2,1)S(1)}, u32[]{:S(2)}, u32[]{:S(2)}) %collective-permute-start.5) | collective-permute-done | bytes 360480 | tf_op jit(solution)/shard_map/ppermute | solution.py:173
  48.7 1.5 %collective-permute-start.8 = (bf16[176,512]{1,0:T(8,128)(2,1)S(1)}, bf16[176,512]{1,0:T(8,128)(2,1)S(1)}, u32[]{:S(2)}, u32[]{:S(2)}) collective-permute-start(bf16[176,512]{1,0:T(8,128)(2,1)S(1)} %fusion.1.refs_0_), channel_id=1, source_target_pairs={{0,24},{8,16},{16,8},{24,0},{1,25},{9,17},{17,9},{25,1},{2,26},{10... | collective-permute-start | bytes 540680 | tf_op jit(solution)/shard_map/ppermute | solution.py:173
  50.2 4.9 %collective-permute-done.13 = bf16[176,1024]{1,0:T(8,128)(2,1)S(1)} collective-permute-done((bf16[176,1024]{1,0:T(8,128)(2,1)S(1)}, bf16[176,1024]{1,0:T(8,128)(2,1)S(1)}, u32[]{:S(2)}, u32[]{:S(2)}) %collective-permute-start.13) | collective-permute-done | bytes 360480 | tf_op jit(solution)/shard_map/ppermute | solution.py:173
  55.1 1.5 %collective-permute-start.7 = (bf16[176,512]{1,0:T(8,128)(2,1)S(1)}, bf16[176,512]{1,0:T(8,128)(2,1)S(1)}, u32[]{:S(2)}, u32[]{:S(2)}) collective-permute-start(bf16[176,512]{1,0:T(8,128)(2,1)S(1)} %fusion.1.refs_0_), channel_id=1, source_target_pairs={{0,16},{8,24},{16,0},{24,8},{1,17},{9,25},{17,1},{25,9},{2,18},{10... | collective-permute-start | bytes 540680 | tf_op jit(solution)/shard_map/ppermute | solution.py:173
  56.7 9.5 %collective-permute-done.14 = bf16[176,1024]{1,0:T(8,128)(2,1)S(1)} collective-permute-done((bf16[176,1024]{1,0:T(8,128)(2,1)S(1)}, bf16[176,1024]{1,0:T(8,128)(2,1)S(1)}, u32[]{:S(2)}, u32[]{:S(2)}) %collective-permute-start.14) | collective-permute-done | bytes 360480 | tf_op jit(solution)/shard_map/ppermute | solution.py:173
  66.5 4.0 %collective-permute-start.18 = (bf16[176,512]{1,0:T(8,128)(2,1)S(1)}, bf16[176,512]{1,0:T(8,128)(2,1)S(1)}, u32[]{:S(2)}, u32[]{:S(2)}) collective-permute-start(bf16[176,512]{1,0:T(8,128)(2,1)S(1)} %fusion.refs_0_), channel_id=1, source_target_pairs={{0,24},{8,16},{16,8},{24,0},{1,25},{9,17},{17,9},{25,1},{2,26},{10... | collective-permute-start | bytes 540680 | tf_op jit(solution)/shard_map/ppermute | solution.py:173
  71.2 2.4 %collective-permute-done.6.refs_1_ = bf16[176,512]{1,0:T(8,128)(2,1)S(1)} collective-permute-done((bf16[176,512]{1,0:T(8,128)(2,1)S(1)}, bf16[176,512]{1,0:T(8,128)(2,1)S(1)}, u32[]{:S(2)}, u32[]{:S(2)}) %collective-permute-start.6) | collective-permute-done | bytes 180256 | tf_op jit(solution)/shard_map/ppermute | solution.py:173
  73.6 2.5 %down.2 = bf16[176,1536]{1,0:T(8,128)(2,1)S(1)} custom-call(s32[4]{0:T(128)S(1)} %iota_xor_fusion.col, bf16[176,512]{1,0:T(8,128)(2,1)S(1)} %fusion.1.refs_0_, bf16[176,512]{1,0:T(8,128)(2,1)S(1)} %collective-permute-done.6.refs_1_, bf16[176,512]{1,0:T(8,128)(2,1)S(1)} %collective-permute-done.7.refs_2_, ...), custom_call_target="tpu_custom_call" | custom-call | tf_op jit(solution)/shard_map/down/pallas_call | solution.py:134
  76.2 2.3 %collective-permute-done.18.refs_3_ = bf16[176,512]{1,0:T(8,128)(2,1)S(1)} collective-permute-done((bf16[176,512]{1,0:T(8,128)(2,1)S(1)}, bf16[176,512]{1,0:T(8,128)(2,1)S(1)}, u32[]{:S(2)}, u32[]{:S(2)}) %collective-permute-start.18) | collective-permute-done | bytes 180256 | tf_op jit(solution)/shard_map/ppermute | solution.py:173
  78.4 1.9 %collective-permute-done.16.refs_1_ = bf16[176,512]{1,0:T(8,128)(2,1)S(1)} collective-permute-done((bf16[176,512]{1,0:T(8,128)(2,1)S(1)}, bf16[176,512]{1,0:T(8,128)(2,1)S(1)}, u32[]{:S(2)}, u32[]{:S(2)}) %collective-permute-start.16) | collective-permute-done | bytes 180256 | tf_op jit(solution)/shard_map/ppermute | solution.py:173
  80.3 2.5 %down.3 = bf16[176,1536]{1,0:T(8,128)(2,1)S(1)} custom-call(s32[4]{0:T(128)S(1)} %iota_xor_fusion.col, bf16[176,512]{1,0:T(8,128)(2,1)S(1)} %fusion.refs_0_, bf16[176,512]{1,0:T(8,128)(2,1)S(1)} %collective-permute-done.16.refs_1_, bf16[176,512]{1,0:T(8,128)(2,1)S(1)} %collective-permute-done.17.refs_2_, ...), custom_call_target="tpu_custom_call" | custom-call | tf_op jit(solution)/shard_map/down/pallas_call | solution.py:134
  82.9 3.3 %collective-permute-start.20 = (bf16[88,1536]{1,0:T(8,128)(2,1)S(1)}, bf16[88,1536]{1,0:T(8,128)(2,1)S(1)}, u32[]{:S(2)}, u32[]{:S(2)}) collective-permute-start(bf16[88,1536]{1,0:T(8,128)(2,1)S(1)} %get-tuple-element.21), channel_id=1, source_target_pairs={{0,6},{1,7},{2,4},{3,5},{4,2},{5,3},{6,0},{7,1},{8,14},{9,15},{10,... | collective-permute-start | bytes 811016 | tf_op jit(solution)/shard_map/ppermute | solution.py:173
  86.1 1.1 collective-permute-start.19
  87.3 6.9 %collective-permute-done.20.refs_3_ = bf16[88,1536]{1,0:T(8,128)(2,1)S(1)} collective-permute-done((bf16[88,1536]{1,0:T(8,128)(2,1)S(1)}, bf16[88,1536]{1,0:T(8,128)(2,1)S(1)}, u32[]{:S(2)}, u32[]{:S(2)}) %collective-permute-start.20) | collective-permute-done | bytes 270368 | tf_op jit(solution)/shard_map/ppermute | solution.py:173
  94.2 14.4 %collective-permute-done.19.refs_2_ = bf16[88,1536]{1,0:T(8,128)(2,1)S(1)} collective-permute-done((bf16[88,1536]{1,0:T(8,128)(2,1)S(1)}, bf16[88,1536]{1,0:T(8,128)(2,1)S(1)}, u32[]{:S(2)}, u32[]{:S(2)}) %collective-permute-start.19) | collective-permute-done | bytes 270368 | tf_op jit(solution)/shard_map/ppermute | solution.py:173
  108.6 2.7 %combine.1 = bf16[288,1536]{1,0:T(8,128)(2,1)} custom-call(s32[2,288]{1,0:T(2,128)S(1)} %bitcast.15, f32[2,288]{1,0:T(2,128)S(1)} %bitcast.16, bf16[88,1536]{1,0:T(8,128)(2,1)S(1)} %get-tuple-element.24.refs_0_, bf16[88,1536]{1,0:T(8,128)(2,1)S(1)} %collective-permute-done.10.refs_1_, bf16[88,1536]{1,0:T(8,128)(2,1)S(1)} %collective-permute-done.19.refs_2_, ...), custom_call_target="tpu_custom_call" | custom-call | tf_op jit(solution)/shard_map/combine/pallas_call | solution.py:161
  (43 shorter events, 5.4 us)
Async XLA Ops:
  0.0 17.3 %collective-permute-start.1 = (bf16[1536,1024]{1,0:T(8,128)(2,1)}, bf16[1536,1024]{1,0:T(8,128)(2,1)}, u32[]{:S(2)}, u32[]{:S(2)}) collective-permute-start(bf16[1536,1024]{1,0:T(8,128)(2,1)} %bitcast.5), channel_id=1, source_target_pairs={{0,1},{1,0},{2,3},{3,2},{4,5},{5,4},{6,7},{7,6},{8,9},{9,8},{10,11... | collective-permute-start | bytes 9437192 | tf_op jit(solution)/shard_map/ppermute | solution.py:173
  0.5 16.9 %collective-permute-start.2 = (bf16[1536,1024]{1,0:T(8,128)(2,1)}, bf16[1536,1024]{1,0:T(8,128)(2,1)}, u32[]{:S(2)}, u32[]{:S(2)}) collective-permute-start(bf16[1536,1024]{1,0:T(8,128)(2,1)} %bitcast.8), channel_id=1, source_target_pairs={{0,1},{1,0},{2,3},{3,2},{4,5},{5,4},{6,7},{7,6},{8,9},{9,8},{10,11... | collective-permute-start | bytes 9437192 | tf_op jit(solution)/shard_map/ppermute | solution.py:173
  0.5 70.0 %collective-permute-start.9 = (bf16[1024,1536]{1,0:T(8,128)(2,1)}, bf16[1024,1536]{1,0:T(8,128)(2,1)S(1)}, u32[]{:S(2)}, u32[]{:S(2)}) collective-permute-start(bf16[1024,1536]{1,0:T(8,128)(2,1)} %bitcast.11), channel_id=1, source_target_pairs={{0,1},{1,0},{2,3},{3,2},{4,5},{5,4},{6,7},{7,6},{8,9},{9,8},{10,11... | collective-permute-start | bytes 9437192 | tf_op jit(solution)/shard_map/ppermute | solution.py:173
  1.0 1.2 %copy-start.5 = (bf16[288,1536]{1,0:T(8,128)(2,1)S(1)}, bf16[288,1536]{1,0:T(8,128)(2,1)}, u32[]{:S(2)}) copy-start(bf16[288,1536]{1,0:T(8,128)(2,1)} %tokens_ref.1) | copy-start | bytes 2654212
  2.1 0.7 copy-start.6
  3.3 9.9 %collective-permute-start = (bf16[88,1536]{1,0:T(8,128)(2,1)S(1)}, bf16[88,1536]{1,0:T(8,128)(2,1)}, u32[]{:S(2)}, u32[]{:S(2)}) collective-permute-start(bf16[88,1536]{1,0:T(8,128)(2,1)S(1)} %pick.1), channel_id=1, source_target_pairs={{0,2},{1,3},{2,0},{3,1},{4,6},{5,7},{6,4},{7,5},{8,10},{9,11},{10,... | collective-permute-start | bytes 811016 | tf_op jit(solution)/shard_map/ppermute | solution.py:173
  5.9 25.4 %collective-permute-start.12 = (bf16[88,1536]{1,0:T(8,128)(2,1)S(1)}, bf16[88,1536]{1,0:T(8,128)(2,1)}, u32[]{:S(2)}, u32[]{:S(2)}) collective-permute-start(bf16[88,1536]{1,0:T(8,128)(2,1)S(1)} %pick.1), channel_id=1, source_target_pairs={{0,6},{1,7},{2,4},{3,5},{4,2},{5,3},{6,0},{7,1},{8,14},{9,15},{10,... | collective-permute-start | bytes 811016 | tf_op jit(solution)/shard_map/ppermute | solution.py:173
  13.2 19.5 %collective-permute-start.11 = (bf16[88,1536]{1,0:T(8,128)(2,1)S(1)}, bf16[88,1536]{1,0:T(8,128)(2,1)S(1)}, u32[]{:S(2)}, u32[]{:S(2)}) collective-permute-start(bf16[88,1536]{1,0:T(8,128)(2,1)S(1)} %pick.1), channel_id=1, source_target_pairs={{0,4},{1,5},{2,6},{3,7},{4,0},{5,1},{6,2},{7,3},{8,12},{9,13},{10,... | collective-permute-start | bytes 811016 | tf_op jit(solution)/shard_map/ppermute | solution.py:173
  17.3 1.9 %copy-start = (bf16[1,1536,1024]{2,1,0:T(8,128)(2,1)S(1)}, bf16[1,1536,1024]{2,1,0:T(8,128)(2,1)}, u32[]{:S(2)}) copy-start(bf16[1,1536,1024]{2,1,0:T(8,128)(2,1)} %param.10) | copy-start | bytes 9437188
  19.2 1.9 %copy-start.2 = (bf16[1,1536,1024]{2,1,0:T(8,128)(2,1)S(1)}, bf16[1,1536,1024]{2,1,0:T(8,128)(2,1)}, u32[]{:S(2)}) copy-start(bf16[1,1536,1024]{2,1,0:T(8,128)(2,1)} %param.11) | copy-start | bytes 9437188
  21.1 12.6 %copy-start.1 = (bf16[1,1536,1024]{2,1,0:T(8,128)(2,1)S(1)}, bf16[1,1536,1024]{2,1,0:T(8,128)(2,1)}, u32[]{:S(2)}) copy-start(bf16[1,1536,1024]{2,1,0:T(8,128)(2,1)} %param.10) | copy-start | bytes 9437188
  21.1 12.6 %copy-start.3 = (bf16[1,1536,1024]{2,1,0:T(8,128)(2,1)S(1)}, bf16[1,1536,1024]{2,1,0:T(8,128)(2,1)}, u32[]{:S(2)}) copy-start(bf16[1,1536,1024]{2,1,0:T(8,128)(2,1)} %param.11) | copy-start | bytes 9437188
  28.2 13.3 %collective-permute-start.3 = (bf16[176,1024]{1,0:T(8,128)(2,1)S(1)}, bf16[176,1024]{1,0:T(8,128)(2,1)S(1)}, u32[]{:S(2)}, u32[]{:S(2)}) collective-permute-start(bf16[176,1024]{1,0:T(8,128)(2,1)S(1)} %get-tuple-element.14), channel_id=1, source_target_pairs={{0,8},{8,0},{16,24},{24,16},{1,9},{9,1},{17,25},{25,17},{2,10},{10... | collective-permute-start | bytes 1081352 | tf_op jit(solution)/shard_map/ppermute | solution.py:173
  29.8 17.0 %collective-permute-start.4 = (bf16[176,1024]{1,0:T(8,128)(2,1)S(1)}, bf16[176,1024]{1,0:T(8,128)(2,1)S(1)}, u32[]{:S(2)}, u32[]{:S(2)}) collective-permute-start(bf16[176,1024]{1,0:T(8,128)(2,1)S(1)} %get-tuple-element.15), channel_id=1, source_target_pairs={{0,16},{8,24},{16,0},{24,8},{1,17},{9,25},{17,1},{25,9},{2,18},{10... | collective-permute-start | bytes 1081352 | tf_op jit(solution)/shard_map/ppermute | solution.py:173
  31.3 17.1 %collective-permute-start.5 = (bf16[176,1024]{1,0:T(8,128)(2,1)S(1)}, bf16[176,1024]{1,0:T(8,128)(2,1)S(1)}, u32[]{:S(2)}, u32[]{:S(2)}) collective-permute-start(bf16[176,1024]{1,0:T(8,128)(2,1)S(1)} %get-tuple-element.16), channel_id=1, source_target_pairs={{0,24},{8,16},{16,8},{24,0},{1,25},{9,17},{17,9},{25,1},{2,26},{10... | collective-permute-start | bytes 1081352 | tf_op jit(solution)/shard_map/ppermute | solution.py:173
  40.0 15.1 %collective-permute-start.13 = (bf16[176,1024]{1,0:T(8,128)(2,1)S(1)}, bf16[176,1024]{1,0:T(8,128)(2,1)S(1)}, u32[]{:S(2)}, u32[]{:S(2)}) collective-permute-start(bf16[176,1024]{1,0:T(8,128)(2,1)S(1)} %get-tuple-element.18), channel_id=1, source_target_pairs={{0,8},{8,0},{16,24},{24,16},{1,9},{9,1},{17,25},{25,17},{2,10},{10... | collective-permute-start | bytes 1081352 | tf_op jit(solution)/shard_map/ppermute | solution.py:173
  41.6 24.6 %collective-permute-start.14 = (bf16[176,1024]{1,0:T(8,128)(2,1)S(1)}, bf16[176,1024]{1,0:T(8,128)(2,1)S(1)}, u32[]{:S(2)}, u32[]{:S(2)}) collective-permute-start(bf16[176,1024]{1,0:T(8,128)(2,1)S(1)} %get-tuple-element.19), channel_id=1, source_target_pairs={{0,16},{8,24},{16,0},{24,8},{1,17},{9,25},{17,1},{25,9},{2,18},{10... | collective-permute-start | bytes 1081352 | tf_op jit(solution)/shard_map/ppermute | solution.py:173
  46.7 19.5 %collective-permute-start.15 = (bf16[176,1024]{1,0:T(8,128)(2,1)S(1)}, bf16[176,1024]{1,0:T(8,128)(2,1)S(1)}, u32[]{:S(2)}, u32[]{:S(2)}) collective-permute-start(bf16[176,1024]{1,0:T(8,128)(2,1)S(1)} %get-tuple-element.20), channel_id=1, source_target_pairs={{0,24},{8,16},{16,8},{24,0},{1,25},{9,17},{17,9},{25,1},{2,26},{10... | collective-permute-start | bytes 1081352 | tf_op jit(solution)/shard_map/ppermute | solution.py:173
  48.4 25.2 %copy-start.4 = (bf16[1,1024,1536]{2,1,0:T(8,128)(2,1)S(1)}, bf16[1,1024,1536]{2,1,0:T(8,128)(2,1)}, u32[]{:S(2)}) copy-start(bf16[1,1024,1536]{2,1,0:T(8,128)(2,1)} %param.12) | copy-start | bytes 9437188
  48.7 21.8 %collective-permute-start.8 = (bf16[176,512]{1,0:T(8,128)(2,1)S(1)}, bf16[176,512]{1,0:T(8,128)(2,1)S(1)}, u32[]{:S(2)}, u32[]{:S(2)}) collective-permute-start(bf16[176,512]{1,0:T(8,128)(2,1)S(1)} %fusion.1.refs_0_), channel_id=1, source_target_pairs={{0,24},{8,16},{16,8},{24,0},{1,25},{9,17},{17,9},{25,1},{2,26},{10... | collective-permute-start | bytes 540680 | tf_op jit(solution)/shard_map/ppermute | solution.py:173
  55.1 16.1 %collective-permute-start.7 = (bf16[176,512]{1,0:T(8,128)(2,1)S(1)}, bf16[176,512]{1,0:T(8,128)(2,1)S(1)}, u32[]{:S(2)}, u32[]{:S(2)}) collective-permute-start(bf16[176,512]{1,0:T(8,128)(2,1)S(1)} %fusion.1.refs_0_), channel_id=1, source_target_pairs={{0,16},{8,24},{16,0},{24,8},{1,17},{9,25},{17,1},{25,9},{2,18},{10... | collective-permute-start | bytes 540680 | tf_op jit(solution)/shard_map/ppermute | solution.py:173
  66.2 7.4 %collective-permute-start.6 = (bf16[176,512]{1,0:T(8,128)(2,1)S(1)}, bf16[176,512]{1,0:T(8,128)(2,1)S(1)}, u32[]{:S(2)}, u32[]{:S(2)}) collective-permute-start(bf16[176,512]{1,0:T(8,128)(2,1)S(1)} %fusion.1.refs_0_), channel_id=1, source_target_pairs={{0,8},{8,0},{16,24},{24,16},{1,9},{9,1},{17,25},{25,17},{2,10},{10... | collective-permute-start | bytes 540680 | tf_op jit(solution)/shard_map/ppermute | solution.py:173
  66.5 11.9 %collective-permute-start.18 = (bf16[176,512]{1,0:T(8,128)(2,1)S(1)}, bf16[176,512]{1,0:T(8,128)(2,1)S(1)}, u32[]{:S(2)}, u32[]{:S(2)}) collective-permute-start(bf16[176,512]{1,0:T(8,128)(2,1)S(1)} %fusion.refs_0_), channel_id=1, source_target_pairs={{0,24},{8,16},{16,8},{24,0},{1,25},{9,17},{17,9},{25,1},{2,26},{10... | collective-permute-start | bytes 540680 | tf_op jit(solution)/shard_map/ppermute | solution.py:173
  70.5 7.9 %collective-permute-start.17 = (bf16[176,512]{1,0:T(8,128)(2,1)S(1)}, bf16[176,512]{1,0:T(8,128)(2,1)S(1)}, u32[]{:S(2)}, u32[]{:S(2)}) collective-permute-start(bf16[176,512]{1,0:T(8,128)(2,1)S(1)} %fusion.refs_0_), channel_id=1, source_target_pairs={{0,16},{8,24},{16,0},{24,8},{1,17},{9,25},{17,1},{25,9},{2,18},{10... | collective-permute-start | bytes 540680 | tf_op jit(solution)/shard_map/ppermute | solution.py:173
  70.5 9.8 %collective-permute-start.16 = (bf16[176,512]{1,0:T(8,128)(2,1)S(1)}, bf16[176,512]{1,0:T(8,128)(2,1)S(1)}, u32[]{:S(2)}, u32[]{:S(2)}) collective-permute-start(bf16[176,512]{1,0:T(8,128)(2,1)S(1)} %fusion.refs_0_), channel_id=1, source_target_pairs={{0,8},{8,0},{16,24},{24,16},{1,9},{9,1},{17,25},{25,17},{2,10},{10... | collective-permute-start | bytes 540680 | tf_op jit(solution)/shard_map/ppermute | solution.py:173
  76.1 32.5 %copy-start.7 = (s32[288,2]{0,1:T(2,128)S(1)}, s32[288,2]{0,1:T(2,128)}, u32[]{:S(2)}) copy-start(s32[288,2]{0,1:T(2,128)} %param.8) | copy-start | bytes 6916
  76.1 32.5 %copy-start.8 = (f32[288,2]{0,1:T(2,128)S(1)}, f32[288,2]{0,1:T(2,128)}, u32[]{:S(2)}) copy-start(f32[288,2]{0,1:T(2,128)} %param.9) | copy-start | bytes 6916
  82.9 11.4 %collective-permute-start.20 = (bf16[88,1536]{1,0:T(8,128)(2,1)S(1)}, bf16[88,1536]{1,0:T(8,128)(2,1)S(1)}, u32[]{:S(2)}, u32[]{:S(2)}) collective-permute-start(bf16[88,1536]{1,0:T(8,128)(2,1)S(1)} %get-tuple-element.21), channel_id=1, source_target_pairs={{0,6},{1,7},{2,4},{3,5},{4,2},{5,3},{6,0},{7,1},{8,14},{9,15},{10,... | collective-permute-start | bytes 811016 | tf_op jit(solution)/shard_map/ppermute | solution.py:173
  86.1 22.5 %collective-permute-start.19 = (bf16[88,1536]{1,0:T(8,128)(2,1)S(1)}, bf16[88,1536]{1,0:T(8,128)(2,1)S(1)}, u32[]{:S(2)}, u32[]{:S(2)}) collective-permute-start(bf16[88,1536]{1,0:T(8,128)(2,1)S(1)} %get-tuple-element.22), channel_id=1, source_target_pairs={{0,4},{1,5},{2,6},{3,7},{4,0},{5,1},{6,2},{7,3},{8,12},{9,13},{10,... | collective-permute-start | bytes 811016 | tf_op jit(solution)/shard_map/ppermute | solution.py:173
  87.2 21.4 %collective-permute-start.10 = (bf16[88,1536]{1,0:T(8,128)(2,1)S(1)}, bf16[88,1536]{1,0:T(8,128)(2,1)S(1)}, u32[]{:S(2)}, u32[]{:S(2)}) collective-permute-start(bf16[88,1536]{1,0:T(8,128)(2,1)S(1)} %get-tuple-element.23), channel_id=1, source_target_pairs={{0,2},{1,3},{2,0},{3,1},{4,6},{5,7},{6,4},{7,5},{8,10},{9,11},{10,... | collective-permute-start | bytes 811016 | tf_op jit(solution)/shard_map/ppermute | solution.py:173

commit v2 on v0

v2 whole, which is shorter than its diff:
```python
import functools
import jax
import jax.numpy as jnp
from jax import lax
from jax.experimental import pallas as pl
from jax.experimental.pallas import tpu as pltpu
from jax.sharding import PartitionSpec as P

CAP = 81
LIMIT = 8 * 1024 * 1024
GROUPS = ((0, 1), (3,), (2,))
SEQ = ("P0", "P1", "A0", "P2", "A1", "D1", "A2", "D0", "D2")
WAIT = 1
ZORDER = (1, 3, 2)


def call(kernel, name, outs, args, after=(), flops=0):
    def body(*refs):
        kernel(*refs[len(after) :])

    return pl.pallas_call(
        body,
        out_shape=outs,
        in_specs=[pl.BlockSpec(memory_space=pl.ANY)] * len(after)
        + [pl.BlockSpec(memory_space=pltpu.VMEM)] * len(args),
        out_specs=[pl.BlockSpec(memory_space=pltpu.VMEM)] * len(outs),
        compiler_params=pltpu.CompilerParams(vmem_limit_bytes=LIMIT),
        cost_estimate=pl.CostEstimate(flops=flops, bytes_accessed=0, transcendentals=0),
        name=name,
    )(*after, *args)


def slot_hits(ids, slots):
    tokens = ids.shape[1]
    routed = jnp.max(jnp.where(ids == 0, 1.0, 0.0), axis=0, keepdims=True)
    upto = lax.broadcasted_iota(jnp.int32, (tokens, tokens), 0) <= lax.broadcasted_iota(
        jnp.int32, (tokens, tokens), 1
    )
    place = jnp.dot(
        jnp.broadcast_to(routed, (8, tokens)).astype(jnp.bfloat16),
        jnp.where(upto, 1.0, 0.0).astype(jnp.bfloat16),
        preferred_element_type=jnp.float32,
    )[0:1]
    place = jnp.where(routed > 0, place, 0.0)
    numbers = lax.broadcasted_iota(jnp.int32, (slots, tokens), 0).astype(jnp.float32) + 1.0
    return jnp.where(numbers == place, 1.0, 0.0)


def pick_kernel(ids_ref, tokens_ref, out_ref):
    hits = slot_hits(ids_ref[...], out_ref.shape[0])
    out_ref[...] = jnp.dot(
        hits.astype(jnp.bfloat16), tokens_ref[...], preferred_element_type=jnp.float32
    ).astype(out_ref.dtype)


def pick(ids, tokens, slots):
    outs = [jax.ShapeDtypeStruct((slots, tokens.shape[1]), tokens.dtype)]
    return call(pick_kernel, "pick", outs, [ids, tokens], flops=30000000000)[0]


def split(value):
    high = value.astype(jnp.bfloat16)
    return high, (value - high.astype(jnp.float32)).astype(jnp.bfloat16)


def back_kernel(ids_ref, scales_ref, high_ref, low_ref):
    ids = ids_ref[...]
    scale = jnp.sum(jnp.where(ids == 0, scales_ref[...], 0.0), axis=0, keepdims=True)
    high_ref[...], low_ref[...] = split((slot_hits(ids, high_ref.shape[1]) * scale).T)


def back(ids, scales, slots, after):
    outs = [jax.ShapeDtypeStruct((ids.shape[1], slots), jnp.bfloat16)] * 2
    return call(back_kernel, "back", outs, [ids, scales], after)


def project_kernel(parts, n_x, *refs):
    xs, weights, outs = refs[:n_x], refs[n_x:-parts], refs[-parts:]
    me = lax.axis_index("fsdp")
    x = xs[0][...] if n_x == 1 else jnp.concatenate([r[...] for r in xs], axis=0)
    quarter = weights[0].shape[1] // parts
    for k in [*range(parts - 1, 0, -1), 0]:
        cols = pl.ds(pl.multiple_of((me ^ k) * quarter, quarter), quarter)
        for j, w in enumerate(weights):
            outs[k][:, j * quarter : (j + 1) * quarter] = jnp.dot(
                x, w[:, cols], preferred_element_type=jnp.float32
            ).astype(outs[k].dtype)


def project(xs, weights, parts, after):
    rows, depth = len(xs) * xs[0].shape[0], xs[0].shape[1]
    quarter = weights[0].shape[1] // parts
    kinds = [jnp.float32] + [jnp.bfloat16] * (parts - 1)
    if quarter % 128:
        outs = []
        me = lax.axis_index("fsdp")
        x = jnp.concatenate(xs, axis=0)
        for k, kind in enumerate(kinds):
            cut = [
                lax.dynamic_slice_in_dim(w, (me ^ k) * quarter, quarter, axis=1) for w in weights
            ]
            out = jnp.dot(x, jnp.concatenate(cut, axis=1), preferred_element_type=jnp.float32)
            outs.append(out.astype(kind))
        return outs
    outs = [jax.ShapeDtypeStruct((rows, len(weights) * quarter), k) for k in kinds]
    kernel = functools.partial(project_kernel, parts, len(xs))
    flops = 2 * rows * depth * len(weights) * quarter * parts
    return call(kernel, "project", outs, [*xs, *weights], after, flops)


def act_kernel(*refs):
    parts, out_ref = refs[:-1], refs[-1]
    total = parts[0][...]
    for part in parts[1:]:
        total += part[...].astype(jnp.float32)
    half = total.shape[1] // 2
    gate, up = total[:, :half], total[:, half:]
    out_ref[...] = (gate / (1.0 + jnp.exp(-gate)) * up).astype(out_ref.dtype)


def activate(parts, after):
    rows, width = parts[0].shape
    outs = [jax.ShapeDtypeStruct((rows, width // 2), jnp.bfloat16)]
    return call(act_kernel, "act", outs, parts, after)[0]


def down_kernel(parts, n_w, *refs):
    acts, weights, outs = refs[:parts], refs[parts : parts + n_w], refs[parts + n_w :]
    me = lax.axis_index("fsdp")
    quarter = weights[0].shape[0] // parts
    rows = outs[0].shape[0]
    total = None
    for k, act in enumerate(acts):
        depth = pl.ds(pl.multiple_of((me ^ k) * quarter, quarter), quarter)
        for j, w in enumerate(weights):
            term = jnp.dot(
                act[:, j * quarter : (j + 1) * quarter],
                w[depth, :],
                preferred_element_type=jnp.float32,
            )
            total = term if total is None else total + term
    for i, out in enumerate(outs):
        out[...] = total[i * rows : (i + 1) * rows].astype(out.dtype)


def down(acts, weights, blocks, after):
    parts, rows, width = len(acts), acts[0].shape[0], weights[0].shape[1]
    outs = [jax.ShapeDtypeStruct((rows // blocks, width), jnp.bfloat16)] * blocks
    kernel = functools.partial(down_kernel, parts, len(weights))
    flops = 2 * rows * weights[0].shape[0] * len(weights) * width
    return call(kernel, "down", outs, [*acts, *weights], after, flops)


def combine_kernel(back_high, back_low, *refs):
    terms, out_ref = refs[:-1], refs[-1]
    slot_out = terms[0][...].astype(jnp.float32)
    for term in terms[1:]:
        slot_out += term[...].astype(jnp.float32)
    high, low = split(slot_out)
    total = jnp.dot(back_low[...], high, preferred_element_type=jnp.float32)
    total += jnp.dot(back_high[...], low, preferred_element_type=jnp.float32)
    total += jnp.dot(back_high[...], high, preferred_element_type=jnp.float32)
    out_ref[...] = total.astype(out_ref.dtype)


def combine(backs, terms):
    outs = [jax.ShapeDtypeStruct((backs[0].shape[0], terms[0].shape[1]), jnp.bfloat16)]
    return call(combine_kernel, "combine", outs, [*backs, *terms])[0]


def local(n_fsdp, n_ed, groups, zorder, seq, tokens, expert_ids, route_weights, w_gate, w_up, w_down):
    slots = -(-CAP // 8) * 8
    swap = lambda v, axis, size, k: lax.ppermute(v, axis, [(i, i ^ k) for i in range(size)])
    partner = lambda v: swap(v, "ed", n_ed, 1)
    along = lambda v, s: swap(v, "ed", n_ed, 2 * s)
    across = lambda v, k: swap(v, "fsdp", n_fsdp, k)
    own = [w_gate[0], w_up[0], w_down[0]]
    other = [partner(w) for w in own]
    mine = pick(expert_ids.T, tokens, slots)
    backs = back(expert_ids.T, route_weights.T, slots, (mine,))
    blocks = {0: mine}
    for s in zorder:
        blocks[s] = along(mine, s)

    parts, acts, terms, last = {}, {}, [], (backs[0],)
    for word in seq:
        op, g = word[0], int(word[1:])
        group = groups[g]
        if op == "P":
            xs = [blocks[s] for s in group]
            weights = [own[0], other[0], own[1], other[1]]
            out = project(xs, weights, n_fsdp, (*last, other[2]) if g == WAIT else last)
            parts[g] = [out[0]] + [across(out[k], k) for k in range(n_fsdp - 1, 0, -1)][::-1]
            last = (out[0],)
        elif op == "A":
            act = activate(parts[g], last)
            acts[g] = [act] + [across(act, k) for k in range(n_fsdp - 1, 0, -1)][::-1]
            last = (act,)
        else:
            outs = down(acts[g], [own[2], other[2]], len(group), last)
            last = (outs[0],)
            terms += [out if s == 0 else along(out, s) for s, out in zip(group, outs)]
    return combine(backs, terms)


def plan(n_ed):
    if n_ed == 8:
        return GROUPS, ZORDER, SEQ
    half = n_ed // 4
    groups = (tuple(range(half)), tuple(range(half, n_ed // 2)))
    return groups, tuple(range(1, n_ed // 2)), ("P0", "P1", "A0", "A1", "D0", "D1")


def solution(mesh):
    n_fsdp, n_ed = mesh.shape["fsdp"], mesh.shape["ed"]
    return jax.shard_map(
        functools.partial(local, n_fsdp, n_ed, *plan(n_ed)),
        mesh=mesh,
        in_specs=(
            P("ed", "fsdp"),
            P("ed", None),
            P("ed", None),
            P(None, "fsdp", "ed"),
            P(None, "fsdp", "ed"),
            P(None, "ed", "fsdp"),
        ),
        out_specs=P("ed", "fsdp"),
        check_vma=False,
    )
```

time: 630 us -> 88.2 us (0.14)
  waiting for transfers between devices: 370 us -> 35.9 us
  blocking collectives: 80.7 us -> 0 us
  local copies, waits for them, and re-layouts: 80.5 us -> 1.87 us
  other arithmetic: 55 us -> 0 us
  starting transfers between devices: 5.16 us -> 36.6 us
  matrix products: 22.7 us -> 0 us
  between operations: 14 us -> 0.13 us
  Pallas kernels: 0 us -> 13.6 us
    all_gather x4 -> x0, waiting for transfers between devices: 346 us -> none  [the longest x1 124 us: local(): lax.all_gather(w_down[0], 'fsdp', axis=1, tiled=True)]
    all_to_all x1 -> x0, blocking collectives: 50.5 us -> none  [local(): lax.all_to_all(selected, 'fsdp', split_axis=1, concat_axis=2, tiled=True)]
    unnamed x2 -> x0, other arithmetic: 48.9 us -> none
    all_to_all x7 -> x0, local copies, waits for them, and re-layouts: 36.7 us -> none  [the longest x4 19.9 us: local(): lax.all_to_all(stacked, 'fsdp', split_axis=2, concat_axis=1, tiled=True)]
    ppermute x0 -> x27, starting transfers between devices: none -> 36.6 us  [local(): lax.ppermute(v, axis, [(i, i ^ k) for i in range(size)])]
    ppermute x0 -> x27, waiting for transfers between devices: none -> 35.9 us  [local(): lax.ppermute(v, axis, [(i, i ^ k) for i in range(size)])]
    unnamed x1 -> x0, blocking collectives: 30.3 us -> none
    unnamed x20 -> x12, local copies, waits for them, and re-layouts: 26.8 us -> 1.87 us
  transfers between devices with their start and end apart: 6 -> 27, of which waited for: 5 -> 14; matrix products, arithmetic and copies ran while one was open for 7% -> 0% of each run, Pallas kernels for 0% -> 13%
where the time goes in v2:
time: 88.2 us; the launch traced here: 88.1 us
  starting transfers between devices  36.6 us (41%)
  waiting for transfers between devices  35.9 us (41%)
  Pallas kernels  13.6 us (15%)
  local copies, waits for them, and re-layouts  1.87 us (2%)
    ppermute x27, starting transfers between devices, local(): lax.ppermute(v, axis, [(i, i ^ k) for i in range(size)])  36.6 us
    ppermute x27, waiting for transfers between devices, local(): lax.ppermute(v, axis, [(i, i ^ k) for i in range(size)])  35.9 us
    pallas_call x12, Pallas kernels, call(): pl.pallas_call(body, out_shape=outs, in_specs=[pl.BlockSpec(memory_space=...  13.6 us
    unnamed x12, local copies, waits for them, and re-layouts  1.87 us
  transfers between devices with their start and end apart: 27, of which 14 were waited for; matrix products, arithmetic and copies ran while one was open for 0% of the time, Pallas kernels for 13%

profile of v2, /device:TPU:0, one launch (start us, length us, event | category | flops | bytes accessed | tf_op | source)
XLA Modules:
  0.0 88.1 jit_solution(1103197758823265840)
XLA Ops:
  1.7 1.2 %copy-done.5 = bf16[288,1536]{1,0:T(8,128)(2,1)S(1)} copy-done((bf16[288,1536]{1,0:T(8,128)(2,1)S(1)}, bf16[288,1536]{1,0:T(8,128)(2,1)}, u32[]{:S(2)}) %copy-start.5) | copy-done | bytes 884760
  3.3 2.6 %collective-permute-start = (bf16[88,1536]{1,0:T(8,128)(2,1)S(1)}, bf16[88,1536]{1,0:T(8,128)(2,1)S(1)}, u32[]{:S(2)}, u32[]{:S(2)}) collective-permute-start(bf16[88,1536]{1,0:T(8,128)(2,1)S(1)} %pick.1.refs_0_.refs_1_), channel_id=1, source_target_pairs={{0,2},{1,3},{2,0},{3,1},{4,6},{5,7},{6,4},{7,5},{8,10},{9,11},{10,... | collective-permute-start | bytes 811016 | tf_op jit(solution)/shard_map/ppermute | solution.py:173
  5.9 2.5 %collective-permute-start.4 = (bf16[88,1536]{1,0:T(8,128)(2,1)S(1)}, bf16[88,1536]{1,0:T(8,128)(2,1)S(1)}, u32[]{:S(2)}, u32[]{:S(2)}) collective-permute-start(bf16[88,1536]{1,0:T(8,128)(2,1)S(1)} %pick.1.refs_0_.refs_1_), channel_id=1, source_target_pairs={{0,6},{1,7},{2,4},{3,5},{4,2},{5,3},{6,0},{7,1},{8,14},{9,15},{10,... | collective-permute-start | bytes 811016 | tf_op jit(solution)/shard_map/ppermute | solution.py:173
  8.7 4.4 %collective-permute-done.refs_2_ = bf16[88,1536]{1,0:T(8,128)(2,1)S(1)} collective-permute-done((bf16[88,1536]{1,0:T(8,128)(2,1)S(1)}, bf16[88,1536]{1,0:T(8,128)(2,1)S(1)}, u32[]{:S(2)}, u32[]{:S(2)}) %collective-permute-start) | collective-permute-done | bytes 270368 | tf_op jit(solution)/shard_map/ppermute | solution.py:173
  13.1 2.5 %project.3 = (f32[176,1024]{1,0:T(8,128)S(1)}, bf16[176,1024]{1,0:T(8,128)(2,1)S(1)}, bf16[176,1024]{1,0:T(8,128)(2,1)S(1)}, bf16[176,1024]{1,0:T(8,128)(2,1)S(1)}) custom-call(bf16[288,88]{1,0:T(8,128)(2,1)S(1)} %get-tuple-element.21.refs_0_, bf16[88,1536]{1,0:T(8,128)(2,1)S(1)} %pick.1.refs_0_.refs_1_, bf16[88,1536]{1,0:T(8,128)(2,1)S(1)} %collective-permute-done.refs_2_, ...), custom_call_target="tpu_custom_call" | custom-call | flops 2214592512 | tf_op jit(solution)/shard_map/project/pallas_call | solution.py:21
  15.6 1.7 %collective-permute-start.5 = (bf16[176,1024]{1,0:T(8,128)(2,1)S(1)}, bf16[176,1024]{1,0:T(8,128)(2,1)S(1)}, u32[]{:S(2)}, u32[]{:S(2)}) collective-permute-start(bf16[176,1024]{1,0:T(8,128)(2,1)S(1)} %get-tuple-element.25), channel_id=1, source_target_pairs={{0,8},{8,0},{16,24},{24,16},{1,9},{9,1},{17,25},{25,17},{2,10},{10... | collective-permute-start | bytes 1081352 | tf_op jit(solution)/shard_map/ppermute | solution.py:173
  17.3 1.5 %collective-permute-start.6 = (bf16[176,1024]{1,0:T(8,128)(2,1)S(1)}, bf16[176,1024]{1,0:T(8,128)(2,1)S(1)}, u32[]{:S(2)}, u32[]{:S(2)}) collective-permute-start(bf16[176,1024]{1,0:T(8,128)(2,1)S(1)} %get-tuple-element.26), channel_id=1, source_target_pairs={{0,16},{8,24},{16,0},{24,8},{1,17},{9,25},{17,1},{25,9},{2,18},{10... | collective-permute-start | bytes 1081352 | tf_op jit(solution)/shard_map/ppermute | solution.py:173
  19.2 2.0 %collective-permute-done.4.refs_2_ = bf16[88,1536]{1,0:T(8,128)(2,1)S(1)} collective-permute-done((bf16[88,1536]{1,0:T(8,128)(2,1)S(1)}, bf16[88,1536]{1,0:T(8,128)(2,1)S(1)}, u32[]{:S(2)}, u32[]{:S(2)}) %collective-permute-start.4) | collective-permute-done | bytes 270368 | tf_op jit(solution)/shard_map/ppermute | solution.py:173
  21.2 1.7 %collective-permute-start.8 = (bf16[88,1536]{1,0:T(8,128)(2,1)S(1)}, bf16[88,1536]{1,0:T(8,128)(2,1)S(1)}, u32[]{:S(2)}, u32[]{:S(2)}) collective-permute-start(bf16[88,1536]{1,0:T(8,128)(2,1)S(1)} %pick.1.refs_0_.refs_1_), channel_id=1, source_target_pairs={{0,4},{1,5},{2,6},{3,7},{4,0},{5,1},{6,2},{7,3},{8,12},{9,13},{10,... | collective-permute-start | bytes 811016 | tf_op jit(solution)/shard_map/ppermute | solution.py:173
  22.9 2.2 %project.4 = (f32[88,1024]{1,0:T(8,128)S(1)}, bf16[88,1024]{1,0:T(8,128)(2,1)S(1)}, bf16[88,1024]{1,0:T(8,128)(2,1)S(1)}, bf16[88,1024]{1,0:T(8,128)(2,1)S(1)}) custom-call(f32[176,1024]{1,0:T(8,128)S(1)} %get-tuple-element.23.refs_0_.refs_1_, bf16[1024,1536]{1,0:T(8,128)(2,1)S(1)} %collective-permute-done.3.refs_1_.refs_6_, ...), custom_call_target="tpu_custom_call" | custom-call | flops 1107296256 | tf_op jit(solution)/shard_map/project/pallas_call | solution.py:21
  25.2 1.6 %collective-permute-start.9 = (bf16[88,1024]{1,0:T(8,128)(2,1)S(1)}, bf16[88,1024]{1,0:T(8,128)(2,1)S(1)}, u32[]{:S(2)}, u32[]{:S(2)}) collective-permute-start(bf16[88,1024]{1,0:T(8,128)(2,1)S(1)} %get-tuple-element.29), channel_id=1, source_target_pairs={{0,8},{8,0},{16,24},{24,16},{1,9},{9,1},{17,25},{25,17},{2,10},{10... | collective-permute-start | bytes 540680 | tf_op jit(solution)/shard_map/ppermute | solution.py:173
  27.0 1.7 %collective-permute-start.10 = (bf16[88,1024]{1,0:T(8,128)(2,1)S(1)}, bf16[88,1024]{1,0:T(8,128)(2,1)S(1)}, u32[]{:S(2)}, u32[]{:S(2)}) collective-permute-start(bf16[88,1024]{1,0:T(8,128)(2,1)S(1)} %get-tuple-element.30), channel_id=1, source_target_pairs={{0,16},{8,24},{16,0},{24,8},{1,17},{9,25},{17,1},{25,9},{2,18},{10... | collective-permute-start | bytes 540680 | tf_op jit(solution)/shard_map/ppermute | solution.py:173
  28.7 6.2 %collective-permute-done.6.refs_3_ = bf16[176,1024]{1,0:T(8,128)(2,1)S(1)} collective-permute-done((bf16[176,1024]{1,0:T(8,128)(2,1)S(1)}, bf16[176,1024]{1,0:T(8,128)(2,1)S(1)}, u32[]{:S(2)}, u32[]{:S(2)}) %collective-permute-start.6) | collective-permute-done | bytes 360480 | tf_op jit(solution)/shard_map/ppermute | solution.py:173
  36.2 2.2 %project.5 = (f32[88,1024]{1,0:T(8,128)S(1)}, bf16[88,1024]{1,0:T(8,128)(2,1)S(1)}, bf16[88,1024]{1,0:T(8,128)(2,1)S(1)}, bf16[88,1024]{1,0:T(8,128)(2,1)S(1)}) custom-call(bf16[176,512]{1,0:T(8,128)(2,1)S(1)} %act.3.refs_0_.refs_1_, bf16[88,1536]{1,0:T(8,128)(2,1)S(1)} %collective-permute-done.8.refs_1_, bf16[1536,1024]{1,0:T(8,128)(2,1)S(1)} %bitcast.12, ...), custom_call_target="tpu_custom_call" | custom-call | flops 1107296256 | tf_op jit(solution)/shard_map/project/pallas_call | solution.py:21
  38.4 3.0 %collective-permute-start.16 = (bf16[88,1024]{1,0:T(8,128)(2,1)S(1)}, bf16[88,1024]{1,0:T(8,128)(2,1)S(1)}, u32[]{:S(2)}, u32[]{:S(2)}) collective-permute-start(bf16[88,1024]{1,0:T(8,128)(2,1)S(1)} %get-tuple-element.32), channel_id=1, source_target_pairs={{0,8},{8,0},{16,24},{24,16},{1,9},{9,1},{17,25},{25,17},{2,10},{10... | collective-permute-start | bytes 540680 | tf_op jit(solution)/shard_map/ppermute | solution.py:173
  41.4 2.2 %collective-permute-done.11.refs_4_ = bf16[88,1024]{1,0:T(8,128)(2,1)S(1)} collective-permute-done((bf16[88,1024]{1,0:T(8,128)(2,1)S(1)}, bf16[88,1024]{1,0:T(8,128)(2,1)S(1)}, u32[]{:S(2)}, u32[]{:S(2)}) %collective-permute-start.11) | collective-permute-done | bytes 180256 | tf_op jit(solution)/shard_map/ppermute | solution.py:173
  43.8 1.5 %collective-permute-start.14 = (bf16[88,512]{1,0:T(8,128)(2,1)S(1)}, bf16[88,512]{1,0:T(8,128)(2,1)S(1)}, u32[]{:S(2)}, u32[]{:S(2)}) collective-permute-start(bf16[88,512]{1,0:T(8,128)(2,1)S(1)} %act.4.refs_0_.refs_1_), channel_id=1, source_target_pairs={{0,24},{8,16},{16,8},{24,0},{1,25},{9,17},{17,9},{25,1},{2,26},{10... | collective-permute-start | bytes 270344 | tf_op jit(solution)/shard_map/ppermute | solution.py:173
  45.3 1.5 %collective-permute-start.13 = (bf16[88,512]{1,0:T(8,128)(2,1)S(1)}, bf16[88,512]{1,0:T(8,128)(2,1)S(1)}, u32[]{:S(2)}, u32[]{:S(2)}) collective-permute-start(bf16[88,512]{1,0:T(8,128)(2,1)S(1)} %act.4.refs_0_.refs_1_), channel_id=1, source_target_pairs={{0,16},{8,24},{16,0},{24,8},{1,17},{9,25},{17,1},{25,9},{2,18},{10... | collective-permute-start | bytes 270344 | tf_op jit(solution)/shard_map/ppermute | solution.py:173
  47.3 1.4 %collective-permute-start.17 = (bf16[88,1024]{1,0:T(8,128)(2,1)S(1)}, bf16[88,1024]{1,0:T(8,128)(2,1)S(1)}, u32[]{:S(2)}, u32[]{:S(2)}) collective-permute-start(bf16[88,1024]{1,0:T(8,128)(2,1)S(1)} %get-tuple-element.33), channel_id=1, source_target_pairs={{0,16},{8,24},{16,0},{24,8},{1,17},{9,25},{17,1},{25,9},{2,18},{10... | collective-permute-start | bytes 540680 | tf_op jit(solution)/shard_map/ppermute | solution.py:173
  49.4 1.4 %collective-permute-start.18 = (bf16[88,1024]{1,0:T(8,128)(2,1)S(1)}, bf16[88,1024]{1,0:T(8,128)(2,1)S(1)}, u32[]{:S(2)}, u32[]{:S(2)}) collective-permute-start(bf16[88,1024]{1,0:T(8,128)(2,1)S(1)} %get-tuple-element.34), channel_id=1, source_target_pairs={{0,24},{8,16},{16,8},{24,0},{1,25},{9,17},{17,9},{25,1},{2,26},{10... | collective-permute-start | bytes 540680 | tf_op jit(solution)/shard_map/ppermute | solution.py:173
  50.8 3.7 %collective-permute-done.13.refs_3_ = bf16[88,512]{1,0:T(8,128)(2,1)S(1)} collective-permute-done((bf16[88,512]{1,0:T(8,128)(2,1)S(1)}, bf16[88,512]{1,0:T(8,128)(2,1)S(1)}, u32[]{:S(2)}, u32[]{:S(2)}) %collective-permute-start.13) | collective-permute-done | bytes 90144 | tf_op jit(solution)/shard_map/ppermute | solution.py:173
  54.6 3.0 %collective-permute-start.20 = (bf16[176,512]{1,0:T(8,128)(2,1)S(1)}, bf16[176,512]{1,0:T(8,128)(2,1)S(1)}, u32[]{:S(2)}, u32[]{:S(2)}) collective-permute-start(bf16[176,512]{1,0:T(8,128)(2,1)S(1)} %act.3.refs_0_.refs_1_), channel_id=1, source_target_pairs={{0,16},{8,24},{16,0},{24,8},{1,17},{9,25},{17,1},{25,9},{2,18},{10... | collective-permute-start | bytes 540680 | tf_op jit(solution)/shard_map/ppermute | solution.py:173
  57.5 1.5 %collective-permute-start.19 = (bf16[176,512]{1,0:T(8,128)(2,1)S(1)}, bf16[176,512]{1,0:T(8,128)(2,1)S(1)}, u32[]{:S(2)}, u32[]{:S(2)}) collective-permute-start(bf16[176,512]{1,0:T(8,128)(2,1)S(1)} %act.3.refs_0_.refs_1_), channel_id=1, source_target_pairs={{0,8},{8,0},{16,24},{24,16},{1,9},{9,1},{17,25},{25,17},{2,10},{10... | collective-permute-start | bytes 540680 | tf_op jit(solution)/shard_map/ppermute | solution.py:173
  59.1 1.1 %down.3.refs_0_ = bf16[88,1536]{1,0:T(8,128)(2,1)S(1)} custom-call(bf16[88,512]{1,0:T(8,128)(2,1)S(1)} %act.4.refs_0_.refs_1_, bf16[88,512]{1,0:T(8,128)(2,1)S(1)} %act.4.refs_0_.refs_1_, bf16[88,512]{1,0:T(8,128)(2,1)S(1)} %collective-permute-done.12.refs_2_, bf16[88,512]{1,0:T(8,128)(2,1)S(1)} %collective-permute-done.13.refs_3_, ...), custom_call_target="tpu_custom_call" | custom-call | flops 553648128 | tf_op jit(solution)/shard_map/down/pallas_call | solution.py:21
  60.2 3.2 %collective-permute-done.17.refs_3_ = bf16[88,1024]{1,0:T(8,128)(2,1)S(1)} collective-permute-done((bf16[88,1024]{1,0:T(8,128)(2,1)S(1)}, bf16[88,1024]{1,0:T(8,128)(2,1)S(1)}, u32[]{:S(2)}, u32[]{:S(2)}) %collective-permute-start.17) | collective-permute-done | bytes 180256 | tf_op jit(solution)/shard_map/ppermute | solution.py:173
  63.5 3.7 %collective-permute-start.15 = (bf16[88,1536]{1,0:T(8,128)(2,1)S(1)}, bf16[88,1536]{1,0:T(8,128)(2,1)S(1)}, u32[]{:S(2)}, u32[]{:S(2)}) collective-permute-start(bf16[88,1536]{1,0:T(8,128)(2,1)S(1)} %down.3.refs_0_), channel_id=1, source_target_pairs={{0,6},{1,7},{2,4},{3,5},{4,2},{5,3},{6,0},{7,1},{8,14},{9,15},{10,... | collective-permute-start | bytes 811016 | tf_op jit(solution)/shard_map/ppermute | solution.py:173
  67.8 2.5 %collective-permute-start.24 = (bf16[88,512]{1,0:T(8,128)(2,1)S(1)}, bf16[88,512]{1,0:T(8,128)(2,1)S(1)}, u32[]{:S(2)}, u32[]{:S(2)}) collective-permute-start(bf16[88,512]{1,0:T(8,128)(2,1)S(1)} %act.5.refs_0_.refs_1_), channel_id=1, source_target_pairs={{0,16},{8,24},{16,0},{24,8},{1,17},{9,25},{17,1},{25,9},{2,18},{10... | collective-permute-start | bytes 270344 | tf_op jit(solution)/shard_map/ppermute | solution.py:173
  70.9 1.3 %down.4 = (bf16[88,1536]{1,0:T(8,128)(2,1)S(1)}, bf16[88,1536]{1,0:T(8,128)(2,1)S(1)}) custom-call(bf16[88,512]{1,0:T(8,128)(2,1)S(1)} %act.5.refs_0_.refs_1_, bf16[176,512]{1,0:T(8,128)(2,1)S(1)} %act.3.refs_0_.refs_1_, bf16[176,512]{1,0:T(8,128)(2,1)S(1)} %collective-permute-done.19.refs_2_, bf16[176,512]{1,0:T(8,128)(2,1)S(1)} %collective-permute-done.20.refs_3_, ...), custom_call_target="tpu_custom_call" | custom-call | flops 1107296256 | tf_op jit(solution)/shard_map/down/pallas_call | solution.py:21
  74.8 1.1 %down.5 = bf16[88,1536]{1,0:T(8,128)(2,1)S(1)} custom-call(bf16[88,1536]{1,0:T(8,128)(2,1)S(1)} %get-tuple-element.35.refs_0_.refs_3_, bf16[88,512]{1,0:T(8,128)(2,1)S(1)} %act.5.refs_0_.refs_1_, bf16[88,512]{1,0:T(8,128)(2,1)S(1)} %collective-permute-done.23.refs_2_, bf16[88,512]{1,0:T(8,128)(2,1)S(1)} %collective-permute-done.24.refs_3_, ...), custom_call_target="tpu_custom_call" | custom-call | flops 553648128 | tf_op jit(solution)/shard_map/down/pallas_call | solution.py:21
  76.0 4.3 %collective-permute-done.22.refs_4_ = bf16[88,1536]{1,0:T(8,128)(2,1)S(1)} collective-permute-done((bf16[88,1536]{1,0:T(8,128)(2,1)S(1)}, bf16[88,1536]{1,0:T(8,128)(2,1)S(1)}, u32[]{:S(2)}, u32[]{:S(2)}) %collective-permute-start.22) | collective-permute-done | bytes 270368 | tf_op jit(solution)/shard_map/ppermute | solution.py:173
  80.3 5.9 %collective-permute-done.26.refs_5_ = bf16[88,1536]{1,0:T(8,128)(2,1)S(1)} collective-permute-done((bf16[88,1536]{1,0:T(8,128)(2,1)S(1)}, bf16[88,1536]{1,0:T(8,128)(2,1)S(1)}, u32[]{:S(2)}, u32[]{:S(2)}) %collective-permute-start.26) | collective-permute-done | bytes 270368 | tf_op jit(solution)/shard_map/ppermute | solution.py:173
  86.2 1.8 %combine.1 = bf16[288,1536]{1,0:T(8,128)(2,1)} custom-call(bf16[288,88]{1,0:T(8,128)(2,1)S(1)} %get-tuple-element.21.refs_0_, bf16[288,88]{1,0:T(8,128)(2,1)S(1)} %get-tuple-element.22.refs_1_, bf16[88,1536]{1,0:T(8,128)(2,1)S(1)} %collective-permute-done.15.refs_2_, bf16[88,1536]{1,0:T(8,128)(2,1)S(1)} %get-tuple-element.35.refs_0_.refs_3_, ...), custom_call_target="tpu_custom_call" | custom-call | tf_op jit(solution)/shard_map/combine/pallas_call | solution.py:21
  (46 shorter events, 9.5 us)
Async XLA Ops:
  0.0 13.1 %collective-permute-start.1 = (bf16[1536,1024]{1,0:T(8,128)(2,1)}, bf16[1536,1024]{1,0:T(8,128)(2,1)S(1)}, u32[]{:S(2)}, u32[]{:S(2)}) collective-permute-start(bf16[1536,1024]{1,0:T(8,128)(2,1)} %bitcast.9), channel_id=1, source_target_pairs={{0,1},{1,0},{2,3},{3,2},{4,5},{5,4},{6,7},{7,6},{8,9},{9,8},{10,11... | collective-permute-start | bytes 9437192 | tf_op jit(solution)/shard_map/ppermute | solution.py:173
  0.5 12.6 %collective-permute-start.2 = (bf16[1536,1024]{1,0:T(8,128)(2,1)}, bf16[1536,1024]{1,0:T(8,128)(2,1)S(1)}, u32[]{:S(2)}, u32[]{:S(2)}) collective-permute-start(bf16[1536,1024]{1,0:T(8,128)(2,1)} %bitcast.13), channel_id=1, source_target_pairs={{0,1},{1,0},{2,3},{3,2},{4,5},{5,4},{6,7},{7,6},{8,9},{9,8},{10,11... | collective-permute-start | bytes 9437192 | tf_op jit(solution)/shard_map/ppermute | solution.py:173
  0.5 22.4 %collective-permute-start.3 = (bf16[1024,1536]{1,0:T(8,128)(2,1)}, bf16[1024,1536]{1,0:T(8,128)(2,1)S(1)}, u32[]{:S(2)}, u32[]{:S(2)}) collective-permute-start(bf16[1024,1536]{1,0:T(8,128)(2,1)} %bitcast.5), channel_id=1, source_target_pairs={{0,1},{1,0},{2,3},{3,2},{4,5},{5,4},{6,7},{7,6},{8,9},{9,8},{10,11... | collective-permute-start | bytes 9437192 | tf_op jit(solution)/shard_map/ppermute | solution.py:173
  1.6 1.2 %copy-start.5 = (bf16[288,1536]{1,0:T(8,128)(2,1)S(1)}, bf16[288,1536]{1,0:T(8,128)(2,1)}, u32[]{:S(2)}) copy-start(bf16[288,1536]{1,0:T(8,128)(2,1)} %refs_1_.1) | copy-start | bytes 2654212
  2.8 5.6 %copy-start.4 = (f32[288,2]{0,1:T(2,128)S(1)}, f32[288,2]{0,1:T(2,128)}, u32[]{:S(2)}) copy-start(f32[288,2]{0,1:T(2,128)} %param.8) | copy-start | bytes 6916
  2.8 10.3 %copy-start.1 = (bf16[1,1536,1024]{2,1,0:T(8,128)(2,1)S(1)}, bf16[1,1536,1024]{2,1,0:T(8,128)(2,1)}, u32[]{:S(2)}) copy-start(bf16[1,1536,1024]{2,1,0:T(8,128)(2,1)} %param.9) | copy-start | bytes 9437188
  2.8 10.3 %copy-start.2 = (bf16[1,1536,1024]{2,1,0:T(8,128)(2,1)S(1)}, bf16[1,1536,1024]{2,1,0:T(8,128)(2,1)}, u32[]{:S(2)}) copy-start(bf16[1,1536,1024]{2,1,0:T(8,128)(2,1)} %param.10) | copy-start | bytes 9437188
  3.3 9.8 %collective-permute-start = (bf16[88,1536]{1,0:T(8,128)(2,1)S(1)}, bf16[88,1536]{1,0:T(8,128)(2,1)S(1)}, u32[]{:S(2)}, u32[]{:S(2)}) collective-permute-start(bf16[88,1536]{1,0:T(8,128)(2,1)S(1)} %pick.1.refs_0_.refs_1_), channel_id=1, source_target_pairs={{0,2},{1,3},{2,0},{3,1},{4,6},{5,7},{6,4},{7,5},{8,10},{9,11},{10,... | collective-permute-start | bytes 811016 | tf_op jit(solution)/shard_map/ppermute | solution.py:173
  5.9 15.3 %collective-permute-start.4 = (bf16[88,1536]{1,0:T(8,128)(2,1)S(1)}, bf16[88,1536]{1,0:T(8,128)(2,1)S(1)}, u32[]{:S(2)}, u32[]{:S(2)}) collective-permute-start(bf16[88,1536]{1,0:T(8,128)(2,1)S(1)} %pick.1.refs_0_.refs_1_), channel_id=1, source_target_pairs={{0,6},{1,7},{2,4},{3,5},{4,2},{5,3},{6,0},{7,1},{8,14},{9,15},{10,... | collective-permute-start | bytes 811016 | tf_op jit(solution)/shard_map/ppermute | solution.py:173
  15.6 11.3 %collective-permute-start.5 = (bf16[176,1024]{1,0:T(8,128)(2,1)S(1)}, bf16[176,1024]{1,0:T(8,128)(2,1)S(1)}, u32[]{:S(2)}, u32[]{:S(2)}) collective-permute-start(bf16[176,1024]{1,0:T(8,128)(2,1)S(1)} %get-tuple-element.25), channel_id=1, source_target_pairs={{0,8},{8,0},{16,24},{24,16},{1,9},{9,1},{17,25},{25,17},{2,10},{10... | collective-permute-start | bytes 1081352 | tf_op jit(solution)/shard_map/ppermute | solution.py:173
  17.3 17.6 %collective-permute-start.6 = (bf16[176,1024]{1,0:T(8,128)(2,1)S(1)}, bf16[176,1024]{1,0:T(8,128)(2,1)S(1)}, u32[]{:S(2)}, u32[]{:S(2)}) collective-permute-start(bf16[176,1024]{1,0:T(8,128)(2,1)S(1)} %get-tuple-element.26), channel_id=1, source_target_pairs={{0,16},{8,24},{16,0},{24,8},{1,17},{9,25},{17,1},{25,9},{2,18},{10... | collective-permute-start | bytes 1081352 | tf_op jit(solution)/shard_map/ppermute | solution.py:173
  18.9 17.0 %collective-permute-start.7 = (bf16[176,1024]{1,0:T(8,128)(2,1)S(1)}, bf16[176,1024]{1,0:T(8,128)(2,1)S(1)}, u32[]{:S(2)}, u32[]{:S(2)}) collective-permute-start(bf16[176,1024]{1,0:T(8,128)(2,1)S(1)} %get-tuple-element.27), channel_id=1, source_target_pairs={{0,24},{8,16},{16,8},{24,0},{1,25},{9,17},{17,9},{25,1},{2,26},{10... | collective-permute-start | bytes 1081352 | tf_op jit(solution)/shard_map/ppermute | solution.py:173
  21.2 15.0 %collective-permute-start.8 = (bf16[88,1536]{1,0:T(8,128)(2,1)S(1)}, bf16[88,1536]{1,0:T(8,128)(2,1)S(1)}, u32[]{:S(2)}, u32[]{:S(2)}) collective-permute-start(bf16[88,1536]{1,0:T(8,128)(2,1)S(1)} %pick.1.refs_0_.refs_1_), channel_id=1, source_target_pairs={{0,4},{1,5},{2,6},{3,7},{4,0},{5,1},{6,2},{7,3},{8,12},{9,13},{10,... | collective-permute-start | bytes 811016 | tf_op jit(solution)/shard_map/ppermute | solution.py:173
  25.2 16.2 %collective-permute-start.9 = (bf16[88,1024]{1,0:T(8,128)(2,1)S(1)}, bf16[88,1024]{1,0:T(8,128)(2,1)S(1)}, u32[]{:S(2)}, u32[]{:S(2)}) collective-permute-start(bf16[88,1024]{1,0:T(8,128)(2,1)S(1)} %get-tuple-element.29), channel_id=1, source_target_pairs={{0,8},{8,0},{16,24},{24,16},{1,9},{9,1},{17,25},{25,17},{2,10},{10... | collective-permute-start | bytes 540680 | tf_op jit(solution)/shard_map/ppermute | solution.py:173
  27.0 14.4 %collective-permute-start.10 = (bf16[88,1024]{1,0:T(8,128)(2,1)S(1)}, bf16[88,1024]{1,0:T(8,128)(2,1)S(1)}, u32[]{:S(2)}, u32[]{:S(2)}) collective-permute-start(bf16[88,1024]{1,0:T(8,128)(2,1)S(1)} %get-tuple-element.30), channel_id=1, source_target_pairs={{0,16},{8,24},{16,0},{24,8},{1,17},{9,25},{17,1},{25,9},{2,18},{10... | collective-permute-start | bytes 540680 | tf_op jit(solution)/shard_map/ppermute | solution.py:173
  34.9 8.8 %collective-permute-start.11 = (bf16[88,1024]{1,0:T(8,128)(2,1)S(1)}, bf16[88,1024]{1,0:T(8,128)(2,1)S(1)}, u32[]{:S(2)}, u32[]{:S(2)}) collective-permute-start(bf16[88,1024]{1,0:T(8,128)(2,1)S(1)} %get-tuple-element.31), channel_id=1, source_target_pairs={{0,24},{8,16},{16,8},{24,0},{1,25},{9,17},{17,9},{25,1},{2,26},{10... | collective-permute-start | bytes 540680 | tf_op jit(solution)/shard_map/ppermute | solution.py:173
  36.1 22.9 %copy-start = (bf16[1,1024,1536]{2,1,0:T(8,128)(2,1)S(1)}, bf16[1,1024,1536]{2,1,0:T(8,128)(2,1)}, u32[]{:S(2)}) copy-start(bf16[1,1024,1536]{2,1,0:T(8,128)(2,1)} %param.11) | copy-start | bytes 9437188
  38.4 19.2 %collective-permute-start.16 = (bf16[88,1024]{1,0:T(8,128)(2,1)S(1)}, bf16[88,1024]{1,0:T(8,128)(2,1)S(1)}, u32[]{:S(2)}, u32[]{:S(2)}) collective-permute-start(bf16[88,1024]{1,0:T(8,128)(2,1)S(1)} %get-tuple-element.32), channel_id=1, source_target_pairs={{0,8},{8,0},{16,24},{24,16},{1,9},{9,1},{17,25},{25,17},{2,10},{10... | collective-permute-start | bytes 540680 | tf_op jit(solution)/shard_map/ppermute | solution.py:173
  43.8 5.6 %collective-permute-start.14 = (bf16[88,512]{1,0:T(8,128)(2,1)S(1)}, bf16[88,512]{1,0:T(8,128)(2,1)S(1)}, u32[]{:S(2)}, u32[]{:S(2)}) collective-permute-start(bf16[88,512]{1,0:T(8,128)(2,1)S(1)} %act.4.refs_0_.refs_1_), channel_id=1, source_target_pairs={{0,24},{8,16},{16,8},{24,0},{1,25},{9,17},{17,9},{25,1},{2,26},{10... | collective-permute-start | bytes 270344 | tf_op jit(solution)/shard_map/ppermute | solution.py:173
  45.3 9.3 %collective-permute-start.13 = (bf16[88,512]{1,0:T(8,128)(2,1)S(1)}, bf16[88,512]{1,0:T(8,128)(2,1)S(1)}, u32[]{:S(2)}, u32[]{:S(2)}) collective-permute-start(bf16[88,512]{1,0:T(8,128)(2,1)S(1)} %act.4.refs_0_.refs_1_), channel_id=1, source_target_pairs={{0,16},{8,24},{16,0},{24,8},{1,17},{9,25},{17,1},{25,9},{2,18},{10... | collective-permute-start | bytes 270344 | tf_op jit(solution)/shard_map/ppermute | solution.py:173
  46.8 7.8 %collective-permute-start.12 = (bf16[88,512]{1,0:T(8,128)(2,1)S(1)}, bf16[88,512]{1,0:T(8,128)(2,1)S(1)}, u32[]{:S(2)}, u32[]{:S(2)}) collective-permute-start(bf16[88,512]{1,0:T(8,128)(2,1)S(1)} %act.4.refs_0_.refs_1_), channel_id=1, source_target_pairs={{0,8},{8,0},{16,24},{24,16},{1,9},{9,1},{17,25},{25,17},{2,10},{10... | collective-permute-start | bytes 270344 | tf_op jit(solution)/shard_map/ppermute | solution.py:173
  47.3 16.1 %collective-permute-start.17 = (bf16[88,1024]{1,0:T(8,128)(2,1)S(1)}, bf16[88,1024]{1,0:T(8,128)(2,1)S(1)}, u32[]{:S(2)}, u32[]{:S(2)}) collective-permute-start(bf16[88,1024]{1,0:T(8,128)(2,1)S(1)} %get-tuple-element.33), channel_id=1, source_target_pairs={{0,16},{8,24},{16,0},{24,8},{1,17},{9,25},{17,1},{25,9},{2,18},{10... | collective-permute-start | bytes 540680 | tf_op jit(solution)/shard_map/ppermute | solution.py:173
  49.4 17.8 %collective-permute-start.18 = (bf16[88,1024]{1,0:T(8,128)(2,1)S(1)}, bf16[88,1024]{1,0:T(8,128)(2,1)S(1)}, u32[]{:S(2)}, u32[]{:S(2)}) collective-permute-start(bf16[88,1024]{1,0:T(8,128)(2,1)S(1)} %get-tuple-element.34), channel_id=1, source_target_pairs={{0,24},{8,16},{16,8},{24,0},{1,25},{9,17},{17,9},{25,1},{2,26},{10... | collective-permute-start | bytes 540680 | tf_op jit(solution)/shard_map/ppermute | solution.py:173
  54.6 13.2 %collective-permute-start.21 = (bf16[176,512]{1,0:T(8,128)(2,1)S(1)}, bf16[176,512]{1,0:T(8,128)(2,1)S(1)}, u32[]{:S(2)}, u32[]{:S(2)}) collective-permute-start(bf16[176,512]{1,0:T(8,128)(2,1)S(1)} %act.3.refs_0_.refs_1_), channel_id=1, source_target_pairs={{0,24},{8,16},{16,8},{24,0},{1,25},{9,17},{17,9},{25,1},{2,26},{10... | collective-permute-start | bytes 540680 | tf_op jit(solution)/shard_map/ppermute | solution.py:173
  54.6 15.7 %collective-permute-start.20 = (bf16[176,512]{1,0:T(8,128)(2,1)S(1)}, bf16[176,512]{1,0:T(8,128)(2,1)S(1)}, u32[]{:S(2)}, u32[]{:S(2)}) collective-permute-start(bf16[176,512]{1,0:T(8,128)(2,1)S(1)} %act.3.refs_0_.refs_1_), channel_id=1, source_target_pairs={{0,16},{8,24},{16,0},{24,8},{1,17},{9,25},{17,1},{25,9},{2,18},{10... | collective-permute-start | bytes 540680 | tf_op jit(solution)/shard_map/ppermute | solution.py:173
  57.5 13.3 %collective-permute-start.19 = (bf16[176,512]{1,0:T(8,128)(2,1)S(1)}, bf16[176,512]{1,0:T(8,128)(2,1)S(1)}, u32[]{:S(2)}, u32[]{:S(2)}) collective-permute-start(bf16[176,512]{1,0:T(8,128)(2,1)S(1)} %act.3.refs_0_.refs_1_), channel_id=1, source_target_pairs={{0,8},{8,0},{16,24},{24,16},{1,9},{9,1},{17,25},{25,17},{2,10},{10... | collective-permute-start | bytes 540680 | tf_op jit(solution)/shard_map/ppermute | solution.py:173
  63.5 12.6 %collective-permute-start.15 = (bf16[88,1536]{1,0:T(8,128)(2,1)S(1)}, bf16[88,1536]{1,0:T(8,128)(2,1)S(1)}, u32[]{:S(2)}, u32[]{:S(2)}) collective-permute-start(bf16[88,1536]{1,0:T(8,128)(2,1)S(1)} %down.3.refs_0_), channel_id=1, source_target_pairs={{0,6},{1,7},{2,4},{3,5},{4,2},{5,3},{6,0},{7,1},{8,14},{9,15},{10,... | collective-permute-start | bytes 811016 | tf_op jit(solution)/shard_map/ppermute | solution.py:173
  67.3 5.6 %collective-permute-start.25 = (bf16[88,512]{1,0:T(8,128)(2,1)S(1)}, bf16[88,512]{1,0:T(8,128)(2,1)S(1)}, u32[]{:S(2)}, u32[]{:S(2)}) collective-permute-start(bf16[88,512]{1,0:T(8,128)(2,1)S(1)} %act.5.refs_0_.refs_1_), channel_id=1, source_target_pairs={{0,24},{8,16},{16,8},{24,0},{1,25},{9,17},{17,9},{25,1},{2,26},{10... | collective-permute-start | bytes 270344 | tf_op jit(solution)/shard_map/ppermute | solution.py:173
  67.8 6.0 %collective-permute-start.24 = (bf16[88,512]{1,0:T(8,128)(2,1)S(1)}, bf16[88,512]{1,0:T(8,128)(2,1)S(1)}, u32[]{:S(2)}, u32[]{:S(2)}) collective-permute-start(bf16[88,512]{1,0:T(8,128)(2,1)S(1)} %act.5.refs_0_.refs_1_), channel_id=1, source_target_pairs={{0,16},{8,24},{16,0},{24,8},{1,17},{9,25},{17,1},{25,9},{2,18},{10... | collective-permute-start | bytes 270344 | tf_op jit(solution)/shard_map/ppermute | solution.py:173
  70.3 4.5 %collective-permute-start.23 = (bf16[88,512]{1,0:T(8,128)(2,1)S(1)}, bf16[88,512]{1,0:T(8,128)(2,1)S(1)}, u32[]{:S(2)}, u32[]{:S(2)}) collective-permute-start(bf16[88,512]{1,0:T(8,128)(2,1)S(1)} %act.5.refs_0_.refs_1_), channel_id=1, source_target_pairs={{0,8},{8,0},{16,24},{24,16},{1,9},{9,1},{17,25},{25,17},{2,10},{10... | collective-permute-start | bytes 270344 | tf_op jit(solution)/shard_map/ppermute | solution.py:173
  72.2 8.2 %collective-permute-start.22 = (bf16[88,1536]{1,0:T(8,128)(2,1)S(1)}, bf16[88,1536]{1,0:T(8,128)(2,1)S(1)}, u32[]{:S(2)}, u32[]{:S(2)}) collective-permute-start(bf16[88,1536]{1,0:T(8,128)(2,1)S(1)} %get-tuple-element.36), channel_id=1, source_target_pairs={{0,2},{1,3},{2,0},{3,1},{4,6},{5,7},{6,4},{7,5},{8,10},{9,11},{10,... | collective-permute-start | bytes 811016 | tf_op jit(solution)/shard_map/ppermute | solution.py:173
  75.9 10.3 %collective-permute-start.26 = (bf16[88,1536]{1,0:T(8,128)(2,1)S(1)}, bf16[88,1536]{1,0:T(8,128)(2,1)S(1)}, u32[]{:S(2)}, u32[]{:S(2)}) collective-permute-start(bf16[88,1536]{1,0:T(8,128)(2,1)S(1)} %down.5), channel_id=1, source_target_pairs={{0,4},{1,5},{2,6},{3,7},{4,0},{5,1},{6,2},{7,3},{8,12},{9,13},{10,... | collective-permute-start | bytes 811016 | tf_op jit(solution)/shard_map/ppermute | solution.py:173
  (1 other events, 0.7 us)

commit v3 on v2

--- a/solution.py
+++ b/solution.py
@@ -14,7 +14,7 @@
 ZORDER = (1, 3, 2)
 
 
-def call(kernel, name, outs, args, after=(), flops=0):
+def call(kernel, name, outs, args, after=(), flops=0, scratch=()):
     def body(*refs):
         kernel(*refs[len(after) :])
 
@@ -24,6 +24,7 @@
         in_specs=[pl.BlockSpec(memory_space=pl.ANY)] * len(after)
         + [pl.BlockSpec(memory_space=pltpu.VMEM)] * len(args),
         out_specs=[pl.BlockSpec(memory_space=pltpu.VMEM)] * len(outs),
+        scratch_shapes=list(scratch),
         compiler_params=pltpu.CompilerParams(vmem_limit_bytes=LIMIT),
         cost_estimate=pl.CostEstimate(flops=flops, bytes_accessed=0, transcendentals=0),
         name=name,
@@ -168,15 +169,200 @@
     return call(combine_kernel, "combine", outs, [*backs, *terms])[0]
 
 
+def lead_of(count):
+    lead = count // 16 * 16
+    return lead, count - lead
+
+
+def packed_rows(blocks, columns):
+    return blocks * CAP * columns // 128
+
+
+def to_rows(value):
+    return [value[:, 128 * j : 128 * (j + 1)] for j in range(value.shape[1] // 128)]
+
+
+def pack(out_ref, value, blocks, first=0, of=None):
+    lead, rest = lead_of(CAP)
+    of = blocks if of is None else of
+    wide = value.shape[1] // 128
+    for n in range(blocks):
+        for j in range(wide):
+            out_ref[(n * wide + j) * lead : (n * wide + j + 1) * lead, :] = value[
+                (first + n) * lead : (first + n + 1) * lead, 128 * j : 128 * (j + 1)
+            ].astype(out_ref.dtype)
+    others = []
+    for n in range(blocks):
+        for i in range(rest):
+            row = of * lead + (first + n) * rest + i
+            others += to_rows(value[row : row + 1])
+    if others:
+        start = blocks * wide * lead
+        out_ref[start : start + len(others), :] = jnp.concatenate(others, axis=0).astype(out_ref.dtype)
+
+
+def unpack(refs, held, at=0):
+    lead, rest = lead_of(CAP)
+    blocks = sum(n for _, n in refs)
+    others, done = [], 0
+    for ref, count in refs:
+        wide = ref.shape[0] // (count * CAP)
+        for n in range(count):
+            for j in range(wide):
+                held[
+                    (done + n) * lead : (done + n + 1) * lead, at + 128 * j : at + 128 * (j + 1)
+                ] = ref[(n * wide + j) * lead : (n * wide + j + 1) * lead, :]
+        if rest:
+            last = ref[count * wide * lead : count * wide * (lead + rest), :].astype(jnp.float32)
+            for n in range(count * rest):
+                rows = [last[n * wide + j : n * wide + j + 1] for j in range(wide)]
+                others.append(jnp.concatenate(rows, axis=1))
+        done += count
+    room = held.shape[0] - blocks * lead
+    if room:
+        width = 128 * wide
+        others.append(jnp.zeros((room - len(others), width), jnp.float32))
+        held[blocks * lead :, at : at + width] = jnp.concatenate(others, axis=0).astype(held.dtype)
+
+
+def room_for(blocks):
+    lead, rest = lead_of(CAP)
+    return blocks * lead + -(-blocks * rest // 16) * 16
+
+
+def pick_packed_kernel(ids_ref, tokens_ref, out_ref):
+    hits = slot_hits(ids_ref[...], -(-CAP // 8) * 8).astype(jnp.bfloat16)
+    pack(out_ref, jnp.dot(hits, tokens_ref[...], preferred_element_type=jnp.float32), 1)
+
+
+def pick_packed(ids, tokens):
+    outs = [jax.ShapeDtypeStruct((packed_rows(1, tokens.shape[1]), 128), tokens.dtype)]
+    return call(pick_packed_kernel, "pick", outs, [ids, tokens], flops=30000000000)[0]
+
+
+def project_packed_kernel(parts, n_x, *refs):
+    xs, weights, outs, held = refs[:n_x], refs[n_x:-parts - 1], refs[-parts - 1 : -1], refs[-1]
+    me = lax.axis_index("fsdp")
+    unpack([(x, 1) for x in xs], held)
+    x = held[...]
+    quarter = weights[0].shape[1] // parts
+    for k in [*range(parts - 1, 0, -1), 0]:
+        cols = pl.ds(pl.multiple_of((me ^ k) * quarter, quarter), quarter)
+        value = [jnp.dot(x, w[:, cols], preferred_element_type=jnp.float32) for w in weights]
+        pack(outs[k], jnp.concatenate(value, axis=1), n_x)
+
+
+def project_packed(xs, weights, parts, after):
+    depth, width = weights[0].shape
+    quarter = width // parts
+    rows = room_for(len(xs))
+    kinds = [jnp.float32] + [jnp.bfloat16] * (parts - 1)
+    size = (packed_rows(len(xs), len(weights) * quarter), 128)
+    outs = [jax.ShapeDtypeStruct(size, kind) for kind in kinds]
+    kernel = functools.partial(project_packed_kernel, parts, len(xs))
+    flops = 2 * rows * depth * len(weights) * width
+    scratch = [pltpu.VMEM((rows, depth), xs[0].dtype)]
+    return call(kernel, "project", outs, [*xs, *weights], after, flops, scratch)
+
+
+def act_packed_kernel(blocks, *refs):
+    parts, out_ref = refs[:-1], refs[-1]
+    total = parts[0][...]
+    for part in parts[1:]:
+        total += part[...].astype(jnp.float32)
+    lead, rest = lead_of(CAP)
+    wide = total.shape[0] // (blocks * CAP)
+    half = wide // 2
+
+    def act(start, rows):
+        gate, up = total[start : start + rows], total[start + rows : start + 2 * rows]
+        return gate / (1.0 + jnp.exp(-gate)) * up
+
+    for n in range(blocks):
+        out_ref[n * half * lead : (n + 1) * half * lead, :] = act(
+            n * wide * lead, half * lead
+        ).astype(out_ref.dtype)
+    others = [act(blocks * wide * lead + n * wide, half) for n in range(blocks * rest)]
+    if others:
+        out_ref[blocks * half * lead :, :] = jnp.concatenate(others, axis=0).astype(out_ref.dtype)
+
+
+def activate_packed(parts, blocks, after):
+    outs = [jax.ShapeDtypeStruct((parts[0].shape[0] // 2, 128), jnp.bfloat16)]
+    return call(functools.partial(act_packed_kernel, blocks), "act", outs, parts, after)[0]
+
+
+def down_packed_kernel(parts, blocks, *refs):
+    acts, weights, outs, held = refs[:parts], refs[parts : parts + 2], refs[parts + 2 : -1], refs[-1]
+    me = lax.axis_index("fsdp")
+    quarter = weights[0].shape[0] // parts
+    total = None
+    for k, act in enumerate(acts):
+        at = k * 2 * quarter
+        unpack([(act, blocks)], held, at)
+        depth = pl.ds(pl.multiple_of((me ^ k) * quarter, quarter), quarter)
+        for j, w in enumerate(weights):
+            term = jnp.dot(
+                held[:, at + j * quarter : at + (j + 1) * quarter],
+                w[depth, :],
+                preferred_element_type=jnp.float32,
+            )
+            total = term if total is None else total + term
+    for n, out in enumerate(outs):
+        pack(out, total, 1, n, blocks)
+
+
+def down_packed(acts, weights, blocks, after):
+    depth, width = weights[0].shape
+    rows = room_for(blocks)
+    outs = [jax.ShapeDtypeStruct((packed_rows(1, width), 128), jnp.bfloat16)] * blocks
+    kernel = functools.partial(down_packed_kernel, len(acts), blocks)
+    flops = 4 * rows * depth * width
+    scratch = [pltpu.VMEM((rows, 2 * depth), acts[0].dtype)]
+    return call(kernel, "down", outs, [*acts, *weights], after, flops, scratch)
+
+
+def combine_packed_kernel(back_high, back_low, *refs):
+    terms, out_ref, held = refs[:-2], refs[-2], refs[-1]
+    lead, rest = lead_of(CAP)
+    total = terms[0][...].astype(jnp.float32)
+    for term in terms[1:]:
+        total += term[...].astype(jnp.float32)
+    wide = total.shape[0] // CAP
+    others = [jnp.zeros((held.shape[0] - CAP, 128 * wide), jnp.float32)]
+    for n in range(rest):
+        start = wide * lead + n * wide
+        rows = [total[start + j : start + j + 1] for j in range(wide)]
+        others.insert(n, jnp.concatenate(rows, axis=1))
+    for j in range(wide):
+        held[:lead, 128 * j : 128 * (j + 1)] = total[j * lead : (j + 1) * lead]
+    held[lead:, :] = jnp.concatenate(others, axis=0)
+    high, low = split(held[...])
+    total = jnp.dot(back_low[...], high, preferred_element_type=jnp.float32)
+    total += jnp.dot(back_high[...], low, preferred_element_type=jnp.float32)
+    total += jnp.dot(back_high[...], high, preferred_element_type=jnp.float32)
+    out_ref[...] = total.astype(out_ref.dtype)
+
+
+def combine_packed(backs, terms):
+    tokens, slots = backs[0].shape
+    width = terms[0].shape[0] // CAP * 128
+    outs = [jax.ShapeDtypeStruct((tokens, width), jnp.bfloat16)]
+    scratch = [pltpu.VMEM((slots, width), jnp.float32)]
+    return call(combine_packed_kernel, "combine", outs, [*backs, *terms], scratch=scratch)[0]
+
+
 def local(n_fsdp, n_ed, groups, zorder, seq, tokens, expert_ids, route_weights, w_gate, w_up, w_down):
     slots = -(-CAP // 8) * 8
     swap = lambda v, axis, size, k: lax.ppermute(v, axis, [(i, i ^ k) for i in range(size)])
     partner = lambda v: swap(v, "ed", n_ed, 1)
     along = lambda v, s: swap(v, "ed", n_ed, 2 * s)
     across = lambda v, k: swap(v, "fsdp", n_fsdp, k)
+    packed = w_gate.shape[2] % (128 * n_fsdp) == 0 and tokens.shape[1] % 128 == 0
+
     own = [w_gate[0], w_up[0], w_down[0]]
     other = [partner(w) for w in own]
-    mine = pick(expert_ids.T, tokens, slots)
+    mine = pick_packed(expert_ids.T, tokens) if packed else pick(expert_ids.T, tokens, slots)
     backs = back(expert_ids.T, route_weights.T, slots, (mine,))
     blocks = {0: mine}
     for s in zorder:
@@ -189,18 +375,19 @@
         if op == "P":
             xs = [blocks[s] for s in group]
             weights = [own[0], other[0], own[1], other[1]]
-            out = project(xs, weights, n_fsdp, (*last, other[2]) if g == WAIT else last)
+            deps = (*last, other[2]) if g == WAIT else last
+            out = (project_packed if packed else project)(xs, weights, n_fsdp, deps)
             parts[g] = [out[0]] + [across(out[k], k) for k in range(n_fsdp - 1, 0, -1)][::-1]
             last = (out[0],)
         elif op == "A":
-            act = activate(parts[g], last)
+            act = activate_packed(parts[g], len(group), last) if packed else activate(parts[g], last)
             acts[g] = [act] + [across(act, k) for k in range(n_fsdp - 1, 0, -1)][::-1]
             last = (act,)
         else:
-            outs = down(acts[g], [own[2], other[2]], len(group), last)
+            outs = (down_packed if packed else down)(acts[g], [own[2], other[2]], len(group), last)
             last = (outs[0],)
             terms += [out if s == 0 else along(out, s) for s, out in zip(group, outs)]
-    return combine(backs, terms)
+    return (combine_packed if packed else combine)(backs, terms)
 
 
 def plan(n_ed):

time: 88.2 us -> 83.7 us (0.949)
  waiting for transfers between devices: 35.9 us -> 28.8 us
  starting transfers between devices: 36.6 us -> 39 us
    ppermute x27, waiting for transfers between devices: 35.9 us -> 28.8 us  [local(): lax.ppermute(v, axis, [(i, i ^ k) for i in range(size)])]
    ppermute x27, starting transfers between devices: 36.6 us -> 39 us  [local(): lax.ppermute(v, axis, [(i, i ^ k) for i in range(size)])]
  transfers between devices with their start and end apart: 27 -> 27, of which waited for: 14 -> 12; matrix products, arithmetic and copies ran while one was open for 0% -> 0% of each run, Pallas kernels for 13% -> 14%
where the time goes in v3:
time: 83.7 us; the launch traced here: 83.5 us
  starting transfers between devices  39 us (47%)
  waiting for transfers between devices  28.8 us (34%)
  Pallas kernels  13.8 us (16%)
  local copies, waits for them, and re-layouts  1.87 us (2%)
    ppermute x27, starting transfers between devices, local(): lax.ppermute(v, axis, [(i, i ^ k) for i in range(size)])  39 us
    ppermute x27, waiting for transfers between devices, local(): lax.ppermute(v, axis, [(i, i ^ k) for i in range(size)])  28.8 us
    pallas_call x12, Pallas kernels, call(): pl.pallas_call(body, out_shape=outs, in_specs=[pl.BlockSpec(memory_space=...  13.8 us
    unnamed x12, local copies, waits for them, and re-layouts  1.87 us
  transfers between devices with their start and end apart: 27, of which 12 were waited for; matrix products, arithmetic and copies ran while one was open for 0% of the time, Pallas kernels for 14%

profile of v3, /device:TPU:0, one launch (start us, length us, event | category | flops | bytes accessed | tf_op | source)
XLA Modules:
  0.0 83.5 jit_solution(3539741552179876369)
XLA Ops:
  1.7 1.2 %copy-done.5 = bf16[288,1536]{1,0:T(8,128)(2,1)S(1)} copy-done((bf16[288,1536]{1,0:T(8,128)(2,1)S(1)}, bf16[288,1536]{1,0:T(8,128)(2,1)}, u32[]{:S(2)}) %copy-start.5) | copy-done | bytes 884760
  3.3 2.6 %collective-permute-start = (bf16[972,128]{1,0:T(8,128)(2,1)S(1)}, bf16[972,128]{1,0:T(8,128)(2,1)S(1)}, u32[]{:S(2)}, u32[]{:S(2)}) collective-permute-start(bf16[972,128]{1,0:T(8,128)(2,1)S(1)} %pick.1.refs_0_.refs_1_), channel_id=1, source_target_pairs={{0,2},{1,3},{2,0},{3,1},{4,6},{5,7},{6,4},{7,5},{8,10},{9,11},{10,... | collective-permute-start | bytes 746504 | tf_op jit(solution)/shard_map/ppermute | solution.py:357
  5.9 2.5 %collective-permute-start.4 = (bf16[972,128]{1,0:T(8,128)(2,1)S(1)}, bf16[972,128]{1,0:T(8,128)(2,1)S(1)}, u32[]{:S(2)}, u32[]{:S(2)}) collective-permute-start(bf16[972,128]{1,0:T(8,128)(2,1)S(1)} %pick.1.refs_0_.refs_1_), channel_id=1, source_target_pairs={{0,6},{1,7},{2,4},{3,5},{4,2},{5,3},{6,0},{7,1},{8,14},{9,15},{10,... | collective-permute-start | bytes 746504 | tf_op jit(solution)/shard_map/ppermute | solution.py:357
  8.7 4.0 %collective-permute-done.refs_2_ = bf16[972,128]{1,0:T(8,128)(2,1)S(1)} collective-permute-done((bf16[972,128]{1,0:T(8,128)(2,1)S(1)}, bf16[972,128]{1,0:T(8,128)(2,1)S(1)}, u32[]{:S(2)}, u32[]{:S(2)}) %collective-permute-start) | collective-permute-done | bytes 248864 | tf_op jit(solution)/shard_map/ppermute | solution.py:357
  12.7 2.6 %project.3 = (f32[1296,128]{1,0:T(8,128)S(1)}, bf16[1296,128]{1,0:T(8,128)(2,1)S(1)}, bf16[1296,128]{1,0:T(8,128)(2,1)S(1)}, bf16[1296,128]{1,0:T(8,128)(2,1)S(1)}) custom-call(bf16[288,88]{1,0:T(8,128)(2,1)S(1)} %get-tuple-element.21.refs_0_, bf16[972,128]{1,0:T(8,128)(2,1)S(1)} %pick.1.refs_0_.refs_1_, bf16[972,128]{1,0:T(8,128)(2,1)S(1)} %collective-permute-done.refs_2_, ...), custom_call_target="tpu_custom_call" | custom-call | flops 2214592512 | tf_op jit(solution)/shard_map/project/pallas_call | solution.py:21
  15.2 1.7 %collective-permute-start.5 = (bf16[1296,128]{1,0:T(8,128)(2,1)S(1)}, bf16[1296,128]{1,0:T(8,128)(2,1)S(1)}, u32[]{:S(2)}, u32[]{:S(2)}) collective-permute-start(bf16[1296,128]{1,0:T(8,128)(2,1)S(1)} %get-tuple-element.25), channel_id=1, source_target_pairs={{0,8},{8,0},{16,24},{24,16},{1,9},{9,1},{17,25},{25,17},{2,10},{10... | collective-permute-start | bytes 995336 | tf_op jit(solution)/shard_map/ppermute | solution.py:357
  16.9 1.5 %collective-permute-start.6 = (bf16[1296,128]{1,0:T(8,128)(2,1)S(1)}, bf16[1296,128]{1,0:T(8,128)(2,1)S(1)}, u32[]{:S(2)}, u32[]{:S(2)}) collective-permute-start(bf16[1296,128]{1,0:T(8,128)(2,1)S(1)} %get-tuple-element.26), channel_id=1, source_target_pairs={{0,16},{8,24},{16,0},{24,8},{1,17},{9,25},{17,1},{25,9},{2,18},{10... | collective-permute-start | bytes 995336 | tf_op jit(solution)/shard_map/ppermute | solution.py:357
  18.8 1.5 %collective-permute-done.4.refs_2_ = bf16[972,128]{1,0:T(8,128)(2,1)S(1)} collective-permute-done((bf16[972,128]{1,0:T(8,128)(2,1)S(1)}, bf16[972,128]{1,0:T(8,128)(2,1)S(1)}, u32[]{:S(2)}, u32[]{:S(2)}) %collective-permute-start.4) | collective-permute-done | bytes 248864 | tf_op jit(solution)/shard_map/ppermute | solution.py:357
  20.3 1.7 %collective-permute-start.8 = (bf16[972,128]{1,0:T(8,128)(2,1)S(1)}, bf16[972,128]{1,0:T(8,128)(2,1)S(1)}, u32[]{:S(2)}, u32[]{:S(2)}) collective-permute-start(bf16[972,128]{1,0:T(8,128)(2,1)S(1)} %pick.1.refs_0_.refs_1_), channel_id=1, source_target_pairs={{0,4},{1,5},{2,6},{3,7},{4,0},{5,1},{6,2},{7,3},{8,12},{9,13},{10,... | collective-permute-start | bytes 746504 | tf_op jit(solution)/shard_map/ppermute | solution.py:357
  22.1 2.3 %project.4 = (f32[648,128]{1,0:T(8,128)S(1)}, bf16[648,128]{1,0:T(8,128)(2,1)S(1)}, bf16[648,128]{1,0:T(8,128)(2,1)S(1)}, bf16[648,128]{1,0:T(8,128)(2,1)S(1)}) custom-call(f32[1296,128]{1,0:T(8,128)S(1)} %get-tuple-element.23.refs_0_.refs_1_, bf16[1024,1536]{1,0:T(8,128)(2,1)S(1)} %collective-permute-done.3.refs_1_.refs_6_, ...), custom_call_target="tpu_custom_call" | custom-call | flops 1207959552 | tf_op jit(solution)/shard_map/project/pallas_call | solution.py:21
  24.4 1.5 %collective-permute-start.9 = (bf16[648,128]{1,0:T(8,128)(2,1)S(1)}, bf16[648,128]{1,0:T(8,128)(2,1)S(1)}, u32[]{:S(2)}, u32[]{:S(2)}) collective-permute-start(bf16[648,128]{1,0:T(8,128)(2,1)S(1)} %get-tuple-element.29), channel_id=1, source_target_pairs={{0,8},{8,0},{16,24},{24,16},{1,9},{9,1},{17,25},{25,17},{2,10},{10... | collective-permute-start | bytes 497672 | tf_op jit(solution)/shard_map/ppermute | solution.py:357
  26.0 1.7 %collective-permute-start.10 = (bf16[648,128]{1,0:T(8,128)(2,1)S(1)}, bf16[648,128]{1,0:T(8,128)(2,1)S(1)}, u32[]{:S(2)}, u32[]{:S(2)}) collective-permute-start(bf16[648,128]{1,0:T(8,128)(2,1)S(1)} %get-tuple-element.30), channel_id=1, source_target_pairs={{0,16},{8,24},{16,0},{24,8},{1,17},{9,25},{17,1},{25,9},{2,18},{10... | collective-permute-start | bytes 497672 | tf_op jit(solution)/shard_map/ppermute | solution.py:357
  27.7 5.6 %collective-permute-done.6.refs_3_ = bf16[1296,128]{1,0:T(8,128)(2,1)S(1)} collective-permute-done((bf16[1296,128]{1,0:T(8,128)(2,1)S(1)}, bf16[1296,128]{1,0:T(8,128)(2,1)S(1)}, u32[]{:S(2)}, u32[]{:S(2)}) %collective-permute-start.6) | collective-permute-done | bytes 331808 | tf_op jit(solution)/shard_map/ppermute | solution.py:357
  34.5 2.3 %project.5 = (f32[648,128]{1,0:T(8,128)S(1)}, bf16[648,128]{1,0:T(8,128)(2,1)S(1)}, bf16[648,128]{1,0:T(8,128)(2,1)S(1)}, bf16[648,128]{1,0:T(8,128)(2,1)S(1)}) custom-call(bf16[648,128]{1,0:T(8,128)(2,1)S(1)} %act.3.refs_0_.refs_1_, bf16[972,128]{1,0:T(8,128)(2,1)S(1)} %collective-permute-done.8.refs_1_, bf16[1536,1024]{1,0:T(8,128)(2,1)S(1)} %bitcast.12, ...), custom_call_target="tpu_custom_call" | custom-call | flops 1207959552 | tf_op jit(solution)/shard_map/project/pallas_call | solution.py:21
  36.8 3.0 %collective-permute-start.16 = (bf16[648,128]{1,0:T(8,128)(2,1)S(1)}, bf16[648,128]{1,0:T(8,128)(2,1)S(1)}, u32[]{:S(2)}, u32[]{:S(2)}) collective-permute-start(bf16[648,128]{1,0:T(8,128)(2,1)S(1)} %get-tuple-element.32), channel_id=1, source_target_pairs={{0,8},{8,0},{16,24},{24,16},{1,9},{9,1},{17,25},{25,17},{2,10},{10... | collective-permute-start | bytes 497672 | tf_op jit(solution)/shard_map/ppermute | solution.py:357
  39.8 1.3 %collective-permute-done.11.refs_4_ = bf16[648,128]{1,0:T(8,128)(2,1)S(1)} collective-permute-done((bf16[648,128]{1,0:T(8,128)(2,1)S(1)}, bf16[648,128]{1,0:T(8,128)(2,1)S(1)}, u32[]{:S(2)}, u32[]{:S(2)}) %collective-permute-start.11) | collective-permute-done | bytes 165920 | tf_op jit(solution)/shard_map/ppermute | solution.py:357
  41.2 1.4 %collective-permute-start.14 = (bf16[324,128]{1,0:T(8,128)(2,1)S(1)}, bf16[324,128]{1,0:T(8,128)(2,1)S(1)}, u32[]{:S(2)}, u32[]{:S(2)}) collective-permute-start(bf16[324,128]{1,0:T(8,128)(2,1)S(1)} %act.4.refs_0_.refs_1_), channel_id=1, source_target_pairs={{0,24},{8,16},{16,8},{24,0},{1,25},{9,17},{17,9},{25,1},{2,26},{10... | collective-permute-start | bytes 248840 | tf_op jit(solution)/shard_map/ppermute | solution.py:357
  42.7 1.5 %collective-permute-start.13 = (bf16[324,128]{1,0:T(8,128)(2,1)S(1)}, bf16[324,128]{1,0:T(8,128)(2,1)S(1)}, u32[]{:S(2)}, u32[]{:S(2)}) collective-permute-start(bf16[324,128]{1,0:T(8,128)(2,1)S(1)} %act.4.refs_0_.refs_1_), channel_id=1, source_target_pairs={{0,16},{8,24},{16,0},{24,8},{1,17},{9,25},{17,1},{25,9},{2,18},{10... | collective-permute-start | bytes 248840 | tf_op jit(solution)/shard_map/ppermute | solution.py:357
  45.0 2.0 %collective-permute-start.17 = (bf16[648,128]{1,0:T(8,128)(2,1)S(1)}, bf16[648,128]{1,0:T(8,128)(2,1)S(1)}, u32[]{:S(2)}, u32[]{:S(2)}) collective-permute-start(bf16[648,128]{1,0:T(8,128)(2,1)S(1)} %get-tuple-element.33), channel_id=1, source_target_pairs={{0,16},{8,24},{16,0},{24,8},{1,17},{9,25},{17,1},{25,9},{2,18},{10... | collective-permute-start | bytes 497672 | tf_op jit(solution)/shard_map/ppermute | solution.py:357
  47.0 1.9 %collective-permute-start.18 = (bf16[648,128]{1,0:T(8,128)(2,1)S(1)}, bf16[648,128]{1,0:T(8,128)(2,1)S(1)}, u32[]{:S(2)}, u32[]{:S(2)}) collective-permute-start(bf16[648,128]{1,0:T(8,128)(2,1)S(1)} %get-tuple-element.34), channel_id=1, source_target_pairs={{0,24},{8,16},{16,8},{24,0},{1,25},{9,17},{17,9},{25,1},{2,26},{10... | collective-permute-start | bytes 497672 | tf_op jit(solution)/shard_map/ppermute | solution.py:357
  49.2 1.3 %collective-permute-start.21 = (bf16[648,128]{1,0:T(8,128)(2,1)S(1)}, bf16[648,128]{1,0:T(8,128)(2,1)S(1)}, u32[]{:S(2)}, u32[]{:S(2)}) collective-permute-start(bf16[648,128]{1,0:T(8,128)(2,1)S(1)} %act.3.refs_0_.refs_1_), channel_id=1, source_target_pairs={{0,24},{8,16},{16,8},{24,0},{1,25},{9,17},{17,9},{25,1},{2,26},{10... | collective-permute-start | bytes 497672 | tf_op jit(solution)/shard_map/ppermute | solution.py:357
  50.5 2.9 %collective-permute-start.20 = (bf16[648,128]{1,0:T(8,128)(2,1)S(1)}, bf16[648,128]{1,0:T(8,128)(2,1)S(1)}, u32[]{:S(2)}, u32[]{:S(2)}) collective-permute-start(bf16[648,128]{1,0:T(8,128)(2,1)S(1)} %act.3.refs_0_.refs_1_), channel_id=1, source_target_pairs={{0,16},{8,24},{16,0},{24,8},{1,17},{9,25},{17,1},{25,9},{2,18},{10... | collective-permute-start | bytes 497672 | tf_op jit(solution)/shard_map/ppermute | solution.py:357
  53.5 1.5 %collective-permute-start.19 = (bf16[648,128]{1,0:T(8,128)(2,1)S(1)}, bf16[648,128]{1,0:T(8,128)(2,1)S(1)}, u32[]{:S(2)}, u32[]{:S(2)}) collective-permute-start(bf16[648,128]{1,0:T(8,128)(2,1)S(1)} %act.3.refs_0_.refs_1_), channel_id=1, source_target_pairs={{0,8},{8,0},{16,24},{24,16},{1,9},{9,1},{17,25},{25,17},{2,10},{10... | collective-permute-start | bytes 497672 | tf_op jit(solution)/shard_map/ppermute | solution.py:357
  56.2 3.9 %collective-permute-done.17.refs_3_ = bf16[648,128]{1,0:T(8,128)(2,1)S(1)} collective-permute-done((bf16[648,128]{1,0:T(8,128)(2,1)S(1)}, bf16[648,128]{1,0:T(8,128)(2,1)S(1)}, u32[]{:S(2)}, u32[]{:S(2)}) %collective-permute-start.17) | collective-permute-done | bytes 165920 | tf_op jit(solution)/shard_map/ppermute | solution.py:357
  60.1 1.5 %collective-permute-start.15 = (bf16[972,128]{1,0:T(8,128)(2,1)S(1)}, bf16[972,128]{1,0:T(8,128)(2,1)S(1)}, u32[]{:S(2)}, u32[]{:S(2)}) collective-permute-start(bf16[972,128]{1,0:T(8,128)(2,1)S(1)} %down.3.refs_0_), channel_id=1, source_target_pairs={{0,6},{1,7},{2,4},{3,5},{4,2},{5,3},{6,0},{7,1},{8,14},{9,15},{10,... | collective-permute-start | bytes 746504 | tf_op jit(solution)/shard_map/ppermute | solution.py:357
  61.8 2.9 %collective-permute-start.25 = (bf16[324,128]{1,0:T(8,128)(2,1)S(1)}, bf16[324,128]{1,0:T(8,128)(2,1)S(1)}, u32[]{:S(2)}, u32[]{:S(2)}) collective-permute-start(bf16[324,128]{1,0:T(8,128)(2,1)S(1)} %act.5.refs_0_.refs_1_), channel_id=1, source_target_pairs={{0,24},{8,16},{16,8},{24,0},{1,25},{9,17},{17,9},{25,1},{2,26},{10... | collective-permute-start | bytes 248840 | tf_op jit(solution)/shard_map/ppermute | solution.py:357
  64.7 2.5 %collective-permute-start.24 = (bf16[324,128]{1,0:T(8,128)(2,1)S(1)}, bf16[324,128]{1,0:T(8,128)(2,1)S(1)}, u32[]{:S(2)}, u32[]{:S(2)}) collective-permute-start(bf16[324,128]{1,0:T(8,128)(2,1)S(1)} %act.5.refs_0_.refs_1_), channel_id=1, source_target_pairs={{0,16},{8,24},{16,0},{24,8},{1,17},{9,25},{17,1},{25,9},{2,18},{10... | collective-permute-start | bytes 248840 | tf_op jit(solution)/shard_map/ppermute | solution.py:357
  67.2 1.3 %down.4 = (bf16[972,128]{1,0:T(8,128)(2,1)S(1)}, bf16[972,128]{1,0:T(8,128)(2,1)S(1)}) custom-call(bf16[324,128]{1,0:T(8,128)(2,1)S(1)} %act.5.refs_0_.refs_1_, bf16[648,128]{1,0:T(8,128)(2,1)S(1)} %act.3.refs_0_.refs_1_, bf16[648,128]{1,0:T(8,128)(2,1)S(1)} %collective-permute-done.19.refs_2_, bf16[648,128]{1,0:T(8,128)(2,1)S(1)} %collective-permute-done.20.refs_3_, ...), custom_call_target="tpu_custom_call" | custom-call | flops 1107296256 | tf_op jit(solution)/shard_map/down/pallas_call | solution.py:21
  69.6 2.0 %collective-permute-done.23.refs_2_ = bf16[324,128]{1,0:T(8,128)(2,1)S(1)} collective-permute-done((bf16[324,128]{1,0:T(8,128)(2,1)S(1)}, bf16[324,128]{1,0:T(8,128)(2,1)S(1)}, u32[]{:S(2)}, u32[]{:S(2)}) %collective-permute-start.23) | collective-permute-done | bytes 82976 | tf_op jit(solution)/shard_map/ppermute | solution.py:357
  72.9 4.4 %collective-permute-done.22.refs_4_ = bf16[972,128]{1,0:T(8,128)(2,1)S(1)} collective-permute-done((bf16[972,128]{1,0:T(8,128)(2,1)S(1)}, bf16[972,128]{1,0:T(8,128)(2,1)S(1)}, u32[]{:S(2)}, u32[]{:S(2)}) %collective-permute-start.22) | collective-permute-done | bytes 248864 | tf_op jit(solution)/shard_map/ppermute | solution.py:357
  77.2 4.5 %collective-permute-done.26.refs_5_ = bf16[972,128]{1,0:T(8,128)(2,1)S(1)} collective-permute-done((bf16[972,128]{1,0:T(8,128)(2,1)S(1)}, bf16[972,128]{1,0:T(8,128)(2,1)S(1)}, u32[]{:S(2)}, u32[]{:S(2)}) %collective-permute-start.26) | collective-permute-done | bytes 248864 | tf_op jit(solution)/shard_map/ppermute | solution.py:357
  81.7 1.8 %combine.1 = bf16[288,1536]{1,0:T(8,128)(2,1)} custom-call(bf16[288,88]{1,0:T(8,128)(2,1)S(1)} %get-tuple-element.21.refs_0_, bf16[288,88]{1,0:T(8,128)(2,1)S(1)} %get-tuple-element.22.refs_1_, bf16[972,128]{1,0:T(8,128)(2,1)S(1)} %collective-permute-done.15.refs_2_, bf16[972,128]{1,0:T(8,128)(2,1)S(1)} %get-tuple-element.35.refs_0_.refs_3_, ...), custom_call_target="tpu_custom_call" | custom-call | tf_op jit(solution)/shard_map/combine/pallas_call | solution.py:21
  (46 shorter events, 9.1 us)
Async XLA Ops:
  0.0 12.7 %collective-permute-start.1 = (bf16[1536,1024]{1,0:T(8,128)(2,1)}, bf16[1536,1024]{1,0:T(8,128)(2,1)S(1)}, u32[]{:S(2)}, u32[]{:S(2)}) collective-permute-start(bf16[1536,1024]{1,0:T(8,128)(2,1)} %bitcast.9), channel_id=1, source_target_pairs={{0,1},{1,0},{2,3},{3,2},{4,5},{5,4},{6,7},{7,6},{8,9},{9,8},{10,11... | collective-permute-start | bytes 9437192 | tf_op jit(solution)/shard_map/ppermute | solution.py:357
  0.5 12.2 %collective-permute-start.2 = (bf16[1536,1024]{1,0:T(8,128)(2,1)}, bf16[1536,1024]{1,0:T(8,128)(2,1)S(1)}, u32[]{:S(2)}, u32[]{:S(2)}) collective-permute-start(bf16[1536,1024]{1,0:T(8,128)(2,1)} %bitcast.13), channel_id=1, source_target_pairs={{0,1},{1,0},{2,3},{3,2},{4,5},{5,4},{6,7},{7,6},{8,9},{9,8},{10,11... | collective-permute-start | bytes 9437192 | tf_op jit(solution)/shard_map/ppermute | solution.py:357
  0.5 21.5 %collective-permute-start.3 = (bf16[1024,1536]{1,0:T(8,128)(2,1)}, bf16[1024,1536]{1,0:T(8,128)(2,1)S(1)}, u32[]{:S(2)}, u32[]{:S(2)}) collective-permute-start(bf16[1024,1536]{1,0:T(8,128)(2,1)} %bitcast.5), channel_id=1, source_target_pairs={{0,1},{1,0},{2,3},{3,2},{4,5},{5,4},{6,7},{7,6},{8,9},{9,8},{10,11... | collective-permute-start | bytes 9437192 | tf_op jit(solution)/shard_map/ppermute | solution.py:357
  1.6 1.2 %copy-start.5 = (bf16[288,1536]{1,0:T(8,128)(2,1)S(1)}, bf16[288,1536]{1,0:T(8,128)(2,1)}, u32[]{:S(2)}) copy-start(bf16[288,1536]{1,0:T(8,128)(2,1)} %refs_1_.1) | copy-start | bytes 2654212
  2.8 5.6 %copy-start.4 = (f32[288,2]{0,1:T(2,128)S(1)}, f32[288,2]{0,1:T(2,128)}, u32[]{:S(2)}) copy-start(f32[288,2]{0,1:T(2,128)} %param.8) | copy-start | bytes 6916
  2.8 9.8 %copy-start.1 = (bf16[1,1536,1024]{2,1,0:T(8,128)(2,1)S(1)}, bf16[1,1536,1024]{2,1,0:T(8,128)(2,1)}, u32[]{:S(2)}) copy-start(bf16[1,1536,1024]{2,1,0:T(8,128)(2,1)} %param.9) | copy-start | bytes 9437188
  2.8 9.9 %copy-start.2 = (bf16[1,1536,1024]{2,1,0:T(8,128)(2,1)S(1)}, bf16[1,1536,1024]{2,1,0:T(8,128)(2,1)}, u32[]{:S(2)}) copy-start(bf16[1,1536,1024]{2,1,0:T(8,128)(2,1)} %param.10) | copy-start | bytes 9437188
  3.3 9.4 %collective-permute-start = (bf16[972,128]{1,0:T(8,128)(2,1)S(1)}, bf16[972,128]{1,0:T(8,128)(2,1)S(1)}, u32[]{:S(2)}, u32[]{:S(2)}) collective-permute-start(bf16[972,128]{1,0:T(8,128)(2,1)S(1)} %pick.1.refs_0_.refs_1_), channel_id=1, source_target_pairs={{0,2},{1,3},{2,0},{3,1},{4,6},{5,7},{6,4},{7,5},{8,10},{9,11},{10,... | collective-permute-start | bytes 746504 | tf_op jit(solution)/shard_map/ppermute | solution.py:357
  5.9 14.4 %collective-permute-start.4 = (bf16[972,128]{1,0:T(8,128)(2,1)S(1)}, bf16[972,128]{1,0:T(8,128)(2,1)S(1)}, u32[]{:S(2)}, u32[]{:S(2)}) collective-permute-start(bf16[972,128]{1,0:T(8,128)(2,1)S(1)} %pick.1.refs_0_.refs_1_), channel_id=1, source_target_pairs={{0,6},{1,7},{2,4},{3,5},{4,2},{5,3},{6,0},{7,1},{8,14},{9,15},{10,... | collective-permute-start | bytes 746504 | tf_op jit(solution)/shard_map/ppermute | solution.py:357
  15.2 10.7 %collective-permute-start.5 = (bf16[1296,128]{1,0:T(8,128)(2,1)S(1)}, bf16[1296,128]{1,0:T(8,128)(2,1)S(1)}, u32[]{:S(2)}, u32[]{:S(2)}) collective-permute-start(bf16[1296,128]{1,0:T(8,128)(2,1)S(1)} %get-tuple-element.25), channel_id=1, source_target_pairs={{0,8},{8,0},{16,24},{24,16},{1,9},{9,1},{17,25},{25,17},{2,10},{10... | collective-permute-start | bytes 995336 | tf_op jit(solution)/shard_map/ppermute | solution.py:357
  16.9 16.3 %collective-permute-start.6 = (bf16[1296,128]{1,0:T(8,128)(2,1)S(1)}, bf16[1296,128]{1,0:T(8,128)(2,1)S(1)}, u32[]{:S(2)}, u32[]{:S(2)}) collective-permute-start(bf16[1296,128]{1,0:T(8,128)(2,1)S(1)} %get-tuple-element.26), channel_id=1, source_target_pairs={{0,16},{8,24},{16,0},{24,8},{1,17},{9,25},{17,1},{25,9},{2,18},{10... | collective-permute-start | bytes 995336 | tf_op jit(solution)/shard_map/ppermute | solution.py:357
  18.5 15.8 %collective-permute-start.7 = (bf16[1296,128]{1,0:T(8,128)(2,1)S(1)}, bf16[1296,128]{1,0:T(8,128)(2,1)S(1)}, u32[]{:S(2)}, u32[]{:S(2)}) collective-permute-start(bf16[1296,128]{1,0:T(8,128)(2,1)S(1)} %get-tuple-element.27), channel_id=1, source_target_pairs={{0,24},{8,16},{16,8},{24,0},{1,25},{9,17},{17,9},{25,1},{2,26},{10... | collective-permute-start | bytes 995336 | tf_op jit(solution)/shard_map/ppermute | solution.py:357
  20.3 14.2 %collective-permute-start.8 = (bf16[972,128]{1,0:T(8,128)(2,1)S(1)}, bf16[972,128]{1,0:T(8,128)(2,1)S(1)}, u32[]{:S(2)}, u32[]{:S(2)}) collective-permute-start(bf16[972,128]{1,0:T(8,128)(2,1)S(1)} %pick.1.refs_0_.refs_1_), channel_id=1, source_target_pairs={{0,4},{1,5},{2,6},{3,7},{4,0},{5,1},{6,2},{7,3},{8,12},{9,13},{10,... | collective-permute-start | bytes 746504 | tf_op jit(solution)/shard_map/ppermute | solution.py:357
  24.4 15.5 %collective-permute-start.9 = (bf16[648,128]{1,0:T(8,128)(2,1)S(1)}, bf16[648,128]{1,0:T(8,128)(2,1)S(1)}, u32[]{:S(2)}, u32[]{:S(2)}) collective-permute-start(bf16[648,128]{1,0:T(8,128)(2,1)S(1)} %get-tuple-element.29), channel_id=1, source_target_pairs={{0,8},{8,0},{16,24},{24,16},{1,9},{9,1},{17,25},{25,17},{2,10},{10... | collective-permute-start | bytes 497672 | tf_op jit(solution)/shard_map/ppermute | solution.py:357
  26.0 13.8 %collective-permute-start.10 = (bf16[648,128]{1,0:T(8,128)(2,1)S(1)}, bf16[648,128]{1,0:T(8,128)(2,1)S(1)}, u32[]{:S(2)}, u32[]{:S(2)}) collective-permute-start(bf16[648,128]{1,0:T(8,128)(2,1)S(1)} %get-tuple-element.30), channel_id=1, source_target_pairs={{0,16},{8,24},{16,0},{24,8},{1,17},{9,25},{17,1},{25,9},{2,18},{10... | collective-permute-start | bytes 497672 | tf_op jit(solution)/shard_map/ppermute | solution.py:357
  33.3 7.9 %collective-permute-start.11 = (bf16[648,128]{1,0:T(8,128)(2,1)S(1)}, bf16[648,128]{1,0:T(8,128)(2,1)S(1)}, u32[]{:S(2)}, u32[]{:S(2)}) collective-permute-start(bf16[648,128]{1,0:T(8,128)(2,1)S(1)} %get-tuple-element.31), channel_id=1, source_target_pairs={{0,24},{8,16},{16,8},{24,0},{1,25},{9,17},{17,9},{25,1},{2,26},{10... | collective-permute-start | bytes 497672 | tf_op jit(solution)/shard_map/ppermute | solution.py:357
  34.5 20.5 %copy-start = (bf16[1,1024,1536]{2,1,0:T(8,128)(2,1)S(1)}, bf16[1,1024,1536]{2,1,0:T(8,128)(2,1)}, u32[]{:S(2)}) copy-start(bf16[1,1024,1536]{2,1,0:T(8,128)(2,1)} %param.11) | copy-start | bytes 9437188
  36.8 16.7 %collective-permute-start.16 = (bf16[648,128]{1,0:T(8,128)(2,1)S(1)}, bf16[648,128]{1,0:T(8,128)(2,1)S(1)}, u32[]{:S(2)}, u32[]{:S(2)}) collective-permute-start(bf16[648,128]{1,0:T(8,128)(2,1)S(1)} %get-tuple-element.32), channel_id=1, source_target_pairs={{0,8},{8,0},{16,24},{24,16},{1,9},{9,1},{17,25},{25,17},{2,10},{10... | collective-permute-start | bytes 497672 | tf_op jit(solution)/shard_map/ppermute | solution.py:357
  41.2 5.8 %collective-permute-start.14 = (bf16[324,128]{1,0:T(8,128)(2,1)S(1)}, bf16[324,128]{1,0:T(8,128)(2,1)S(1)}, u32[]{:S(2)}, u32[]{:S(2)}) collective-permute-start(bf16[324,128]{1,0:T(8,128)(2,1)S(1)} %act.4.refs_0_.refs_1_), channel_id=1, source_target_pairs={{0,24},{8,16},{16,8},{24,0},{1,25},{9,17},{17,9},{25,1},{2,26},{10... | collective-permute-start | bytes 248840 | tf_op jit(solution)/shard_map/ppermute | solution.py:357
  42.7 6.6 %collective-permute-start.13 = (bf16[324,128]{1,0:T(8,128)(2,1)S(1)}, bf16[324,128]{1,0:T(8,128)(2,1)S(1)}, u32[]{:S(2)}, u32[]{:S(2)}) collective-permute-start(bf16[324,128]{1,0:T(8,128)(2,1)S(1)} %act.4.refs_0_.refs_1_), channel_id=1, source_target_pairs={{0,16},{8,24},{16,0},{24,8},{1,17},{9,25},{17,1},{25,9},{2,18},{10... | collective-permute-start | bytes 248840 | tf_op jit(solution)/shard_map/ppermute | solution.py:357
  44.1 6.4 %collective-permute-start.12 = (bf16[324,128]{1,0:T(8,128)(2,1)S(1)}, bf16[324,128]{1,0:T(8,128)(2,1)S(1)}, u32[]{:S(2)}, u32[]{:S(2)}) collective-permute-start(bf16[324,128]{1,0:T(8,128)(2,1)S(1)} %act.4.refs_0_.refs_1_), channel_id=1, source_target_pairs={{0,8},{8,0},{16,24},{24,16},{1,9},{9,1},{17,25},{25,17},{2,10},{10... | collective-permute-start | bytes 248840 | tf_op jit(solution)/shard_map/ppermute | solution.py:357
  45.0 15.1 %collective-permute-start.17 = (bf16[648,128]{1,0:T(8,128)(2,1)S(1)}, bf16[648,128]{1,0:T(8,128)(2,1)S(1)}, u32[]{:S(2)}, u32[]{:S(2)}) collective-permute-start(bf16[648,128]{1,0:T(8,128)(2,1)S(1)} %get-tuple-element.33), channel_id=1, source_target_pairs={{0,16},{8,24},{16,0},{24,8},{1,17},{9,25},{17,1},{25,9},{2,18},{10... | collective-permute-start | bytes 497672 | tf_op jit(solution)/shard_map/ppermute | solution.py:357
  47.0 14.7 %collective-permute-start.18 = (bf16[648,128]{1,0:T(8,128)(2,1)S(1)}, bf16[648,128]{1,0:T(8,128)(2,1)S(1)}, u32[]{:S(2)}, u32[]{:S(2)}) collective-permute-start(bf16[648,128]{1,0:T(8,128)(2,1)S(1)} %get-tuple-element.34), channel_id=1, source_target_pairs={{0,24},{8,16},{16,8},{24,0},{1,25},{9,17},{17,9},{25,1},{2,26},{10... | collective-permute-start | bytes 497672 | tf_op jit(solution)/shard_map/ppermute | solution.py:357
  49.2 15.5 %collective-permute-start.21 = (bf16[648,128]{1,0:T(8,128)(2,1)S(1)}, bf16[648,128]{1,0:T(8,128)(2,1)S(1)}, u32[]{:S(2)}, u32[]{:S(2)}) collective-permute-start(bf16[648,128]{1,0:T(8,128)(2,1)S(1)} %act.3.refs_0_.refs_1_), channel_id=1, source_target_pairs={{0,24},{8,16},{16,8},{24,0},{1,25},{9,17},{17,9},{25,1},{2,26},{10... | collective-permute-start | bytes 497672 | tf_op jit(solution)/shard_map/ppermute | solution.py:357
  50.5 16.6 %collective-permute-start.20 = (bf16[648,128]{1,0:T(8,128)(2,1)S(1)}, bf16[648,128]{1,0:T(8,128)(2,1)S(1)}, u32[]{:S(2)}, u32[]{:S(2)}) collective-permute-start(bf16[648,128]{1,0:T(8,128)(2,1)S(1)} %act.3.refs_0_.refs_1_), channel_id=1, source_target_pairs={{0,16},{8,24},{16,0},{24,8},{1,17},{9,25},{17,1},{25,9},{2,18},{10... | collective-permute-start | bytes 497672 | tf_op jit(solution)/shard_map/ppermute | solution.py:357
  53.5 13.7 %collective-permute-start.19 = (bf16[648,128]{1,0:T(8,128)(2,1)S(1)}, bf16[648,128]{1,0:T(8,128)(2,1)S(1)}, u32[]{:S(2)}, u32[]{:S(2)}) collective-permute-start(bf16[648,128]{1,0:T(8,128)(2,1)S(1)} %act.3.refs_0_.refs_1_), channel_id=1, source_target_pairs={{0,8},{8,0},{16,24},{24,16},{1,9},{9,1},{17,25},{25,17},{2,10},{10... | collective-permute-start | bytes 497672 | tf_op jit(solution)/shard_map/ppermute | solution.py:357
  60.1 12.8 %collective-permute-start.15 = (bf16[972,128]{1,0:T(8,128)(2,1)S(1)}, bf16[972,128]{1,0:T(8,128)(2,1)S(1)}, u32[]{:S(2)}, u32[]{:S(2)}) collective-permute-start(bf16[972,128]{1,0:T(8,128)(2,1)S(1)} %down.3.refs_0_), channel_id=1, source_target_pairs={{0,6},{1,7},{2,4},{3,5},{4,2},{5,3},{6,0},{7,1},{8,14},{9,15},{10,... | collective-permute-start | bytes 746504 | tf_op jit(solution)/shard_map/ppermute | solution.py:357
  61.8 6.9 %collective-permute-start.25 = (bf16[324,128]{1,0:T(8,128)(2,1)S(1)}, bf16[324,128]{1,0:T(8,128)(2,1)S(1)}, u32[]{:S(2)}, u32[]{:S(2)}) collective-permute-start(bf16[324,128]{1,0:T(8,128)(2,1)S(1)} %act.5.refs_0_.refs_1_), channel_id=1, source_target_pairs={{0,24},{8,16},{16,8},{24,0},{1,25},{9,17},{17,9},{25,1},{2,26},{10... | collective-permute-start | bytes 248840 | tf_op jit(solution)/shard_map/ppermute | solution.py:357
  64.7 4.9 %collective-permute-start.24 = (bf16[324,128]{1,0:T(8,128)(2,1)S(1)}, bf16[324,128]{1,0:T(8,128)(2,1)S(1)}, u32[]{:S(2)}, u32[]{:S(2)}) collective-permute-start(bf16[324,128]{1,0:T(8,128)(2,1)S(1)} %act.5.refs_0_.refs_1_), channel_id=1, source_target_pairs={{0,16},{8,24},{16,0},{24,8},{1,17},{9,25},{17,1},{25,9},{2,18},{10... | collective-permute-start | bytes 248840 | tf_op jit(solution)/shard_map/ppermute | solution.py:357
  67.2 4.5 %collective-permute-start.23 = (bf16[324,128]{1,0:T(8,128)(2,1)S(1)}, bf16[324,128]{1,0:T(8,128)(2,1)S(1)}, u32[]{:S(2)}, u32[]{:S(2)}) collective-permute-start(bf16[324,128]{1,0:T(8,128)(2,1)S(1)} %act.5.refs_0_.refs_1_), channel_id=1, source_target_pairs={{0,8},{8,0},{16,24},{24,16},{1,9},{9,1},{17,25},{25,17},{2,10},{10... | collective-permute-start | bytes 248840 | tf_op jit(solution)/shard_map/ppermute | solution.py:357
  68.5 8.7 %collective-permute-start.22 = (bf16[972,128]{1,0:T(8,128)(2,1)S(1)}, bf16[972,128]{1,0:T(8,128)(2,1)S(1)}, u32[]{:S(2)}, u32[]{:S(2)}) collective-permute-start(bf16[972,128]{1,0:T(8,128)(2,1)S(1)} %get-tuple-element.36), channel_id=1, source_target_pairs={{0,2},{1,3},{2,0},{3,1},{4,6},{5,7},{6,4},{7,5},{8,10},{9,11},{10,... | collective-permute-start | bytes 746504 | tf_op jit(solution)/shard_map/ppermute | solution.py:357
  72.8 8.9 %collective-permute-start.26 = (bf16[972,128]{1,0:T(8,128)(2,1)S(1)}, bf16[972,128]{1,0:T(8,128)(2,1)S(1)}, u32[]{:S(2)}, u32[]{:S(2)}) collective-permute-start(bf16[972,128]{1,0:T(8,128)(2,1)S(1)} %down.5), channel_id=1, source_target_pairs={{0,4},{1,5},{2,6},{3,7},{4,0},{5,1},{6,2},{7,3},{8,12},{9,13},{10,... | collective-permute-start | bytes 746504 | tf_op jit(solution)/shard_map/ppermute | solution.py:357
  (1 other events, 0.7 us)

commit v4 on v3

--- a/solution.py
+++ b/solution.py
@@ -64,14 +64,19 @@
     return high, (value - high.astype(jnp.float32)).astype(jnp.bfloat16)
 
 
-def back_kernel(ids_ref, scales_ref, high_ref, low_ref):
+def back_kernel(ids_ref, scales_ref, hits_ref, scale_ref):
     ids = ids_ref[...]
     scale = jnp.sum(jnp.where(ids == 0, scales_ref[...], 0.0), axis=0, keepdims=True)
-    high_ref[...], low_ref[...] = split((slot_hits(ids, high_ref.shape[1]) * scale).T)
+    hits = slot_hits(ids, hits_ref.shape[1])
+    hits_ref[...] = hits.T.astype(hits_ref.dtype)
+    scale_ref[...] = jnp.broadcast_to(scale, (scale_ref.shape[1], scale.shape[1])).T
 
 
 def back(ids, scales, slots, after):
-    outs = [jax.ShapeDtypeStruct((ids.shape[1], slots), jnp.bfloat16)] * 2
+    outs = [
+        jax.ShapeDtypeStruct((ids.shape[1], slots), jnp.bfloat16),
+        jax.ShapeDtypeStruct((ids.shape[1], 128), jnp.float32),
+    ]
     return call(back_kernel, "back", outs, [ids, scales], after)
 
 
@@ -152,16 +157,15 @@
     return call(kernel, "down", outs, [*acts, *weights], after, flops)
 
 
-def combine_kernel(back_high, back_low, *refs):
+def combine_kernel(hits, scale, *refs):
     terms, out_ref = refs[:-1], refs[-1]
     slot_out = terms[0][...].astype(jnp.float32)
     for term in terms[1:]:
         slot_out += term[...].astype(jnp.float32)
     high, low = split(slot_out)
-    total = jnp.dot(back_low[...], high, preferred_element_type=jnp.float32)
-    total += jnp.dot(back_high[...], low, preferred_element_type=jnp.float32)
-    total += jnp.dot(back_high[...], high, preferred_element_type=jnp.float32)
-    out_ref[...] = total.astype(out_ref.dtype)
+    total = jnp.dot(hits[...], low, preferred_element_type=jnp.float32)
+    total += jnp.dot(hits[...], high, preferred_element_type=jnp.float32)
+    out_ref[...] = (total * scale[:, 0:1]).astype(out_ref.dtype)
 
 
 def combine(backs, terms):
@@ -240,27 +244,27 @@
     return call(pick_packed_kernel, "pick", outs, [ids, tokens], flops=30000000000)[0]
 
 
-def project_packed_kernel(parts, n_x, *refs):
-    xs, weights, outs, held = refs[:n_x], refs[n_x:-parts - 1], refs[-parts - 1 : -1], refs[-1]
+def project_packed_kernel(parts, chosen, n_x, *refs):
+    xs, weights, outs, held = refs[:n_x], refs[n_x : n_x + 4], refs[n_x + 4 : -1], refs[-1]
     me = lax.axis_index("fsdp")
     unpack([(x, 1) for x in xs], held)
     x = held[...]
     quarter = weights[0].shape[1] // parts
-    for k in [*range(parts - 1, 0, -1), 0]:
+    for out, k in zip(outs, chosen):
         cols = pl.ds(pl.multiple_of((me ^ k) * quarter, quarter), quarter)
         value = [jnp.dot(x, w[:, cols], preferred_element_type=jnp.float32) for w in weights]
-        pack(outs[k], jnp.concatenate(value, axis=1), n_x)
-
-
-def project_packed(xs, weights, parts, after):
+        pack(out, jnp.concatenate(value, axis=1), n_x)
+
+
+def project_packed(xs, weights, parts, chosen, after):
     depth, width = weights[0].shape
     quarter = width // parts
     rows = room_for(len(xs))
-    kinds = [jnp.float32] + [jnp.bfloat16] * (parts - 1)
+    kinds = [jnp.bfloat16 if k else jnp.float32 for k in chosen]
     size = (packed_rows(len(xs), len(weights) * quarter), 128)
     outs = [jax.ShapeDtypeStruct(size, kind) for kind in kinds]
-    kernel = functools.partial(project_packed_kernel, parts, len(xs))
-    flops = 2 * rows * depth * len(weights) * width
+    kernel = functools.partial(project_packed_kernel, parts, chosen, len(xs))
+    flops = 2 * rows * depth * len(weights) * quarter * len(chosen)
     scratch = [pltpu.VMEM((rows, depth), xs[0].dtype)]
     return call(kernel, "project", outs, [*xs, *weights], after, flops, scratch)
 
@@ -322,7 +326,7 @@
     return call(kernel, "down", outs, [*acts, *weights], after, flops, scratch)
 
 
-def combine_packed_kernel(back_high, back_low, *refs):
+def combine_packed_kernel(hits, scale, *refs):
     terms, out_ref, held = refs[:-2], refs[-2], refs[-1]
     lead, rest = lead_of(CAP)
     total = terms[0][...].astype(jnp.float32)
@@ -338,10 +342,9 @@
         held[:lead, 128 * j : 128 * (j + 1)] = total[j * lead : (j + 1) * lead]
     held[lead:, :] = jnp.concatenate(others, axis=0)
     high, low = split(held[...])
-    total = jnp.dot(back_low[...], high, preferred_element_type=jnp.float32)
-    total += jnp.dot(back_high[...], low, preferred_element_type=jnp.float32)
-    total += jnp.dot(back_high[...], high, preferred_element_type=jnp.float32)
-    out_ref[...] = total.astype(out_ref.dtype)
+    total = jnp.dot(hits[...], low, preferred_element_type=jnp.float32)
+    total += jnp.dot(hits[...], high, preferred_element_type=jnp.float32)
+    out_ref[...] = (total * scale[:, 0:1]).astype(out_ref.dtype)
 
 
 def combine_packed(backs, terms):
@@ -376,7 +379,14 @@
             xs = [blocks[s] for s in group]
             weights = [own[0], other[0], own[1], other[1]]
             deps = (*last, other[2]) if g == WAIT else last
-            out = (project_packed if packed else project)(xs, weights, n_fsdp, deps)
+            if packed:
+                others = list(range(n_fsdp - 1, 0, -1))
+                out = []
+                for k in [*others, 0]:
+                    out = [*project_packed(xs, weights, n_fsdp, [k], deps), *out]
+                    deps = (out[0],)
+            else:
+                out = project(xs, weights, n_fsdp, deps)
             parts[g] = [out[0]] + [across(out[k], k) for k in range(n_fsdp - 1, 0, -1)][::-1]
             last = (out[0],)
         elif op == "A":

time: 83.7 us -> 82.9 us (level)
  starting transfers between devices: 39 us -> 37 us
  Pallas kernels: 13.8 us -> 15.3 us
    ppermute x27, starting transfers between devices: 39 us -> 37 us  [local(): lax.ppermute(v, axis, [(i, i ^ k) for i in range(size)])]
    pallas_call x12 -> x21, Pallas kernels: 13.8 us -> 15.3 us  [call(): pl.pallas_call(body, out_shape=outs, in_specs=[pl.BlockSpec(memory_space=...]
  transfers between devices with their start and end apart: 27 -> 27, of which waited for: 12 -> 13; matrix products, arithmetic and copies ran while one was open for 0% -> 0% of each run, Pallas kernels for 14% -> 17%
where the time goes in v4:
time: 82.9 us; the launch traced here: 82.7 us
  starting transfers between devices  37 us (45%)
  waiting for transfers between devices  28.4 us (34%)
  Pallas kernels  15.3 us (18%)
  local copies, waits for them, and re-layouts  1.87 us (2%)
    ppermute x27, starting transfers between devices, local(): lax.ppermute(v, axis, [(i, i ^ k) for i in range(size)])  37 us
    ppermute x27, waiting for transfers between devices, local(): lax.ppermute(v, axis, [(i, i ^ k) for i in range(size)])  28.4 us
    pallas_call x21, Pallas kernels, call(): pl.pallas_call(body, out_shape=outs, in_specs=[pl.BlockSpec(memory_space=...  15.3 us
    unnamed x12, local copies, waits for them, and re-layouts  1.87 us
  transfers between devices with their start and end apart: 27, of which 13 were waited for; matrix products, arithmetic and copies ran while one was open for 0% of the time, Pallas kernels for 17%

profile of v4, /device:TPU:0, one launch (start us, length us, event | category | flops | bytes accessed | tf_op | source)
XLA Modules:
  0.0 82.7 jit_solution(15455814312439893738)
XLA Ops:
  1.7 1.2 %copy-done.5 = bf16[288,1536]{1,0:T(8,128)(2,1)S(1)} copy-done((bf16[288,1536]{1,0:T(8,128)(2,1)S(1)}, bf16[288,1536]{1,0:T(8,128)(2,1)}, u32[]{:S(2)}) %copy-start.5) | copy-done | bytes 884760
  3.3 2.6 %collective-permute-start = (bf16[972,128]{1,0:T(8,128)(2,1)S(1)}, bf16[972,128]{1,0:T(8,128)(2,1)S(1)}, u32[]{:S(2)}, u32[]{:S(2)}) collective-permute-start(bf16[972,128]{1,0:T(8,128)(2,1)S(1)} %pick.1.refs_0_.refs_1_), channel_id=1, source_target_pairs={{0,2},{1,3},{2,0},{3,1},{4,6},{5,7},{6,4},{7,5},{8,10},{9,11},{10,... | collective-permute-start | bytes 746504 | tf_op jit(solution)/shard_map/ppermute | solution.py:360
  5.9 2.5 %collective-permute-start.4 = (bf16[972,128]{1,0:T(8,128)(2,1)S(1)}, bf16[972,128]{1,0:T(8,128)(2,1)S(1)}, u32[]{:S(2)}, u32[]{:S(2)}) collective-permute-start(bf16[972,128]{1,0:T(8,128)(2,1)S(1)} %pick.1.refs_0_.refs_1_), channel_id=1, source_target_pairs={{0,6},{1,7},{2,4},{3,5},{4,2},{5,3},{6,0},{7,1},{8,14},{9,15},{10,... | collective-permute-start | bytes 746504 | tf_op jit(solution)/shard_map/ppermute | solution.py:360
  8.7 4.0 %collective-permute-done.refs_2_ = bf16[972,128]{1,0:T(8,128)(2,1)S(1)} collective-permute-done((bf16[972,128]{1,0:T(8,128)(2,1)S(1)}, bf16[972,128]{1,0:T(8,128)(2,1)S(1)}, u32[]{:S(2)}, u32[]{:S(2)}) %collective-permute-start) | collective-permute-done | bytes 248864 | tf_op jit(solution)/shard_map/ppermute | solution.py:360
  12.7 0.8 project.12.refs_0_
  15.1 1.7 %collective-permute-start.5 = (bf16[1296,128]{1,0:T(8,128)(2,1)S(1)}, bf16[1296,128]{1,0:T(8,128)(2,1)S(1)}, u32[]{:S(2)}, u32[]{:S(2)}) collective-permute-start(bf16[1296,128]{1,0:T(8,128)(2,1)S(1)} %project.14.refs_0_), channel_id=1, source_target_pairs={{0,8},{8,0},{16,24},{24,16},{1,9},{9,1},{17,25},{25,17},{2,10},{10... | collective-permute-start | bytes 995336 | tf_op jit(solution)/shard_map/ppermute | solution.py:360
  16.8 1.5 %collective-permute-start.6 = (bf16[1296,128]{1,0:T(8,128)(2,1)S(1)}, bf16[1296,128]{1,0:T(8,128)(2,1)S(1)}, u32[]{:S(2)}, u32[]{:S(2)}) collective-permute-start(bf16[1296,128]{1,0:T(8,128)(2,1)S(1)} %project.13.refs_0_), channel_id=1, source_target_pairs={{0,16},{8,24},{16,0},{24,8},{1,17},{9,25},{17,1},{25,9},{2,18},{10... | collective-permute-start | bytes 995336 | tf_op jit(solution)/shard_map/ppermute | solution.py:360
  18.7 1.6 %collective-permute-done.4.refs_2_.refs_1_ = bf16[972,128]{1,0:T(8,128)(2,1)S(1)} collective-permute-done((bf16[972,128]{1,0:T(8,128)(2,1)S(1)}, bf16[972,128]{1,0:T(8,128)(2,1)S(1)}, u32[]{:S(2)}, u32[]{:S(2)}) %collective-permute-start.4) | collective-permute-done | bytes 248864 | tf_op jit(solution)/shard_map/ppermute | solution.py:360
  20.3 1.7 %collective-permute-start.8 = (bf16[972,128]{1,0:T(8,128)(2,1)S(1)}, bf16[972,128]{1,0:T(8,128)(2,1)S(1)}, u32[]{:S(2)}, u32[]{:S(2)}) collective-permute-start(bf16[972,128]{1,0:T(8,128)(2,1)S(1)} %pick.1.refs_0_.refs_1_), channel_id=1, source_target_pairs={{0,4},{1,5},{2,6},{3,7},{4,0},{5,1},{6,2},{7,3},{8,12},{9,13},{10,... | collective-permute-start | bytes 746504 | tf_op jit(solution)/shard_map/ppermute | solution.py:360
  25.0 1.6 %collective-permute-start.9 = (bf16[648,128]{1,0:T(8,128)(2,1)S(1)}, bf16[648,128]{1,0:T(8,128)(2,1)S(1)}, u32[]{:S(2)}, u32[]{:S(2)}) collective-permute-start(bf16[648,128]{1,0:T(8,128)(2,1)S(1)} %project.18.refs_0_), channel_id=1, source_target_pairs={{0,8},{8,0},{16,24},{24,16},{1,9},{9,1},{17,25},{25,17},{2,10},{10... | collective-permute-start | bytes 497672 | tf_op jit(solution)/shard_map/ppermute | solution.py:360
  27.2 1.6 %collective-permute-start.10 = (bf16[648,128]{1,0:T(8,128)(2,1)S(1)}, bf16[648,128]{1,0:T(8,128)(2,1)S(1)}, u32[]{:S(2)}, u32[]{:S(2)}) collective-permute-start(bf16[648,128]{1,0:T(8,128)(2,1)S(1)} %project.17.refs_0_), channel_id=1, source_target_pairs={{0,16},{8,24},{16,0},{24,8},{1,17},{9,25},{17,1},{25,9},{2,18},{10... | collective-permute-start | bytes 497672 | tf_op jit(solution)/shard_map/ppermute | solution.py:360
  28.8 4.3 %collective-permute-done.6.refs_3_ = bf16[1296,128]{1,0:T(8,128)(2,1)S(1)} collective-permute-done((bf16[1296,128]{1,0:T(8,128)(2,1)S(1)}, bf16[1296,128]{1,0:T(8,128)(2,1)S(1)}, u32[]{:S(2)}, u32[]{:S(2)}) %collective-permute-start.6) | collective-permute-done | bytes 331808 | tf_op jit(solution)/shard_map/ppermute | solution.py:360
  36.5 3.0 %collective-permute-start.16 = (bf16[648,128]{1,0:T(8,128)(2,1)S(1)}, bf16[648,128]{1,0:T(8,128)(2,1)S(1)}, u32[]{:S(2)}, u32[]{:S(2)}) collective-permute-start(bf16[648,128]{1,0:T(8,128)(2,1)S(1)} %project.22.refs_0_), channel_id=1, source_target_pairs={{0,8},{8,0},{16,24},{24,16},{1,9},{9,1},{17,25},{25,17},{2,10},{10... | collective-permute-start | bytes 497672 | tf_op jit(solution)/shard_map/ppermute | solution.py:360
  40.2 0.9 %collective-permute-done.11.refs_4_ = bf16[648,128]{1,0:T(8,128)(2,1)S(1)} collective-permute-done((bf16[648,128]{1,0:T(8,128)(2,1)S(1)}, bf16[648,128]{1,0:T(8,128)(2,1)S(1)}, u32[]{:S(2)}, u32[]{:S(2)}) %collective-permute-start.11) | collective-permute-done | bytes 165920 | tf_op jit(solution)/shard_map/ppermute | solution.py:360
  41.3 1.5 %collective-permute-start.14 = (bf16[324,128]{1,0:T(8,128)(2,1)S(1)}, bf16[324,128]{1,0:T(8,128)(2,1)S(1)}, u32[]{:S(2)}, u32[]{:S(2)}) collective-permute-start(bf16[324,128]{1,0:T(8,128)(2,1)S(1)} %act.4.refs_0_.refs_1_), channel_id=1, source_target_pairs={{0,24},{8,16},{16,8},{24,0},{1,25},{9,17},{17,9},{25,1},{2,26},{10... | collective-permute-start | bytes 248840 | tf_op jit(solution)/shard_map/ppermute | solution.py:360
  42.7 1.5 %collective-permute-start.13 = (bf16[324,128]{1,0:T(8,128)(2,1)S(1)}, bf16[324,128]{1,0:T(8,128)(2,1)S(1)}, u32[]{:S(2)}, u32[]{:S(2)}) collective-permute-start(bf16[324,128]{1,0:T(8,128)(2,1)S(1)} %act.4.refs_0_.refs_1_), channel_id=1, source_target_pairs={{0,16},{8,24},{16,0},{24,8},{1,17},{9,25},{17,1},{25,9},{2,18},{10... | collective-permute-start | bytes 248840 | tf_op jit(solution)/shard_map/ppermute | solution.py:360
  44.8 1.7 %collective-permute-start.17 = (bf16[648,128]{1,0:T(8,128)(2,1)S(1)}, bf16[648,128]{1,0:T(8,128)(2,1)S(1)}, u32[]{:S(2)}, u32[]{:S(2)}) collective-permute-start(bf16[648,128]{1,0:T(8,128)(2,1)S(1)} %project.21.refs_0_), channel_id=1, source_target_pairs={{0,16},{8,24},{16,0},{24,8},{1,17},{9,25},{17,1},{25,9},{2,18},{10... | collective-permute-start | bytes 497672 | tf_op jit(solution)/shard_map/ppermute | solution.py:360
  46.8 1.7 %collective-permute-start.18 = (bf16[648,128]{1,0:T(8,128)(2,1)S(1)}, bf16[648,128]{1,0:T(8,128)(2,1)S(1)}, u32[]{:S(2)}, u32[]{:S(2)}) collective-permute-start(bf16[648,128]{1,0:T(8,128)(2,1)S(1)} %project.20.refs_0_), channel_id=1, source_target_pairs={{0,24},{8,16},{16,8},{24,0},{1,25},{9,17},{17,9},{25,1},{2,26},{10... | collective-permute-start | bytes 497672 | tf_op jit(solution)/shard_map/ppermute | solution.py:360
  48.5 2.4 %collective-permute-done.13.refs_3_ = bf16[324,128]{1,0:T(8,128)(2,1)S(1)} collective-permute-done((bf16[324,128]{1,0:T(8,128)(2,1)S(1)}, bf16[324,128]{1,0:T(8,128)(2,1)S(1)}, u32[]{:S(2)}, u32[]{:S(2)}) %collective-permute-start.13) | collective-permute-done | bytes 82976 | tf_op jit(solution)/shard_map/ppermute | solution.py:360
  51.0 2.6 %collective-permute-start.20 = (bf16[648,128]{1,0:T(8,128)(2,1)S(1)}, bf16[648,128]{1,0:T(8,128)(2,1)S(1)}, u32[]{:S(2)}, u32[]{:S(2)}) collective-permute-start(bf16[648,128]{1,0:T(8,128)(2,1)S(1)} %act.3.refs_0_.refs_1_), channel_id=1, source_target_pairs={{0,16},{8,24},{16,0},{24,8},{1,17},{9,25},{17,1},{25,9},{2,18},{10... | collective-permute-start | bytes 497672 | tf_op jit(solution)/shard_map/ppermute | solution.py:360
  53.6 1.5 %collective-permute-start.19 = (bf16[648,128]{1,0:T(8,128)(2,1)S(1)}, bf16[648,128]{1,0:T(8,128)(2,1)S(1)}, u32[]{:S(2)}, u32[]{:S(2)}) collective-permute-start(bf16[648,128]{1,0:T(8,128)(2,1)S(1)} %act.3.refs_0_.refs_1_), channel_id=1, source_target_pairs={{0,8},{8,0},{16,24},{24,16},{1,9},{9,1},{17,25},{25,17},{2,10},{10... | collective-permute-start | bytes 497672 | tf_op jit(solution)/shard_map/ppermute | solution.py:360
  55.1 1.1 %down.3.refs_0_ = bf16[972,128]{1,0:T(8,128)(2,1)S(1)} custom-call(bf16[324,128]{1,0:T(8,128)(2,1)S(1)} %act.4.refs_0_.refs_1_, bf16[324,128]{1,0:T(8,128)(2,1)S(1)} %act.4.refs_0_.refs_1_, bf16[324,128]{1,0:T(8,128)(2,1)S(1)} %collective-permute-done.12.refs_2_, bf16[324,128]{1,0:T(8,128)(2,1)S(1)} %collective-permute-done.13.refs_3_, ...), custom_call_target="tpu_custom_call" | custom-call | flops 603979776 | tf_op jit(solution)/shard_map/down/pallas_call | solution.py:21
  56.3 3.4 %collective-permute-done.17.refs_3_ = bf16[648,128]{1,0:T(8,128)(2,1)S(1)} collective-permute-done((bf16[648,128]{1,0:T(8,128)(2,1)S(1)}, bf16[648,128]{1,0:T(8,128)(2,1)S(1)}, u32[]{:S(2)}, u32[]{:S(2)}) %collective-permute-start.17) | collective-permute-done | bytes 165920 | tf_op jit(solution)/shard_map/ppermute | solution.py:360
  59.7 3.8 %collective-permute-start.15 = (bf16[972,128]{1,0:T(8,128)(2,1)S(1)}, bf16[972,128]{1,0:T(8,128)(2,1)S(1)}, u32[]{:S(2)}, u32[]{:S(2)}) collective-permute-start(bf16[972,128]{1,0:T(8,128)(2,1)S(1)} %down.3.refs_0_), channel_id=1, source_target_pairs={{0,6},{1,7},{2,4},{3,5},{4,2},{5,3},{6,0},{7,1},{8,14},{9,15},{10,... | collective-permute-start | bytes 746504 | tf_op jit(solution)/shard_map/ppermute | solution.py:360
  64.2 2.5 %collective-permute-start.24 = (bf16[324,128]{1,0:T(8,128)(2,1)S(1)}, bf16[324,128]{1,0:T(8,128)(2,1)S(1)}, u32[]{:S(2)}, u32[]{:S(2)}) collective-permute-start(bf16[324,128]{1,0:T(8,128)(2,1)S(1)} %act.5.refs_0_.refs_1_), channel_id=1, source_target_pairs={{0,16},{8,24},{16,0},{24,8},{1,17},{9,25},{17,1},{25,9},{2,18},{10... | collective-permute-start | bytes 248840 | tf_op jit(solution)/shard_map/ppermute | solution.py:360
  67.2 1.3 %down.4 = (bf16[972,128]{1,0:T(8,128)(2,1)S(1)}, bf16[972,128]{1,0:T(8,128)(2,1)S(1)}) custom-call(bf16[324,128]{1,0:T(8,128)(2,1)S(1)} %act.5.refs_0_.refs_1_, bf16[648,128]{1,0:T(8,128)(2,1)S(1)} %act.3.refs_0_.refs_1_, bf16[648,128]{1,0:T(8,128)(2,1)S(1)} %collective-permute-done.19.refs_2_, bf16[648,128]{1,0:T(8,128)(2,1)S(1)} %collective-permute-done.20.refs_3_, ...), custom_call_target="tpu_custom_call" | custom-call | flops 1107296256 | tf_op jit(solution)/shard_map/down/pallas_call | solution.py:21
  69.2 0.8 collective-permute-done.24.refs_3_
  70.0 1.2 %collective-permute-done.23.refs_2_ = bf16[324,128]{1,0:T(8,128)(2,1)S(1)} collective-permute-done((bf16[324,128]{1,0:T(8,128)(2,1)S(1)}, bf16[324,128]{1,0:T(8,128)(2,1)S(1)}, u32[]{:S(2)}, u32[]{:S(2)}) %collective-permute-start.23) | collective-permute-done | bytes 82976 | tf_op jit(solution)/shard_map/ppermute | solution.py:360
  71.2 1.1 %down.5 = bf16[972,128]{1,0:T(8,128)(2,1)S(1)} custom-call(bf16[972,128]{1,0:T(8,128)(2,1)S(1)} %get-tuple-element.11.refs_0_.refs_3_, bf16[324,128]{1,0:T(8,128)(2,1)S(1)} %act.5.refs_0_.refs_1_, bf16[324,128]{1,0:T(8,128)(2,1)S(1)} %collective-permute-done.23.refs_2_, bf16[324,128]{1,0:T(8,128)(2,1)S(1)} %collective-permute-done.24.refs_3_, ...), custom_call_target="tpu_custom_call" | custom-call | flops 603979776 | tf_op jit(solution)/shard_map/down/pallas_call | solution.py:21
  72.4 4.0 %collective-permute-done.22.refs_4_ = bf16[972,128]{1,0:T(8,128)(2,1)S(1)} collective-permute-done((bf16[972,128]{1,0:T(8,128)(2,1)S(1)}, bf16[972,128]{1,0:T(8,128)(2,1)S(1)}, u32[]{:S(2)}, u32[]{:S(2)}) %collective-permute-start.22) | collective-permute-done | bytes 248864 | tf_op jit(solution)/shard_map/ppermute | solution.py:360
  76.4 4.7 %collective-permute-done.26.refs_5_ = bf16[972,128]{1,0:T(8,128)(2,1)S(1)} collective-permute-done((bf16[972,128]{1,0:T(8,128)(2,1)S(1)}, bf16[972,128]{1,0:T(8,128)(2,1)S(1)}, u32[]{:S(2)}, u32[]{:S(2)}) %collective-permute-start.26) | collective-permute-done | bytes 248864 | tf_op jit(solution)/shard_map/ppermute | solution.py:360
  81.2 1.6 %combine.1 = bf16[288,1536]{1,0:T(8,128)(2,1)} custom-call(bf16[288,88]{1,0:T(8,128)(2,1)S(1)} %get-tuple-element.9.refs_0_, f32[288,128]{1,0:T(8,128)S(1)} %get-tuple-element.10.refs_1_, bf16[972,128]{1,0:T(8,128)(2,1)S(1)} %collective-permute-done.15.refs_2_, bf16[972,128]{1,0:T(8,128)(2,1)S(1)} %get-tuple-element.11.refs_0_.refs_3_, ...), custom_call_target="tpu_custom_call" | custom-call | tf_op jit(solution)/shard_map/combine/pallas_call | solution.py:21
  (55 shorter events, 14.8 us)
Async XLA Ops:
  0.0 12.7 %collective-permute-start.1 = (bf16[1536,1024]{1,0:T(8,128)(2,1)}, bf16[1536,1024]{1,0:T(8,128)(2,1)S(1)}, u32[]{:S(2)}, u32[]{:S(2)}) collective-permute-start(bf16[1536,1024]{1,0:T(8,128)(2,1)} %bitcast.5), channel_id=1, source_target_pairs={{0,1},{1,0},{2,3},{3,2},{4,5},{5,4},{6,7},{7,6},{8,9},{9,8},{10,11... | collective-permute-start | bytes 9437192 | tf_op jit(solution)/shard_map/ppermute | solution.py:360
  0.5 12.2 %collective-permute-start.2 = (bf16[1536,1024]{1,0:T(8,128)(2,1)}, bf16[1536,1024]{1,0:T(8,128)(2,1)S(1)}, u32[]{:S(2)}, u32[]{:S(2)}) collective-permute-start(bf16[1536,1024]{1,0:T(8,128)(2,1)} %bitcast.18), channel_id=1, source_target_pairs={{0,1},{1,0},{2,3},{3,2},{4,5},{5,4},{6,7},{7,6},{8,9},{9,8},{10,11... | collective-permute-start | bytes 9437192 | tf_op jit(solution)/shard_map/ppermute | solution.py:360
  0.5 22.4 %collective-permute-start.3 = (bf16[1024,1536]{1,0:T(8,128)(2,1)}, bf16[1024,1536]{1,0:T(8,128)(2,1)S(1)}, u32[]{:S(2)}, u32[]{:S(2)}) collective-permute-start(bf16[1024,1536]{1,0:T(8,128)(2,1)} %bitcast.31), channel_id=1, source_target_pairs={{0,1},{1,0},{2,3},{3,2},{4,5},{5,4},{6,7},{7,6},{8,9},{9,8},{10,11... | collective-permute-start | bytes 9437192 | tf_op jit(solution)/shard_map/ppermute | solution.py:360
  1.6 1.2 %copy-start.5 = (bf16[288,1536]{1,0:T(8,128)(2,1)S(1)}, bf16[288,1536]{1,0:T(8,128)(2,1)}, u32[]{:S(2)}) copy-start(bf16[288,1536]{1,0:T(8,128)(2,1)} %refs_1_.1) | copy-start | bytes 2654212
  2.8 5.6 %copy-start.4 = (f32[288,2]{0,1:T(2,128)S(1)}, f32[288,2]{0,1:T(2,128)}, u32[]{:S(2)}) copy-start(f32[288,2]{0,1:T(2,128)} %param.8) | copy-start | bytes 6916
  2.8 9.8 %copy-start = (bf16[1,1536,1024]{2,1,0:T(8,128)(2,1)S(1)}, bf16[1,1536,1024]{2,1,0:T(8,128)(2,1)}, u32[]{:S(2)}) copy-start(bf16[1,1536,1024]{2,1,0:T(8,128)(2,1)} %param.9) | copy-start | bytes 9437188
  2.8 9.9 %copy-start.1 = (bf16[1,1536,1024]{2,1,0:T(8,128)(2,1)S(1)}, bf16[1,1536,1024]{2,1,0:T(8,128)(2,1)}, u32[]{:S(2)}) copy-start(bf16[1,1536,1024]{2,1,0:T(8,128)(2,1)} %param.10) | copy-start | bytes 9437188
  3.3 9.4 %collective-permute-start = (bf16[972,128]{1,0:T(8,128)(2,1)S(1)}, bf16[972,128]{1,0:T(8,128)(2,1)S(1)}, u32[]{:S(2)}, u32[]{:S(2)}) collective-permute-start(bf16[972,128]{1,0:T(8,128)(2,1)S(1)} %pick.1.refs_0_.refs_1_), channel_id=1, source_target_pairs={{0,2},{1,3},{2,0},{3,1},{4,6},{5,7},{6,4},{7,5},{8,10},{9,11},{10,... | collective-permute-start | bytes 746504 | tf_op jit(solution)/shard_map/ppermute | solution.py:360
  5.9 14.4 %collective-permute-start.4 = (bf16[972,128]{1,0:T(8,128)(2,1)S(1)}, bf16[972,128]{1,0:T(8,128)(2,1)S(1)}, u32[]{:S(2)}, u32[]{:S(2)}) collective-permute-start(bf16[972,128]{1,0:T(8,128)(2,1)S(1)} %pick.1.refs_0_.refs_1_), channel_id=1, source_target_pairs={{0,6},{1,7},{2,4},{3,5},{4,2},{5,3},{6,0},{7,1},{8,14},{9,15},{10,... | collective-permute-start | bytes 746504 | tf_op jit(solution)/shard_map/ppermute | solution.py:360
  15.1 12.1 %collective-permute-start.5 = (bf16[1296,128]{1,0:T(8,128)(2,1)S(1)}, bf16[1296,128]{1,0:T(8,128)(2,1)S(1)}, u32[]{:S(2)}, u32[]{:S(2)}) collective-permute-start(bf16[1296,128]{1,0:T(8,128)(2,1)S(1)} %project.14.refs_0_), channel_id=1, source_target_pairs={{0,8},{8,0},{16,24},{24,16},{1,9},{9,1},{17,25},{25,17},{2,10},{10... | collective-permute-start | bytes 995336 | tf_op jit(solution)/shard_map/ppermute | solution.py:360
  16.8 16.3 %collective-permute-start.6 = (bf16[1296,128]{1,0:T(8,128)(2,1)S(1)}, bf16[1296,128]{1,0:T(8,128)(2,1)S(1)}, u32[]{:S(2)}, u32[]{:S(2)}) collective-permute-start(bf16[1296,128]{1,0:T(8,128)(2,1)S(1)} %project.13.refs_0_), channel_id=1, source_target_pairs={{0,16},{8,24},{16,0},{24,8},{1,17},{9,25},{17,1},{25,9},{2,18},{10... | collective-permute-start | bytes 995336 | tf_op jit(solution)/shard_map/ppermute | solution.py:360
  18.3 15.8 %collective-permute-start.7 = (bf16[1296,128]{1,0:T(8,128)(2,1)S(1)}, bf16[1296,128]{1,0:T(8,128)(2,1)S(1)}, u32[]{:S(2)}, u32[]{:S(2)}) collective-permute-start(bf16[1296,128]{1,0:T(8,128)(2,1)S(1)} %project.12.refs_0_), channel_id=1, source_target_pairs={{0,24},{8,16},{16,8},{24,0},{1,25},{9,17},{17,9},{25,1},{2,26},{10... | collective-permute-start | bytes 995336 | tf_op jit(solution)/shard_map/ppermute | solution.py:360
  20.3 14.1 %collective-permute-start.8 = (bf16[972,128]{1,0:T(8,128)(2,1)S(1)}, bf16[972,128]{1,0:T(8,128)(2,1)S(1)}, u32[]{:S(2)}, u32[]{:S(2)}) collective-permute-start(bf16[972,128]{1,0:T(8,128)(2,1)S(1)} %pick.1.refs_0_.refs_1_), channel_id=1, source_target_pairs={{0,4},{1,5},{2,6},{3,7},{4,0},{5,1},{6,2},{7,3},{8,12},{9,13},{10,... | collective-permute-start | bytes 746504 | tf_op jit(solution)/shard_map/ppermute | solution.py:360
  25.0 15.2 %collective-permute-start.9 = (bf16[648,128]{1,0:T(8,128)(2,1)S(1)}, bf16[648,128]{1,0:T(8,128)(2,1)S(1)}, u32[]{:S(2)}, u32[]{:S(2)}) collective-permute-start(bf16[648,128]{1,0:T(8,128)(2,1)S(1)} %project.18.refs_0_), channel_id=1, source_target_pairs={{0,8},{8,0},{16,24},{24,16},{1,9},{9,1},{17,25},{25,17},{2,10},{10... | collective-permute-start | bytes 497672 | tf_op jit(solution)/shard_map/ppermute | solution.py:360
  27.2 12.9 %collective-permute-start.10 = (bf16[648,128]{1,0:T(8,128)(2,1)S(1)}, bf16[648,128]{1,0:T(8,128)(2,1)S(1)}, u32[]{:S(2)}, u32[]{:S(2)}) collective-permute-start(bf16[648,128]{1,0:T(8,128)(2,1)S(1)} %project.17.refs_0_), channel_id=1, source_target_pairs={{0,16},{8,24},{16,0},{24,8},{1,17},{9,25},{17,1},{25,9},{2,18},{10... | collective-permute-start | bytes 497672 | tf_op jit(solution)/shard_map/ppermute | solution.py:360
  33.1 8.0 %collective-permute-start.11 = (bf16[648,128]{1,0:T(8,128)(2,1)S(1)}, bf16[648,128]{1,0:T(8,128)(2,1)S(1)}, u32[]{:S(2)}, u32[]{:S(2)}) collective-permute-start(bf16[648,128]{1,0:T(8,128)(2,1)S(1)} %project.16.refs_0_), channel_id=1, source_target_pairs={{0,24},{8,16},{16,8},{24,0},{1,25},{9,17},{17,9},{25,1},{2,26},{10... | collective-permute-start | bytes 497672 | tf_op jit(solution)/shard_map/ppermute | solution.py:360
  36.5 17.1 %collective-permute-start.16 = (bf16[648,128]{1,0:T(8,128)(2,1)S(1)}, bf16[648,128]{1,0:T(8,128)(2,1)S(1)}, u32[]{:S(2)}, u32[]{:S(2)}) collective-permute-start(bf16[648,128]{1,0:T(8,128)(2,1)S(1)} %project.22.refs_0_), channel_id=1, source_target_pairs={{0,8},{8,0},{16,24},{24,16},{1,9},{9,1},{17,25},{25,17},{2,10},{10... | collective-permute-start | bytes 497672 | tf_op jit(solution)/shard_map/ppermute | solution.py:360
  39.5 15.6 %copy-start.2 = (bf16[1,1024,1536]{2,1,0:T(8,128)(2,1)S(1)}, bf16[1,1024,1536]{2,1,0:T(8,128)(2,1)}, u32[]{:S(2)}) copy-start(bf16[1,1024,1536]{2,1,0:T(8,128)(2,1)} %param.11) | copy-start | bytes 9437188
  41.3 5.5 %collective-permute-start.14 = (bf16[324,128]{1,0:T(8,128)(2,1)S(1)}, bf16[324,128]{1,0:T(8,128)(2,1)S(1)}, u32[]{:S(2)}, u32[]{:S(2)}) collective-permute-start(bf16[324,128]{1,0:T(8,128)(2,1)S(1)} %act.4.refs_0_.refs_1_), channel_id=1, source_target_pairs={{0,24},{8,16},{16,8},{24,0},{1,25},{9,17},{17,9},{25,1},{2,26},{10... | collective-permute-start | bytes 248840 | tf_op jit(solution)/shard_map/ppermute | solution.py:360
  42.7 8.2 %collective-permute-start.13 = (bf16[324,128]{1,0:T(8,128)(2,1)S(1)}, bf16[324,128]{1,0:T(8,128)(2,1)S(1)}, u32[]{:S(2)}, u32[]{:S(2)}) collective-permute-start(bf16[324,128]{1,0:T(8,128)(2,1)S(1)} %act.4.refs_0_.refs_1_), channel_id=1, source_target_pairs={{0,16},{8,24},{16,0},{24,8},{1,17},{9,25},{17,1},{25,9},{2,18},{10... | collective-permute-start | bytes 248840 | tf_op jit(solution)/shard_map/ppermute | solution.py:360
  44.2 6.8 %collective-permute-start.12 = (bf16[324,128]{1,0:T(8,128)(2,1)S(1)}, bf16[324,128]{1,0:T(8,128)(2,1)S(1)}, u32[]{:S(2)}, u32[]{:S(2)}) collective-permute-start(bf16[324,128]{1,0:T(8,128)(2,1)S(1)} %act.4.refs_0_.refs_1_), channel_id=1, source_target_pairs={{0,8},{8,0},{16,24},{24,16},{1,9},{9,1},{17,25},{25,17},{2,10},{10... | collective-permute-start | bytes 248840 | tf_op jit(solution)/shard_map/ppermute | solution.py:360
  44.8 14.8 %collective-permute-start.17 = (bf16[648,128]{1,0:T(8,128)(2,1)S(1)}, bf16[648,128]{1,0:T(8,128)(2,1)S(1)}, u32[]{:S(2)}, u32[]{:S(2)}) collective-permute-start(bf16[648,128]{1,0:T(8,128)(2,1)S(1)} %project.21.refs_0_), channel_id=1, source_target_pairs={{0,16},{8,24},{16,0},{24,8},{1,17},{9,25},{17,1},{25,9},{2,18},{10... | collective-permute-start | bytes 497672 | tf_op jit(solution)/shard_map/ppermute | solution.py:360
  46.8 16.7 %collective-permute-start.18 = (bf16[648,128]{1,0:T(8,128)(2,1)S(1)}, bf16[648,128]{1,0:T(8,128)(2,1)S(1)}, u32[]{:S(2)}, u32[]{:S(2)}) collective-permute-start(bf16[648,128]{1,0:T(8,128)(2,1)S(1)} %project.20.refs_0_), channel_id=1, source_target_pairs={{0,24},{8,16},{16,8},{24,0},{1,25},{9,17},{17,9},{25,1},{2,26},{10... | collective-permute-start | bytes 497672 | tf_op jit(solution)/shard_map/ppermute | solution.py:360
  50.9 13.2 %collective-permute-start.21 = (bf16[648,128]{1,0:T(8,128)(2,1)S(1)}, bf16[648,128]{1,0:T(8,128)(2,1)S(1)}, u32[]{:S(2)}, u32[]{:S(2)}) collective-permute-start(bf16[648,128]{1,0:T(8,128)(2,1)S(1)} %act.3.refs_0_.refs_1_), channel_id=1, source_target_pairs={{0,24},{8,16},{16,8},{24,0},{1,25},{9,17},{17,9},{25,1},{2,26},{10... | collective-permute-start | bytes 497672 | tf_op jit(solution)/shard_map/ppermute | solution.py:360
  51.0 15.8 %collective-permute-start.20 = (bf16[648,128]{1,0:T(8,128)(2,1)S(1)}, bf16[648,128]{1,0:T(8,128)(2,1)S(1)}, u32[]{:S(2)}, u32[]{:S(2)}) collective-permute-start(bf16[648,128]{1,0:T(8,128)(2,1)S(1)} %act.3.refs_0_.refs_1_), channel_id=1, source_target_pairs={{0,16},{8,24},{16,0},{24,8},{1,17},{9,25},{17,1},{25,9},{2,18},{10... | collective-permute-start | bytes 497672 | tf_op jit(solution)/shard_map/ppermute | solution.py:360
  53.6 13.6 %collective-permute-start.19 = (bf16[648,128]{1,0:T(8,128)(2,1)S(1)}, bf16[648,128]{1,0:T(8,128)(2,1)S(1)}, u32[]{:S(2)}, u32[]{:S(2)}) collective-permute-start(bf16[648,128]{1,0:T(8,128)(2,1)S(1)} %act.3.refs_0_.refs_1_), channel_id=1, source_target_pairs={{0,8},{8,0},{16,24},{24,16},{1,9},{9,1},{17,25},{25,17},{2,10},{10... | collective-permute-start | bytes 497672 | tf_op jit(solution)/shard_map/ppermute | solution.py:360
  59.7 12.7 %collective-permute-start.15 = (bf16[972,128]{1,0:T(8,128)(2,1)S(1)}, bf16[972,128]{1,0:T(8,128)(2,1)S(1)}, u32[]{:S(2)}, u32[]{:S(2)}) collective-permute-start(bf16[972,128]{1,0:T(8,128)(2,1)S(1)} %down.3.refs_0_), channel_id=1, source_target_pairs={{0,6},{1,7},{2,4},{3,5},{4,2},{5,3},{6,0},{7,1},{8,14},{9,15},{10,... | collective-permute-start | bytes 746504 | tf_op jit(solution)/shard_map/ppermute | solution.py:360
  63.6 5.5 %collective-permute-start.25 = (bf16[324,128]{1,0:T(8,128)(2,1)S(1)}, bf16[324,128]{1,0:T(8,128)(2,1)S(1)}, u32[]{:S(2)}, u32[]{:S(2)}) collective-permute-start(bf16[324,128]{1,0:T(8,128)(2,1)S(1)} %act.5.refs_0_.refs_1_), channel_id=1, source_target_pairs={{0,24},{8,16},{16,8},{24,0},{1,25},{9,17},{17,9},{25,1},{2,26},{10... | collective-permute-start | bytes 248840 | tf_op jit(solution)/shard_map/ppermute | solution.py:360
  64.2 5.8 %collective-permute-start.24 = (bf16[324,128]{1,0:T(8,128)(2,1)S(1)}, bf16[324,128]{1,0:T(8,128)(2,1)S(1)}, u32[]{:S(2)}, u32[]{:S(2)}) collective-permute-start(bf16[324,128]{1,0:T(8,128)(2,1)S(1)} %act.5.refs_0_.refs_1_), channel_id=1, source_target_pairs={{0,16},{8,24},{16,0},{24,8},{1,17},{9,25},{17,1},{25,9},{2,18},{10... | collective-permute-start | bytes 248840 | tf_op jit(solution)/shard_map/ppermute | solution.py:360
  66.7 4.5 %collective-permute-start.23 = (bf16[324,128]{1,0:T(8,128)(2,1)S(1)}, bf16[324,128]{1,0:T(8,128)(2,1)S(1)}, u32[]{:S(2)}, u32[]{:S(2)}) collective-permute-start(bf16[324,128]{1,0:T(8,128)(2,1)S(1)} %act.5.refs_0_.refs_1_), channel_id=1, source_target_pairs={{0,8},{8,0},{16,24},{24,16},{1,9},{9,1},{17,25},{25,17},{2,10},{10... | collective-permute-start | bytes 248840 | tf_op jit(solution)/shard_map/ppermute | solution.py:360
  68.5 7.9 %collective-permute-start.22 = (bf16[972,128]{1,0:T(8,128)(2,1)S(1)}, bf16[972,128]{1,0:T(8,128)(2,1)S(1)}, u32[]{:S(2)}, u32[]{:S(2)}) collective-permute-start(bf16[972,128]{1,0:T(8,128)(2,1)S(1)} %get-tuple-element.12), channel_id=1, source_target_pairs={{0,2},{1,3},{2,0},{3,1},{4,6},{5,7},{6,4},{7,5},{8,10},{9,11},{10,... | collective-permute-start | bytes 746504 | tf_op jit(solution)/shard_map/ppermute | solution.py:360
  72.3 8.8 %collective-permute-start.26 = (bf16[972,128]{1,0:T(8,128)(2,1)S(1)}, bf16[972,128]{1,0:T(8,128)(2,1)S(1)}, u32[]{:S(2)}, u32[]{:S(2)}) collective-permute-start(bf16[972,128]{1,0:T(8,128)(2,1)S(1)} %down.5), channel_id=1, source_target_pairs={{0,4},{1,5},{2,6},{3,7},{4,0},{5,1},{6,2},{7,3},{8,12},{9,13},{10,... | collective-permute-start | bytes 746504 | tf_op jit(solution)/shard_map/ppermute | solution.py:360
  (1 other events, 0.7 us)

commit v5 on v4

--- a/solution.py
+++ b/solution.py
@@ -380,11 +380,12 @@
             weights = [own[0], other[0], own[1], other[1]]
             deps = (*last, other[2]) if g == WAIT else last
             if packed:
-                others = list(range(n_fsdp - 1, 0, -1))
+                others = list(range(1, n_fsdp))
                 out = []
                 for k in [*others, 0]:
-                    out = [*project_packed(xs, weights, n_fsdp, [k], deps), *out]
-                    deps = (out[0],)
+                    out.append(project_packed(xs, weights, n_fsdp, [k], deps)[0])
+                    deps = (out[-1],)
+                out = [out[-1], *out[:-1]]
             else:
                 out = project(xs, weights, n_fsdp, deps)
             parts[g] = [out[0]] + [across(out[k], k) for k in range(n_fsdp - 1, 0, -1)][::-1]

time: 82.9 us -> 81.4 us (0.982)
  waiting for transfers between devices: 28.4 us -> 24.8 us
  starting transfers between devices: 37 us -> 39.2 us
    ppermute x27, waiting for transfers between devices: 28.4 us -> 24.8 us  [local(): lax.ppermute(v, axis, [(i, i ^ k) for i in range(size)])]
    ppermute x27, starting transfers between devices: 37 us -> 39.2 us  [local(): lax.ppermute(v, axis, [(i, i ^ k) for i in range(size)])]
  transfers between devices with their start and end apart: 27 -> 27, of which waited for: 13 -> 10; matrix products, arithmetic and copies ran while one was open for 0% -> 0% of each run, Pallas kernels for 17% -> 17%
where the time goes in v5:
time: 81.4 us; the launch traced here: 81.2 us
  starting transfers between devices  39.2 us (48%)
  waiting for transfers between devices  24.8 us (30%)
  Pallas kernels  15.2 us (19%)
  local copies, waits for them, and re-layouts  1.87 us (2%)
    ppermute x27, starting transfers between devices, local(): lax.ppermute(v, axis, [(i, i ^ k) for i in range(size)])  39.2 us
    ppermute x27, waiting for transfers between devices, local(): lax.ppermute(v, axis, [(i, i ^ k) for i in range(size)])  24.8 us
    pallas_call x21, Pallas kernels, call(): pl.pallas_call(body, out_shape=outs, in_specs=[pl.BlockSpec(memory_space=...  15.2 us
    unnamed x12, local copies, waits for them, and re-layouts  1.87 us
  transfers between devices with their start and end apart: 27, of which 10 were waited for; matrix products, arithmetic and copies ran while one was open for 0% of the time, Pallas kernels for 17%

profile of v5, /device:TPU:0, one launch (start us, length us, event | category | flops | bytes accessed | tf_op | source)
XLA Modules:
  0.0 81.2 jit_solution(7847901768307887182)
XLA Ops:
  1.7 1.2 %copy-done.5 = bf16[288,1536]{1,0:T(8,128)(2,1)S(1)} copy-done((bf16[288,1536]{1,0:T(8,128)(2,1)S(1)}, bf16[288,1536]{1,0:T(8,128)(2,1)}, u32[]{:S(2)}) %copy-start.5) | copy-done | bytes 884760
  3.3 2.6 %collective-permute-start = (bf16[972,128]{1,0:T(8,128)(2,1)S(1)}, bf16[972,128]{1,0:T(8,128)(2,1)S(1)}, u32[]{:S(2)}, u32[]{:S(2)}) collective-permute-start(bf16[972,128]{1,0:T(8,128)(2,1)S(1)} %pick.1.refs_0_.refs_1_), channel_id=1, source_target_pairs={{0,2},{1,3},{2,0},{3,1},{4,6},{5,7},{6,4},{7,5},{8,10},{9,11},{10,... | collective-permute-start | bytes 746504 | tf_op jit(solution)/shard_map/ppermute | solution.py:360
  5.9 2.5 %collective-permute-start.4 = (bf16[972,128]{1,0:T(8,128)(2,1)S(1)}, bf16[972,128]{1,0:T(8,128)(2,1)S(1)}, u32[]{:S(2)}, u32[]{:S(2)}) collective-permute-start(bf16[972,128]{1,0:T(8,128)(2,1)S(1)} %pick.1.refs_0_.refs_1_), channel_id=1, source_target_pairs={{0,6},{1,7},{2,4},{3,5},{4,2},{5,3},{6,0},{7,1},{8,14},{9,15},{10,... | collective-permute-start | bytes 746504 | tf_op jit(solution)/shard_map/ppermute | solution.py:360
  8.7 4.0 %collective-permute-done.refs_2_ = bf16[972,128]{1,0:T(8,128)(2,1)S(1)} collective-permute-done((bf16[972,128]{1,0:T(8,128)(2,1)S(1)}, bf16[972,128]{1,0:T(8,128)(2,1)S(1)}, u32[]{:S(2)}, u32[]{:S(2)}) %collective-permute-start) | collective-permute-done | bytes 248864 | tf_op jit(solution)/shard_map/ppermute | solution.py:360
  12.7 0.8 project.12.refs_0_
  13.5 0.8 project.13.refs_0_
  14.3 0.8 %project.14.refs_0_ = bf16[1296,128]{1,0:T(8,128)(2,1)S(1)} custom-call(bf16[1296,128]{1,0:T(8,128)(2,1)S(1)} %project.13.refs_0_, bf16[972,128]{1,0:T(8,128)(2,1)S(1)} %pick.1.refs_0_.refs_1_, bf16[972,128]{1,0:T(8,128)(2,1)S(1)} %collective-permute-done.refs_2_, bf16[1536,1024]{1,0:T(8,128)(2,1)S(1)} %bitcast.8, ...), custom_call_target="tpu_custom_call" | custom-call | flops 553648128 | tf_op jit(solution)/shard_map/project/pallas_call | solution.py:21
  15.1 2.7 %collective-permute-start.7 = (bf16[1296,128]{1,0:T(8,128)(2,1)S(1)}, bf16[1296,128]{1,0:T(8,128)(2,1)S(1)}, u32[]{:S(2)}, u32[]{:S(2)}) collective-permute-start(bf16[1296,128]{1,0:T(8,128)(2,1)S(1)} %project.14.refs_0_), channel_id=1, source_target_pairs={{0,24},{8,16},{16,8},{24,0},{1,25},{9,17},{17,9},{25,1},{2,26},{10... | collective-permute-start | bytes 995336 | tf_op jit(solution)/shard_map/ppermute | solution.py:360
  18.7 1.6 %collective-permute-done.4.refs_2_.refs_1_ = bf16[972,128]{1,0:T(8,128)(2,1)S(1)} collective-permute-done((bf16[972,128]{1,0:T(8,128)(2,1)S(1)}, bf16[972,128]{1,0:T(8,128)(2,1)S(1)}, u32[]{:S(2)}, u32[]{:S(2)}) %collective-permute-start.4) | collective-permute-done | bytes 248864 | tf_op jit(solution)/shard_map/ppermute | solution.py:360
  20.3 1.7 %collective-permute-start.8 = (bf16[972,128]{1,0:T(8,128)(2,1)S(1)}, bf16[972,128]{1,0:T(8,128)(2,1)S(1)}, u32[]{:S(2)}, u32[]{:S(2)}) collective-permute-start(bf16[972,128]{1,0:T(8,128)(2,1)S(1)} %pick.1.refs_0_.refs_1_), channel_id=1, source_target_pairs={{0,4},{1,5},{2,6},{3,7},{4,0},{5,1},{6,2},{7,3},{8,12},{9,13},{10,... | collective-permute-start | bytes 746504 | tf_op jit(solution)/shard_map/ppermute | solution.py:360
  25.0 2.5 %collective-permute-start.11 = (bf16[648,128]{1,0:T(8,128)(2,1)S(1)}, bf16[648,128]{1,0:T(8,128)(2,1)S(1)}, u32[]{:S(2)}, u32[]{:S(2)}) collective-permute-start(bf16[648,128]{1,0:T(8,128)(2,1)S(1)} %project.18.refs_0_), channel_id=1, source_target_pairs={{0,24},{8,16},{16,8},{24,0},{1,25},{9,17},{17,9},{25,1},{2,26},{10... | collective-permute-start | bytes 497672 | tf_op jit(solution)/shard_map/ppermute | solution.py:360
  28.8 5.2 %collective-permute-done.6.refs_3_ = bf16[1296,128]{1,0:T(8,128)(2,1)S(1)} collective-permute-done((bf16[1296,128]{1,0:T(8,128)(2,1)S(1)}, bf16[1296,128]{1,0:T(8,128)(2,1)S(1)}, u32[]{:S(2)}, u32[]{:S(2)}) %collective-permute-start.6) | collective-permute-done | bytes 331808 | tf_op jit(solution)/shard_map/ppermute | solution.py:360
  34.0 1.7 %collective-permute-start.9 = (bf16[648,128]{1,0:T(8,128)(2,1)S(1)}, bf16[648,128]{1,0:T(8,128)(2,1)S(1)}, u32[]{:S(2)}, u32[]{:S(2)}) collective-permute-start(bf16[648,128]{1,0:T(8,128)(2,1)S(1)} %project.16.refs_0_), channel_id=1, source_target_pairs={{0,8},{8,0},{16,24},{24,16},{1,9},{9,1},{17,25},{25,17},{2,10},{10... | collective-permute-start | bytes 497672 | tf_op jit(solution)/shard_map/ppermute | solution.py:360
  38.0 1.6 %collective-permute-start.18 = (bf16[648,128]{1,0:T(8,128)(2,1)S(1)}, bf16[648,128]{1,0:T(8,128)(2,1)S(1)}, u32[]{:S(2)}, u32[]{:S(2)}) collective-permute-start(bf16[648,128]{1,0:T(8,128)(2,1)S(1)} %project.22.refs_0_), channel_id=1, source_target_pairs={{0,24},{8,16},{16,8},{24,0},{1,25},{9,17},{17,9},{25,1},{2,26},{10... | collective-permute-start | bytes 497672 | tf_op jit(solution)/shard_map/ppermute | solution.py:360
  40.4 2.2 %collective-permute-start.14 = (bf16[324,128]{1,0:T(8,128)(2,1)S(1)}, bf16[324,128]{1,0:T(8,128)(2,1)S(1)}, u32[]{:S(2)}, u32[]{:S(2)}) collective-permute-start(bf16[324,128]{1,0:T(8,128)(2,1)S(1)} %act.4.refs_0_.refs_1_), channel_id=1, source_target_pairs={{0,24},{8,16},{16,8},{24,0},{1,25},{9,17},{17,9},{25,1},{2,26},{10... | collective-permute-start | bytes 248840 | tf_op jit(solution)/shard_map/ppermute | solution.py:360
  42.6 0.8 collective-permute-start.13
  44.0 1.3 %collective-permute-start.17 = (bf16[648,128]{1,0:T(8,128)(2,1)S(1)}, bf16[648,128]{1,0:T(8,128)(2,1)S(1)}, u32[]{:S(2)}, u32[]{:S(2)}) collective-permute-start(bf16[648,128]{1,0:T(8,128)(2,1)S(1)} %project.21.refs_0_), channel_id=1, source_target_pairs={{0,16},{8,24},{16,0},{24,8},{1,17},{9,25},{17,1},{25,9},{2,18},{10... | collective-permute-start | bytes 497672 | tf_op jit(solution)/shard_map/ppermute | solution.py:360
  45.3 2.1 %collective-permute-done.14.refs_4_ = bf16[324,128]{1,0:T(8,128)(2,1)S(1)} collective-permute-done((bf16[324,128]{1,0:T(8,128)(2,1)S(1)}, bf16[324,128]{1,0:T(8,128)(2,1)S(1)}, u32[]{:S(2)}, u32[]{:S(2)}) %collective-permute-start.14) | collective-permute-done | bytes 82976 | tf_op jit(solution)/shard_map/ppermute | solution.py:360
  48.7 1.2 %collective-permute-start.21 = (bf16[648,128]{1,0:T(8,128)(2,1)S(1)}, bf16[648,128]{1,0:T(8,128)(2,1)S(1)}, u32[]{:S(2)}, u32[]{:S(2)}) collective-permute-start(bf16[648,128]{1,0:T(8,128)(2,1)S(1)} %act.3.refs_0_.refs_1_), channel_id=1, source_target_pairs={{0,24},{8,16},{16,8},{24,0},{1,25},{9,17},{17,9},{25,1},{2,26},{10... | collective-permute-start | bytes 497672 | tf_op jit(solution)/shard_map/ppermute | solution.py:360
  49.9 1.0 %collective-permute-start.20 = (bf16[648,128]{1,0:T(8,128)(2,1)S(1)}, bf16[648,128]{1,0:T(8,128)(2,1)S(1)}, u32[]{:S(2)}, u32[]{:S(2)}) collective-permute-start(bf16[648,128]{1,0:T(8,128)(2,1)S(1)} %act.3.refs_0_.refs_1_), channel_id=1, source_target_pairs={{0,16},{8,24},{16,0},{24,8},{1,17},{9,25},{17,1},{25,9},{2,18},{10... | collective-permute-start | bytes 497672 | tf_op jit(solution)/shard_map/ppermute | solution.py:360
  50.9 1.3 %collective-permute-start.19 = (bf16[648,128]{1,0:T(8,128)(2,1)S(1)}, bf16[648,128]{1,0:T(8,128)(2,1)S(1)}, u32[]{:S(2)}, u32[]{:S(2)}) collective-permute-start(bf16[648,128]{1,0:T(8,128)(2,1)S(1)} %act.3.refs_0_.refs_1_), channel_id=1, source_target_pairs={{0,8},{8,0},{16,24},{24,16},{1,9},{9,1},{17,25},{25,17},{2,10},{10... | collective-permute-start | bytes 497672 | tf_op jit(solution)/shard_map/ppermute | solution.py:360
  52.2 1.1 %down.3.refs_0_ = bf16[972,128]{1,0:T(8,128)(2,1)S(1)} custom-call(bf16[324,128]{1,0:T(8,128)(2,1)S(1)} %act.4.refs_0_.refs_1_, bf16[324,128]{1,0:T(8,128)(2,1)S(1)} %act.4.refs_0_.refs_1_, bf16[324,128]{1,0:T(8,128)(2,1)S(1)} %collective-permute-done.12.refs_2_, bf16[324,128]{1,0:T(8,128)(2,1)S(1)} %collective-permute-done.13.refs_3_, ...), custom_call_target="tpu_custom_call" | custom-call | flops 603979776 | tf_op jit(solution)/shard_map/down/pallas_call | solution.py:21
  53.3 8.7 %collective-permute-start.15 = (bf16[972,128]{1,0:T(8,128)(2,1)S(1)}, bf16[972,128]{1,0:T(8,128)(2,1)S(1)}, u32[]{:S(2)}, u32[]{:S(2)}) collective-permute-start(bf16[972,128]{1,0:T(8,128)(2,1)S(1)} %down.3.refs_0_), channel_id=1, source_target_pairs={{0,6},{1,7},{2,4},{3,5},{4,2},{5,3},{6,0},{7,1},{8,14},{9,15},{10,... | collective-permute-start | bytes 746504 | tf_op jit(solution)/shard_map/ppermute | solution.py:360
  62.2 1.5 %collective-permute-start.25 = (bf16[324,128]{1,0:T(8,128)(2,1)S(1)}, bf16[324,128]{1,0:T(8,128)(2,1)S(1)}, u32[]{:S(2)}, u32[]{:S(2)}) collective-permute-start(bf16[324,128]{1,0:T(8,128)(2,1)S(1)} %act.5.refs_0_.refs_1_), channel_id=1, source_target_pairs={{0,24},{8,16},{16,8},{24,0},{1,25},{9,17},{17,9},{25,1},{2,26},{10... | collective-permute-start | bytes 248840 | tf_op jit(solution)/shard_map/ppermute | solution.py:360
  63.7 1.3 %collective-permute-start.24 = (bf16[324,128]{1,0:T(8,128)(2,1)S(1)}, bf16[324,128]{1,0:T(8,128)(2,1)S(1)}, u32[]{:S(2)}, u32[]{:S(2)}) collective-permute-start(bf16[324,128]{1,0:T(8,128)(2,1)S(1)} %act.5.refs_0_.refs_1_), channel_id=1, source_target_pairs={{0,16},{8,24},{16,0},{24,8},{1,17},{9,25},{17,1},{25,9},{2,18},{10... | collective-permute-start | bytes 248840 | tf_op jit(solution)/shard_map/ppermute | solution.py:360
  65.7 1.3 %down.4 = (bf16[972,128]{1,0:T(8,128)(2,1)S(1)}, bf16[972,128]{1,0:T(8,128)(2,1)S(1)}) custom-call(bf16[324,128]{1,0:T(8,128)(2,1)S(1)} %act.5.refs_0_.refs_1_, bf16[648,128]{1,0:T(8,128)(2,1)S(1)} %act.3.refs_0_.refs_1_, bf16[648,128]{1,0:T(8,128)(2,1)S(1)} %collective-permute-done.19.refs_2_, bf16[648,128]{1,0:T(8,128)(2,1)S(1)} %collective-permute-done.20.refs_3_, ...), custom_call_target="tpu_custom_call" | custom-call | flops 1107296256 | tf_op jit(solution)/shard_map/down/pallas_call | solution.py:21
  67.6 0.9 %collective-permute-done.24.refs_3_ = bf16[324,128]{1,0:T(8,128)(2,1)S(1)} collective-permute-done((bf16[324,128]{1,0:T(8,128)(2,1)S(1)}, bf16[324,128]{1,0:T(8,128)(2,1)S(1)}, u32[]{:S(2)}, u32[]{:S(2)}) %collective-permute-start.24) | collective-permute-done | bytes 82976 | tf_op jit(solution)/shard_map/ppermute | solution.py:360
  68.5 0.9 %collective-permute-done.23.refs_2_ = bf16[324,128]{1,0:T(8,128)(2,1)S(1)} collective-permute-done((bf16[324,128]{1,0:T(8,128)(2,1)S(1)}, bf16[324,128]{1,0:T(8,128)(2,1)S(1)}, u32[]{:S(2)}, u32[]{:S(2)}) %collective-permute-start.23) | collective-permute-done | bytes 82976 | tf_op jit(solution)/shard_map/ppermute | solution.py:360
  69.4 1.1 %down.5 = bf16[972,128]{1,0:T(8,128)(2,1)S(1)} custom-call(bf16[972,128]{1,0:T(8,128)(2,1)S(1)} %get-tuple-element.11.refs_0_.refs_3_, bf16[324,128]{1,0:T(8,128)(2,1)S(1)} %act.5.refs_0_.refs_1_, bf16[324,128]{1,0:T(8,128)(2,1)S(1)} %collective-permute-done.23.refs_2_, bf16[324,128]{1,0:T(8,128)(2,1)S(1)} %collective-permute-done.24.refs_3_, ...), custom_call_target="tpu_custom_call" | custom-call | flops 603979776 | tf_op jit(solution)/shard_map/down/pallas_call | solution.py:21
  70.7 3.6 %collective-permute-done.22.refs_4_ = bf16[972,128]{1,0:T(8,128)(2,1)S(1)} collective-permute-done((bf16[972,128]{1,0:T(8,128)(2,1)S(1)}, bf16[972,128]{1,0:T(8,128)(2,1)S(1)}, u32[]{:S(2)}, u32[]{:S(2)}) %collective-permute-start.22) | collective-permute-done | bytes 248864 | tf_op jit(solution)/shard_map/ppermute | solution.py:360
  74.3 5.4 %collective-permute-done.26.refs_5_ = bf16[972,128]{1,0:T(8,128)(2,1)S(1)} collective-permute-done((bf16[972,128]{1,0:T(8,128)(2,1)S(1)}, bf16[972,128]{1,0:T(8,128)(2,1)S(1)}, u32[]{:S(2)}, u32[]{:S(2)}) %collective-permute-start.26) | collective-permute-done | bytes 248864 | tf_op jit(solution)/shard_map/ppermute | solution.py:360
  79.7 1.6 %combine.1 = bf16[288,1536]{1,0:T(8,128)(2,1)} custom-call(bf16[288,88]{1,0:T(8,128)(2,1)S(1)} %get-tuple-element.9.refs_0_, f32[288,128]{1,0:T(8,128)S(1)} %get-tuple-element.10.refs_1_, bf16[972,128]{1,0:T(8,128)(2,1)S(1)} %collective-permute-done.15.refs_2_, bf16[972,128]{1,0:T(8,128)(2,1)S(1)} %get-tuple-element.11.refs_0_.refs_3_, ...), custom_call_target="tpu_custom_call" | custom-call | tf_op jit(solution)/shard_map/combine/pallas_call | solution.py:21
  (55 shorter events, 14.0 us)
Async XLA Ops:
  0.0 12.7 %collective-permute-start.1 = (bf16[1536,1024]{1,0:T(8,128)(2,1)}, bf16[1536,1024]{1,0:T(8,128)(2,1)S(1)}, u32[]{:S(2)}, u32[]{:S(2)}) collective-permute-start(bf16[1536,1024]{1,0:T(8,128)(2,1)} %bitcast.5), channel_id=1, source_target_pairs={{0,1},{1,0},{2,3},{3,2},{4,5},{5,4},{6,7},{7,6},{8,9},{9,8},{10,11... | collective-permute-start | bytes 9437192 | tf_op jit(solution)/shard_map/ppermute | solution.py:360
  0.5 12.2 %collective-permute-start.2 = (bf16[1536,1024]{1,0:T(8,128)(2,1)}, bf16[1536,1024]{1,0:T(8,128)(2,1)S(1)}, u32[]{:S(2)}, u32[]{:S(2)}) collective-permute-start(bf16[1536,1024]{1,0:T(8,128)(2,1)} %bitcast.18), channel_id=1, source_target_pairs={{0,1},{1,0},{2,3},{3,2},{4,5},{5,4},{6,7},{7,6},{8,9},{9,8},{10,11... | collective-permute-start | bytes 9437192 | tf_op jit(solution)/shard_map/ppermute | solution.py:360
  0.5 22.3 %collective-permute-start.3 = (bf16[1024,1536]{1,0:T(8,128)(2,1)}, bf16[1024,1536]{1,0:T(8,128)(2,1)S(1)}, u32[]{:S(2)}, u32[]{:S(2)}) collective-permute-start(bf16[1024,1536]{1,0:T(8,128)(2,1)} %bitcast.31), channel_id=1, source_target_pairs={{0,1},{1,0},{2,3},{3,2},{4,5},{5,4},{6,7},{7,6},{8,9},{9,8},{10,11... | collective-permute-start | bytes 9437192 | tf_op jit(solution)/shard_map/ppermute | solution.py:360
  1.6 1.2 %copy-start.5 = (bf16[288,1536]{1,0:T(8,128)(2,1)S(1)}, bf16[288,1536]{1,0:T(8,128)(2,1)}, u32[]{:S(2)}) copy-start(bf16[288,1536]{1,0:T(8,128)(2,1)} %refs_1_.1) | copy-start | bytes 2654212
  2.8 5.6 %copy-start.4 = (f32[288,2]{0,1:T(2,128)S(1)}, f32[288,2]{0,1:T(2,128)}, u32[]{:S(2)}) copy-start(f32[288,2]{0,1:T(2,128)} %param.8) | copy-start | bytes 6916
  2.8 9.8 %copy-start = (bf16[1,1536,1024]{2,1,0:T(8,128)(2,1)S(1)}, bf16[1,1536,1024]{2,1,0:T(8,128)(2,1)}, u32[]{:S(2)}) copy-start(bf16[1,1536,1024]{2,1,0:T(8,128)(2,1)} %param.9) | copy-start | bytes 9437188
  2.8 9.9 %copy-start.1 = (bf16[1,1536,1024]{2,1,0:T(8,128)(2,1)S(1)}, bf16[1,1536,1024]{2,1,0:T(8,128)(2,1)}, u32[]{:S(2)}) copy-start(bf16[1,1536,1024]{2,1,0:T(8,128)(2,1)} %param.10) | copy-start | bytes 9437188
  3.3 9.4 %collective-permute-start = (bf16[972,128]{1,0:T(8,128)(2,1)S(1)}, bf16[972,128]{1,0:T(8,128)(2,1)S(1)}, u32[]{:S(2)}, u32[]{:S(2)}) collective-permute-start(bf16[972,128]{1,0:T(8,128)(2,1)S(1)} %pick.1.refs_0_.refs_1_), channel_id=1, source_target_pairs={{0,2},{1,3},{2,0},{3,1},{4,6},{5,7},{6,4},{7,5},{8,10},{9,11},{10,... | collective-permute-start | bytes 746504 | tf_op jit(solution)/shard_map/ppermute | solution.py:360
  5.9 14.4 %collective-permute-start.4 = (bf16[972,128]{1,0:T(8,128)(2,1)S(1)}, bf16[972,128]{1,0:T(8,128)(2,1)S(1)}, u32[]{:S(2)}, u32[]{:S(2)}) collective-permute-start(bf16[972,128]{1,0:T(8,128)(2,1)S(1)} %pick.1.refs_0_.refs_1_), channel_id=1, source_target_pairs={{0,6},{1,7},{2,4},{3,5},{4,2},{5,3},{6,0},{7,1},{8,14},{9,15},{10,... | collective-permute-start | bytes 746504 | tf_op jit(solution)/shard_map/ppermute | solution.py:360
  15.1 13.1 %collective-permute-start.7 = (bf16[1296,128]{1,0:T(8,128)(2,1)S(1)}, bf16[1296,128]{1,0:T(8,128)(2,1)S(1)}, u32[]{:S(2)}, u32[]{:S(2)}) collective-permute-start(bf16[1296,128]{1,0:T(8,128)(2,1)S(1)} %project.14.refs_0_), channel_id=1, source_target_pairs={{0,24},{8,16},{16,8},{24,0},{1,25},{9,17},{17,9},{25,1},{2,26},{10... | collective-permute-start | bytes 995336 | tf_op jit(solution)/shard_map/ppermute | solution.py:360
  17.8 16.2 %collective-permute-start.6 = (bf16[1296,128]{1,0:T(8,128)(2,1)S(1)}, bf16[1296,128]{1,0:T(8,128)(2,1)S(1)}, u32[]{:S(2)}, u32[]{:S(2)}) collective-permute-start(bf16[1296,128]{1,0:T(8,128)(2,1)S(1)} %project.13.refs_0_), channel_id=1, source_target_pairs={{0,16},{8,24},{16,0},{24,8},{1,17},{9,25},{17,1},{25,9},{2,18},{10... | collective-permute-start | bytes 995336 | tf_op jit(solution)/shard_map/ppermute | solution.py:360
  18.3 17.4 %collective-permute-start.5 = (bf16[1296,128]{1,0:T(8,128)(2,1)S(1)}, bf16[1296,128]{1,0:T(8,128)(2,1)S(1)}, u32[]{:S(2)}, u32[]{:S(2)}) collective-permute-start(bf16[1296,128]{1,0:T(8,128)(2,1)S(1)} %project.12.refs_0_), channel_id=1, source_target_pairs={{0,8},{8,0},{16,24},{24,16},{1,9},{9,1},{17,25},{25,17},{2,10},{10... | collective-permute-start | bytes 995336 | tf_op jit(solution)/shard_map/ppermute | solution.py:360
  20.3 15.6 %collective-permute-start.8 = (bf16[972,128]{1,0:T(8,128)(2,1)S(1)}, bf16[972,128]{1,0:T(8,128)(2,1)S(1)}, u32[]{:S(2)}, u32[]{:S(2)}) collective-permute-start(bf16[972,128]{1,0:T(8,128)(2,1)S(1)} %pick.1.refs_0_.refs_1_), channel_id=1, source_target_pairs={{0,4},{1,5},{2,6},{3,7},{4,0},{5,1},{6,2},{7,3},{8,12},{9,13},{10,... | collective-permute-start | bytes 746504 | tf_op jit(solution)/shard_map/ppermute | solution.py:360
  25.0 15.3 %collective-permute-start.11 = (bf16[648,128]{1,0:T(8,128)(2,1)S(1)}, bf16[648,128]{1,0:T(8,128)(2,1)S(1)}, u32[]{:S(2)}, u32[]{:S(2)}) collective-permute-start(bf16[648,128]{1,0:T(8,128)(2,1)S(1)} %project.18.refs_0_), channel_id=1, source_target_pairs={{0,24},{8,16},{16,8},{24,0},{1,25},{9,17},{17,9},{25,1},{2,26},{10... | collective-permute-start | bytes 497672 | tf_op jit(solution)/shard_map/ppermute | solution.py:360
  28.2 12.1 %collective-permute-start.10 = (bf16[648,128]{1,0:T(8,128)(2,1)S(1)}, bf16[648,128]{1,0:T(8,128)(2,1)S(1)}, u32[]{:S(2)}, u32[]{:S(2)}) collective-permute-start(bf16[648,128]{1,0:T(8,128)(2,1)S(1)} %project.17.refs_0_), channel_id=1, source_target_pairs={{0,16},{8,24},{16,0},{24,8},{1,17},{9,25},{17,1},{25,9},{2,18},{10... | collective-permute-start | bytes 497672 | tf_op jit(solution)/shard_map/ppermute | solution.py:360
  34.0 6.3 %collective-permute-start.9 = (bf16[648,128]{1,0:T(8,128)(2,1)S(1)}, bf16[648,128]{1,0:T(8,128)(2,1)S(1)}, u32[]{:S(2)}, u32[]{:S(2)}) collective-permute-start(bf16[648,128]{1,0:T(8,128)(2,1)S(1)} %project.16.refs_0_), channel_id=1, source_target_pairs={{0,8},{8,0},{16,24},{24,16},{1,9},{9,1},{17,25},{25,17},{2,10},{10... | collective-permute-start | bytes 497672 | tf_op jit(solution)/shard_map/ppermute | solution.py:360
  38.0 12.9 %collective-permute-start.18 = (bf16[648,128]{1,0:T(8,128)(2,1)S(1)}, bf16[648,128]{1,0:T(8,128)(2,1)S(1)}, u32[]{:S(2)}, u32[]{:S(2)}) collective-permute-start(bf16[648,128]{1,0:T(8,128)(2,1)S(1)} %project.22.refs_0_), channel_id=1, source_target_pairs={{0,24},{8,16},{16,8},{24,0},{1,25},{9,17},{17,9},{25,1},{2,26},{10... | collective-permute-start | bytes 497672 | tf_op jit(solution)/shard_map/ppermute | solution.py:360
  39.6 12.6 %copy-start.2 = (bf16[1,1024,1536]{2,1,0:T(8,128)(2,1)S(1)}, bf16[1,1024,1536]{2,1,0:T(8,128)(2,1)}, u32[]{:S(2)}) copy-start(bf16[1,1024,1536]{2,1,0:T(8,128)(2,1)} %param.11) | copy-start | bytes 9437188
  40.4 7.0 %collective-permute-start.14 = (bf16[324,128]{1,0:T(8,128)(2,1)S(1)}, bf16[324,128]{1,0:T(8,128)(2,1)S(1)}, u32[]{:S(2)}, u32[]{:S(2)}) collective-permute-start(bf16[324,128]{1,0:T(8,128)(2,1)S(1)} %act.4.refs_0_.refs_1_), channel_id=1, source_target_pairs={{0,24},{8,16},{16,8},{24,0},{1,25},{9,17},{17,9},{25,1},{2,26},{10... | collective-permute-start | bytes 248840 | tf_op jit(solution)/shard_map/ppermute | solution.py:360
  42.6 6.0 %collective-permute-start.13 = (bf16[324,128]{1,0:T(8,128)(2,1)S(1)}, bf16[324,128]{1,0:T(8,128)(2,1)S(1)}, u32[]{:S(2)}, u32[]{:S(2)}) collective-permute-start(bf16[324,128]{1,0:T(8,128)(2,1)S(1)} %act.4.refs_0_.refs_1_), channel_id=1, source_target_pairs={{0,16},{8,24},{16,0},{24,8},{1,17},{9,25},{17,1},{25,9},{2,18},{10... | collective-permute-start | bytes 248840 | tf_op jit(solution)/shard_map/ppermute | solution.py:360
  43.5 6.4 %collective-permute-start.12 = (bf16[324,128]{1,0:T(8,128)(2,1)S(1)}, bf16[324,128]{1,0:T(8,128)(2,1)S(1)}, u32[]{:S(2)}, u32[]{:S(2)}) collective-permute-start(bf16[324,128]{1,0:T(8,128)(2,1)S(1)} %act.4.refs_0_.refs_1_), channel_id=1, source_target_pairs={{0,8},{8,0},{16,24},{24,16},{1,9},{9,1},{17,25},{25,17},{2,10},{10... | collective-permute-start | bytes 248840 | tf_op jit(solution)/shard_map/ppermute | solution.py:360
  44.0 9.4 %collective-permute-start.17 = (bf16[648,128]{1,0:T(8,128)(2,1)S(1)}, bf16[648,128]{1,0:T(8,128)(2,1)S(1)}, u32[]{:S(2)}, u32[]{:S(2)}) collective-permute-start(bf16[648,128]{1,0:T(8,128)(2,1)S(1)} %project.21.refs_0_), channel_id=1, source_target_pairs={{0,16},{8,24},{16,0},{24,8},{1,17},{9,25},{17,1},{25,9},{2,18},{10... | collective-permute-start | bytes 497672 | tf_op jit(solution)/shard_map/ppermute | solution.py:360
  47.4 14.7 %collective-permute-start.16 = (bf16[648,128]{1,0:T(8,128)(2,1)S(1)}, bf16[648,128]{1,0:T(8,128)(2,1)S(1)}, u32[]{:S(2)}, u32[]{:S(2)}) collective-permute-start(bf16[648,128]{1,0:T(8,128)(2,1)S(1)} %project.20.refs_0_), channel_id=1, source_target_pairs={{0,8},{8,0},{16,24},{24,16},{1,9},{9,1},{17,25},{25,17},{2,10},{10... | collective-permute-start | bytes 497672 | tf_op jit(solution)/shard_map/ppermute | solution.py:360
  48.7 15.0 %collective-permute-start.21 = (bf16[648,128]{1,0:T(8,128)(2,1)S(1)}, bf16[648,128]{1,0:T(8,128)(2,1)S(1)}, u32[]{:S(2)}, u32[]{:S(2)}) collective-permute-start(bf16[648,128]{1,0:T(8,128)(2,1)S(1)} %act.3.refs_0_.refs_1_), channel_id=1, source_target_pairs={{0,24},{8,16},{16,8},{24,0},{1,25},{9,17},{17,9},{25,1},{2,26},{10... | collective-permute-start | bytes 497672 | tf_op jit(solution)/shard_map/ppermute | solution.py:360
  49.9 15.1 %collective-permute-start.20 = (bf16[648,128]{1,0:T(8,128)(2,1)S(1)}, bf16[648,128]{1,0:T(8,128)(2,1)S(1)}, u32[]{:S(2)}, u32[]{:S(2)}) collective-permute-start(bf16[648,128]{1,0:T(8,128)(2,1)S(1)} %act.3.refs_0_.refs_1_), channel_id=1, source_target_pairs={{0,16},{8,24},{16,0},{24,8},{1,17},{9,25},{17,1},{25,9},{2,18},{10... | collective-permute-start | bytes 497672 | tf_op jit(solution)/shard_map/ppermute | solution.py:360
  50.9 14.9 %collective-permute-start.19 = (bf16[648,128]{1,0:T(8,128)(2,1)S(1)}, bf16[648,128]{1,0:T(8,128)(2,1)S(1)}, u32[]{:S(2)}, u32[]{:S(2)}) collective-permute-start(bf16[648,128]{1,0:T(8,128)(2,1)S(1)} %act.3.refs_0_.refs_1_), channel_id=1, source_target_pairs={{0,8},{8,0},{16,24},{24,16},{1,9},{9,1},{17,25},{25,17},{2,10},{10... | collective-permute-start | bytes 497672 | tf_op jit(solution)/shard_map/ppermute | solution.py:360
  53.3 17.3 %collective-permute-start.15 = (bf16[972,128]{1,0:T(8,128)(2,1)S(1)}, bf16[972,128]{1,0:T(8,128)(2,1)S(1)}, u32[]{:S(2)}, u32[]{:S(2)}) collective-permute-start(bf16[972,128]{1,0:T(8,128)(2,1)S(1)} %down.3.refs_0_), channel_id=1, source_target_pairs={{0,6},{1,7},{2,4},{3,5},{4,2},{5,3},{6,0},{7,1},{8,14},{9,15},{10,... | collective-permute-start | bytes 746504 | tf_op jit(solution)/shard_map/ppermute | solution.py:360
  62.2 5.5 %collective-permute-start.25 = (bf16[324,128]{1,0:T(8,128)(2,1)S(1)}, bf16[324,128]{1,0:T(8,128)(2,1)S(1)}, u32[]{:S(2)}, u32[]{:S(2)}) collective-permute-start(bf16[324,128]{1,0:T(8,128)(2,1)S(1)} %act.5.refs_0_.refs_1_), channel_id=1, source_target_pairs={{0,24},{8,16},{16,8},{24,0},{1,25},{9,17},{17,9},{25,1},{2,26},{10... | collective-permute-start | bytes 248840 | tf_op jit(solution)/shard_map/ppermute | solution.py:360
  63.7 4.8 %collective-permute-start.24 = (bf16[324,128]{1,0:T(8,128)(2,1)S(1)}, bf16[324,128]{1,0:T(8,128)(2,1)S(1)}, u32[]{:S(2)}, u32[]{:S(2)}) collective-permute-start(bf16[324,128]{1,0:T(8,128)(2,1)S(1)} %act.5.refs_0_.refs_1_), channel_id=1, source_target_pairs={{0,16},{8,24},{16,0},{24,8},{1,17},{9,25},{17,1},{25,9},{2,18},{10... | collective-permute-start | bytes 248840 | tf_op jit(solution)/shard_map/ppermute | solution.py:360
  65.0 4.5 %collective-permute-start.23 = (bf16[324,128]{1,0:T(8,128)(2,1)S(1)}, bf16[324,128]{1,0:T(8,128)(2,1)S(1)}, u32[]{:S(2)}, u32[]{:S(2)}) collective-permute-start(bf16[324,128]{1,0:T(8,128)(2,1)S(1)} %act.5.refs_0_.refs_1_), channel_id=1, source_target_pairs={{0,8},{8,0},{16,24},{24,16},{1,9},{9,1},{17,25},{25,17},{2,10},{10... | collective-permute-start | bytes 248840 | tf_op jit(solution)/shard_map/ppermute | solution.py:360
  67.1 7.2 %collective-permute-start.22 = (bf16[972,128]{1,0:T(8,128)(2,1)S(1)}, bf16[972,128]{1,0:T(8,128)(2,1)S(1)}, u32[]{:S(2)}, u32[]{:S(2)}) collective-permute-start(bf16[972,128]{1,0:T(8,128)(2,1)S(1)} %get-tuple-element.12), channel_id=1, source_target_pairs={{0,2},{1,3},{2,0},{3,1},{4,6},{5,7},{6,4},{7,5},{8,10},{9,11},{10,... | collective-permute-start | bytes 746504 | tf_op jit(solution)/shard_map/ppermute | solution.py:360
  70.6 9.1 %collective-permute-start.26 = (bf16[972,128]{1,0:T(8,128)(2,1)S(1)}, bf16[972,128]{1,0:T(8,128)(2,1)S(1)}, u32[]{:S(2)}, u32[]{:S(2)}) collective-permute-start(bf16[972,128]{1,0:T(8,128)(2,1)S(1)} %down.5), channel_id=1, source_target_pairs={{0,4},{1,5},{2,6},{3,7},{4,0},{5,1},{6,2},{7,3},{8,12},{9,13},{10,... | collective-permute-start | bytes 746504 | tf_op jit(solution)/shard_map/ppermute | solution.py:360
  (1 other events, 0.7 us)
